TPU v7x, 512 devices: a whole 4x8x8 slice. The times are simulated.
512 devices in a mesh: ctx: 16 (over z_hi, x, core), exp: 32 (over z_lo, y).
Axes of the slice: x: 4, y: 8, z: 8 (z_hi: 2, z_lo: 4; z = z_hi * 4 + z_lo), core: 2. Of those that a mesh axis runs over, the one named last changes fastest.
Arguments:
- queries: bfloat16 [8192, 8192], P('ctx', 'exp'), may hold values from -80 to 80
- key_states: bfloat16 [8192, 512], P('ctx'), may hold values from -4 to 4
- value_states: bfloat16 [8192, 512], P('ctx'), may hold values from -6 to 6
- token_states: bfloat16 [2048, 4096], P('exp', 'ctx'), may hold values from -6 to 6
- expert_ids: int32 [2048, 8], P('exp'), may hold values from 0 to 31, all different within a row; in each aligned block of 64 rows (0 to 63, 64 to 127, ...) at most 18 rows name the same one
- combine_weights: float32 [2048, 8], P('exp'), may hold values from 0.1 to 1
- gate_weight: bfloat16 [32, 4096, 1536], P('exp', 'ctx'), may hold values from -0.09375 to 0.09375
- up_weight: bfloat16 [32, 4096, 1536], P('exp', 'ctx'), may hold values from -0.09375 to 0.09375
- down_weight: bfloat16 [32, 1536, 4096], P('exp', None, 'ctx'), may hold values from -0.15625 to 0.15625
Outputs:
- context: bfloat16 [8192, 8192], P('ctx', 'exp')
- moe_output: bfloat16 [2048, 4096], P('exp', 'ctx')
Inputs may be any that keep to these rules, and one draw needn't show every extreme that they name: `expert_ids`: each row names 8 different experts. Within each aligned block of 64 rows (the tokens of one device) no expert is named by more than 18 rows, and in every draw some expert is named by exactly 18 rows of some block.
All inputs are finite; a program needn't handle non-finite values.
Results may differ from a plain program's by a relative error of at most 0.011.
Values may be sent and summed in bfloat16 or wider, within the bound.
No kernel may reach another device: no remote copies, remote signals or barrier semaphores. Data moves between devices by JAX's collectives and lax.ppermute only.
A program may use at most 64 MiB of HBM per device.

v0:
```python
import jax
import jax.numpy as jnp
from jax import lax
from jax.sharding import PartitionSpec as P

FF = 1536
HEADS = 64
KVH = 4
HD = 128
TOPK = 8
EXPERTS = 32
CAP = 18


neg_big = -1e30


def shifted(shard, axis, by):
    size = lax.axis_size(axis)
    pairs = [(i, i + by) for i in range(size) if 0 <= i + by < size]
    return lax.ppermute(shard, axis, pairs)


def attend_block(running, query_blocks, key_block, value_block, query_pos, key_start):
    peak_now, row_total, weighted = running
    scores = jnp.einsum(
        "qhd,kd->qhk", query_blocks, key_block, preferred_element_type=jnp.float32
    ) * query_blocks.shape[2] ** (-0.5)
    key_pos = key_start + lax.iota(jnp.int32, key_block.shape[0])
    allowed = (query_pos[:, None] >= key_pos[None, :])[:, None, :]
    peak_new = jnp.maximum(peak_now, jnp.max(jnp.where(allowed, scores, neg_big), axis=2))
    weights = jnp.where(allowed, jnp.exp(scores - peak_new[:, :, None]), 0.0)
    shrink = jnp.exp(peak_now - peak_new)
    row_total = row_total * shrink + jnp.sum(weights, axis=2)
    weighted = weighted * shrink[:, :, None] + jnp.einsum(
        "qhk,kd->qhd", weights.astype(jnp.bfloat16), value_block, preferred_element_type=jnp.float32
    )
    return (peak_new, row_total, weighted)


def expert_rows(inputs, matrices):
    partial_value = jnp.dot(inputs, matrices[0], preferred_element_type=jnp.float32)
    return partial_value


def body(
    queries,
    key_states,
    value_states,
    token_states,
    expert_ids,
    combine_weights,
    gate_weight,
    up_weight,
    down_weight,
):
    ctx_count = lax.axis_size("ctx")
    ctx_index = lax.axis_index("ctx")
    exp_index = lax.axis_index("exp")
    query_rows = queries.shape[0]
    query_heads = queries.shape[1] // HD
    kv_head = exp_index * query_heads // (HEADS // KVH)
    own_keys = lax.dynamic_slice_in_dim(key_states, kv_head * HD, HD, 1)
    own_values = lax.dynamic_slice_in_dim(value_states, kv_head * HD, HD, 1)
    key_value = jnp.stack([own_keys, own_values])
    query_blocks = queries.reshape(query_rows, query_heads, HD)
    query_pos = ctx_index * query_rows + lax.iota(jnp.int32, query_rows)
    running = (
        jnp.full((query_rows, query_heads), neg_big, jnp.float32),
        jnp.zeros((query_rows, query_heads), jnp.float32),
        jnp.zeros((query_rows, query_heads, HD), jnp.float32),
    )
    running = attend_block(
        running, query_blocks, own_keys, own_values, query_pos, ctx_index * query_rows
    )

    def turn(turn_index, loop_carry):
        travelled, status = loop_carry
        travelled = shifted(travelled, "ctx", 1)
        source = ctx_index - turn_index
        status = lax.cond(
            source >= 0,
            lambda inside: attend_block(
                inside, query_blocks, travelled[0], travelled[1], query_pos, source * query_rows
            ),
            lambda inside: inside,
            status,
        )
        return (travelled, status)

    travelled, running = lax.fori_loop(1, ctx_count, turn, (key_value, running))
    peak_now, row_total, weighted = running
    context = (
        (weighted / row_total[:, :, None])
        .astype(jnp.bfloat16)
        .reshape(query_rows, query_heads * HD)
    )
    token_count = token_states.shape[0]
    width_dev = token_states.shape[1]
    flat_ids = expert_ids.reshape(-1)
    choose = (flat_ids[:, None] == lax.iota(jnp.int32, EXPERTS)[None, :]).astype(jnp.int32)
    before = jnp.cumsum(choose, axis=0) - choose
    slot_index = jnp.sum(before * choose, axis=1)
    target = flat_ids * CAP + slot_index
    placed = (target[:, None] == lax.iota(jnp.int32, EXPERTS * CAP)[None, :]).reshape(
        token_count, TOPK, EXPERTS * CAP
    )
    dispatch_map = jnp.any(placed, axis=1).astype(jnp.bfloat16)
    combine_map = jnp.sum(jnp.where(placed, combine_weights[:, :, None], 0.0), axis=1)
    outbound = jnp.einsum(
        "ts,td->sd", dispatch_map, token_states, preferred_element_type=jnp.float32
    ).astype(jnp.bfloat16)
    outbound = outbound.reshape(EXPERTS, CAP, width_dev)
    received = lax.all_to_all(outbound, "exp", split_axis=0, concat_axis=1, tiled=True)
    gate_part = jnp.einsum(
        "erd,edf->erf", received, gate_weight, preferred_element_type=jnp.float32
    )
    up_part = jnp.einsum("erd,edf->erf", received, up_weight, preferred_element_type=jnp.float32)
    both = jnp.concatenate([gate_part, up_part], axis=2).astype(jnp.bfloat16)
    arrived = lax.all_to_all(both, "ctx", split_axis=1, concat_axis=0, tiled=True)
    summed = jnp.sum(arrived.astype(jnp.float32), axis=0)
    hidden_share = (jax.nn.silu(summed[:, :FF]) * summed[:, FF:]).astype(jnp.bfloat16)
    projected = expert_rows(lax.all_gather(hidden_share, "ctx", axis=0, tiled=True), down_weight)
    expert_out = projected.astype(jnp.bfloat16).reshape(received.shape)
    returned = lax.all_to_all(expert_out, "exp", split_axis=1, concat_axis=0, tiled=True)
    flat_back = returned.reshape(EXPERTS * CAP, width_dev).astype(jnp.float32)
    moe_output = jnp.dot(combine_map, flat_back, precision=lax.Precision.HIGHEST).astype(
        jnp.bfloat16
    )
    return (context, moe_output)


def solution(mesh):
    in_specs = (
        P("ctx", "exp"),
        P("ctx", None),
        P("ctx", None),
        P("exp", "ctx"),
        P("exp", None),
        P("exp", None),
        P("exp", "ctx", None),
        P("exp", "ctx", None),
        P("exp", None, "ctx"),
    )
    out_specs = (P("ctx", "exp"), P("exp", "ctx"))
    return jax.shard_map(body, mesh=mesh, in_specs=in_specs, out_specs=out_specs, check_vma=False)
```

profile of v0, /device:TPU:320, one launch (start us, length us, event | category | flops | bytes accessed | tf_op | source)
XLA Modules:
  0.0 678.2 jit_solution(15311926466821213151)
XLA Ops:
  12.4 24.1 %all_to_all.12 = bf16[32,18,256]{2,1,0:T(8,128)(2,1)S(1)} all-to-all(bf16[32,18,256]{2,1,0:T(8,128)(2,1)S(1)} %reshape.190), channel_id=1, replica_groups=mesh['ctx'=16,'exp'=32] {'exp'}, dimensions={0} | all-to-all | bytes 589824 | tf_op jit(solution)/shard_map/all_to_all | solution.py:114
  38.4 31.0 %copy.99 = bf16[1,576,3072]{2,0,1:T(2,128)(2,1)} copy(bf16[1,576,3072]{2,1,0:T(8,128)(2,1)S(1)} %pad_maximum_fusion) | data formatting | bytes 7077888 | tf_op jit(solution)/shard_map/concatenate | solution.py:119
  69.9 77.2 %reduce.4 = bf16[576,3072]{1,0:T(8,128)(2,1)} reduce(bf16[576,1,3072]{2,1,0:T(2,128)(2,1)} %bitcast.98, bf16[]{:T(256)} %broadcast.114), dimensions={1}, to_apply=%bitcast.96.reduce_sub_computation | reduce | bytes 7077890
  147.1 7.1 %reshape.205 = bf16[16,2,55296]{2,1,0:T(2,128)(2,1)} reshape(bf16[576,3072]{1,0:T(8,128)(2,1)} %reduce.4) | data formatting | bytes 7077888
  154.2 89.6 %all_to_all.13 = bf16[16,2,55296]{2,1,0:T(2,128)(2,1)} all-to-all(bf16[16,2,55296]{2,1,0:T(2,128)(2,1)} %reshape.205), channel_id=1, replica_groups=mesh['ctx'=16,'exp'=32] {'ctx'}, dimensions={0} | all-to-all | bytes 7077888 | tf_op jit(solution)/shard_map/all_to_all | solution.py:120
  243.8 11.9 %reshape.206 = bf16[576,1,3072]{2,1,0:T(2,128)(2,1)} reshape(bf16[16,2,55296]{2,1,0:T(2,128)(2,1)} %all_to_all.13) | data formatting | bytes 7077888
  255.6 63.7 %convert_reduce_fusion = f32[576,3072]{1,0:T(8,128)} fusion(bf16[576,1,3072]{2,1,0:T(2,128)(2,1)} %reshape.206), kind=kLoop, calls=%fused_computation.22 | loop fusion | flops 1769472 | bytes 10616832 | tf_op jit(solution)/shard_map/convert_element_type | solution.py:121
  319.3 6.6 reshape.196
  325.9 3.7 reduce_sum.51
  335.7 54.4 %all-gather.3.cloned.1.call-done = bf16[16,36,1536]{2,1,0:T(8,128)(2,1)} async-done(((bf16[1,36,1536]{2,1,0:T(8,128)(2,1)}), bf16[16,36,1536]{2,1,0:T(8,128)(2,1)}) %all-gather.3.cloned.1.call-update) | async-done | bytes 1769488 | tf_op jit(solution)/shard_map/all_gather | solution.py:123
  390.1 3.5 reshape.198
  397.1 4.0 reduce.5
  402.9 10.3 %all-to-all-start.2 = ((bf16[32,2,2304]{2,1,0:T(2,128)(2,1)}), bf16[32,2,2304]{2,1,0:T(2,128)(2,1)}, u32[]{:S(2)}, u32[]{:S(2)}) async-start(bf16[32,2,2304]{2,1,0:T(2,128)(2,1)} %reshape.207), calls=%async_computation.2 | async-start | bytes 589824 | tf_op jit(solution)/shard_map/all_to_all | solution.py:125
  418.2 248.0 %while.20 = (s32[]{:T(128)}, bf16[2,512,128]{2,1,0:T(8,128)(2,1)}, f32[512,2]{0,1:T(2,128)S(1)}, f32[512,2]{0,1:T(2,128)S(1)}, f32[512,2,128]{2,0,1:T(8,128)}, /...) while((s32[]{:T(128)}, bf16[2,512,128]{2,1,0:T(8,128)(2,1)}, ...), condition=%wide.region_7.8_spmd.clone, body=%wide.region_2.7_spmd.clone.sunk | while | flops 274729984 | bytes 14758251 | solution.py:91
  420.3 14.8 %collective-permute-done = bf16[2,512,128]{2,1,0:T(8,128)(2,1)S(1)} collective-permute-done((bf16[2,512,128]{2,1,0:T(8,128)(2,1)}, bf16[2,512,128]{2,1,0:T(8,128)(2,1)S(1)}, u32[]{:S(2)}, u32[]{:S(2)}) %collective-permute-start) | collective-permute-done | bytes 262176 | tf_op jit(solution)/shard_map/while/body/eval_jaxpr/ppermute | solution.py:21
  440.7 13.9 %collective-permute-done = bf16[2,512,128]{2,1,0:T(8,128)(2,1)S(1)} collective-permute-done((bf16[2,512,128]{2,1,0:T(8,128)(2,1)}, bf16[2,512,128]{2,1,0:T(8,128)(2,1)S(1)}, u32[]{:S(2)}, u32[]{:S(2)}) %collective-permute-start) | collective-permute-done | bytes 262176 | tf_op jit(solution)/shard_map/while/body/eval_jaxpr/ppermute | solution.py:21
  460.2 12.1 %collective-permute-done = bf16[2,512,128]{2,1,0:T(8,128)(2,1)S(1)} collective-permute-done((bf16[2,512,128]{2,1,0:T(8,128)(2,1)}, bf16[2,512,128]{2,1,0:T(8,128)(2,1)S(1)}, u32[]{:S(2)}, u32[]{:S(2)}) %collective-permute-start) | collective-permute-done | bytes 262176 | tf_op jit(solution)/shard_map/while/body/eval_jaxpr/ppermute | solution.py:21
  477.9 12.0 %collective-permute-done = bf16[2,512,128]{2,1,0:T(8,128)(2,1)S(1)} collective-permute-done((bf16[2,512,128]{2,1,0:T(8,128)(2,1)}, bf16[2,512,128]{2,1,0:T(8,128)(2,1)S(1)}, u32[]{:S(2)}, u32[]{:S(2)}) %collective-permute-start) | collective-permute-done | bytes 262176 | tf_op jit(solution)/shard_map/while/body/eval_jaxpr/ppermute | solution.py:21
  489.9 3.0 conditional.3
  495.5 12.0 %collective-permute-done = bf16[2,512,128]{2,1,0:T(8,128)(2,1)S(1)} collective-permute-done((bf16[2,512,128]{2,1,0:T(8,128)(2,1)}, bf16[2,512,128]{2,1,0:T(8,128)(2,1)S(1)}, u32[]{:S(2)}, u32[]{:S(2)}) %collective-permute-start) | collective-permute-done | bytes 262176 | tf_op jit(solution)/shard_map/while/body/eval_jaxpr/ppermute | solution.py:21
  507.5 3.0 conditional.3
  513.1 12.0 %collective-permute-done = bf16[2,512,128]{2,1,0:T(8,128)(2,1)S(1)} collective-permute-done((bf16[2,512,128]{2,1,0:T(8,128)(2,1)}, bf16[2,512,128]{2,1,0:T(8,128)(2,1)S(1)}, u32[]{:S(2)}, u32[]{:S(2)}) %collective-permute-start) | collective-permute-done | bytes 262176 | tf_op jit(solution)/shard_map/while/body/eval_jaxpr/ppermute | solution.py:21
  530.7 12.0 %collective-permute-done = bf16[2,512,128]{2,1,0:T(8,128)(2,1)S(1)} collective-permute-done((bf16[2,512,128]{2,1,0:T(8,128)(2,1)}, bf16[2,512,128]{2,1,0:T(8,128)(2,1)S(1)}, u32[]{:S(2)}, u32[]{:S(2)}) %collective-permute-start) | collective-permute-done | bytes 262176 | tf_op jit(solution)/shard_map/while/body/eval_jaxpr/ppermute | solution.py:21
  548.3 12.0 %collective-permute-done = bf16[2,512,128]{2,1,0:T(8,128)(2,1)S(1)} collective-permute-done((bf16[2,512,128]{2,1,0:T(8,128)(2,1)}, bf16[2,512,128]{2,1,0:T(8,128)(2,1)S(1)}, u32[]{:S(2)}, u32[]{:S(2)}) %collective-permute-start) | collective-permute-done | bytes 262176 | tf_op jit(solution)/shard_map/while/body/eval_jaxpr/ppermute | solution.py:21
  560.3 3.0 conditional.3
  565.9 12.0 %collective-permute-done = bf16[2,512,128]{2,1,0:T(8,128)(2,1)S(1)} collective-permute-done((bf16[2,512,128]{2,1,0:T(8,128)(2,1)}, bf16[2,512,128]{2,1,0:T(8,128)(2,1)S(1)}, u32[]{:S(2)}, u32[]{:S(2)}) %collective-permute-start) | collective-permute-done | bytes 262176 | tf_op jit(solution)/shard_map/while/body/eval_jaxpr/ppermute | solution.py:21
  580.5 12.0 %collective-permute-done = bf16[2,512,128]{2,1,0:T(8,128)(2,1)S(1)} collective-permute-done((bf16[2,512,128]{2,1,0:T(8,128)(2,1)}, bf16[2,512,128]{2,1,0:T(8,128)(2,1)S(1)}, u32[]{:S(2)}, u32[]{:S(2)}) %collective-permute-start) | collective-permute-done | bytes 262176 | tf_op jit(solution)/shard_map/while/body/eval_jaxpr/ppermute | solution.py:21
  595.1 12.0 %collective-permute-done = bf16[2,512,128]{2,1,0:T(8,128)(2,1)S(1)} collective-permute-done((bf16[2,512,128]{2,1,0:T(8,128)(2,1)}, bf16[2,512,128]{2,1,0:T(8,128)(2,1)S(1)}, u32[]{:S(2)}, u32[]{:S(2)}) %collective-permute-start) | collective-permute-done | bytes 262176 | tf_op jit(solution)/shard_map/while/body/eval_jaxpr/ppermute | solution.py:21
  609.7 12.0 %collective-permute-done = bf16[2,512,128]{2,1,0:T(8,128)(2,1)S(1)} collective-permute-done((bf16[2,512,128]{2,1,0:T(8,128)(2,1)}, bf16[2,512,128]{2,1,0:T(8,128)(2,1)S(1)}, u32[]{:S(2)}, u32[]{:S(2)}) %collective-permute-start) | collective-permute-done | bytes 262176 | tf_op jit(solution)/shard_map/while/body/eval_jaxpr/ppermute | solution.py:21
  624.3 12.0 %collective-permute-done = bf16[2,512,128]{2,1,0:T(8,128)(2,1)S(1)} collective-permute-done((bf16[2,512,128]{2,1,0:T(8,128)(2,1)}, bf16[2,512,128]{2,1,0:T(8,128)(2,1)S(1)}, u32[]{:S(2)}, u32[]{:S(2)}) %collective-permute-start) | collective-permute-done | bytes 262176 | tf_op jit(solution)/shard_map/while/body/eval_jaxpr/ppermute | solution.py:21
  638.9 12.0 %collective-permute-done = bf16[2,512,128]{2,1,0:T(8,128)(2,1)S(1)} collective-permute-done((bf16[2,512,128]{2,1,0:T(8,128)(2,1)}, bf16[2,512,128]{2,1,0:T(8,128)(2,1)S(1)}, u32[]{:S(2)}, u32[]{:S(2)}) %collective-permute-start) | collective-permute-done | bytes 262176 | tf_op jit(solution)/shard_map/while/body/eval_jaxpr/ppermute | solution.py:21
  653.5 12.0 %collective-permute-done = bf16[2,512,128]{2,1,0:T(8,128)(2,1)S(1)} collective-permute-done((bf16[2,512,128]{2,1,0:T(8,128)(2,1)}, bf16[2,512,128]{2,1,0:T(8,128)(2,1)S(1)}, u32[]{:S(2)}, u32[]{:S(2)}) %collective-permute-start) | collective-permute-done | bytes 262176 | tf_op jit(solution)/shard_map/while/body/eval_jaxpr/ppermute | solution.py:21
  (209 shorter events, 106.3 us)
Async XLA Ops:
  7.2 29.4 %copy-start = (bf16[1,256,1536]{2,1,0:T(8,128)(2,1)S(1)}, bf16[1,256,1536]{2,1,0:T(8,128)(2,1)}, u32[]{:S(2)}) copy-start(bf16[1,256,1536]{2,1,0:T(8,128)(2,1)} %param.19) | copy-start | bytes 2359300
  7.2 382.9 %all-gather.3.cloned.1.call-start = ((), (), s32[]{:S(2)}) async-start(), calls=%async_computation.3 | async-start | bytes 2088960 | tf_op jit(solution)/shard_map/all_gather | solution.py:123
  12.4 24.9 %copy-start.1 = (bf16[1,256,1536]{2,1,0:T(8,128)(2,1)S(1)}, bf16[1,256,1536]{2,1,0:T(8,128)(2,1)}, u32[]{:S(2)}) copy-start(bf16[1,256,1536]{2,1,0:T(8,128)(2,1)} %param.20) | copy-start | bytes 2359300
  325.9 4.5 copy-start.5
  325.9 4.7 copy-start.7
  402.9 265.2 %all-to-all-start.2 = ((bf16[32,2,2304]{2,1,0:T(2,128)(2,1)}), bf16[32,2,2304]{2,1,0:T(2,128)(2,1)}, u32[]{:S(2)}, u32[]{:S(2)}) async-start(bf16[32,2,2304]{2,1,0:T(2,128)(2,1)} %reshape.207), calls=%async_computation.2 | async-start | bytes 589824 | tf_op jit(solution)/shard_map/all_to_all | solution.py:125
  415.8 2.5 copy-start.6
  418.2 252.2 %copy-start.2 = (f32[64,576]{1,0:T(8,128)S(1)}, f32[64,576]{1,0:T(8,128)}, u32[]{:S(2)}) copy-start(f32[64,576]{1,0:T(8,128)} %select_reduce_fusion.1) | copy-start | bytes 442372
  418.2 16.8 %collective-permute-start = (bf16[2,512,128]{2,1,0:T(8,128)(2,1)}, bf16[2,512,128]{2,1,0:T(8,128)(2,1)S(1)}, u32[]{:S(2)}, u32[]{:S(2)}) collective-permute-start(bf16[2,512,128]{2,1,0:T(8,128)(2,1)} %get-tuple-element.345), channel_id=1, source_target_pairs={{0,32},{32,64},{64,96},{96,128},{128,160},{160,192},{192,224},{224... | collective-permute-start | bytes 786440 | tf_op jit(solution)/shard_map/while/body/eval_jaxpr/ppermute | solution.py:21
  435.3 1.1 copy-start.3
  437.3 0.8 copy-start.4
  438.8 15.8 %collective-permute-start = (bf16[2,512,128]{2,1,0:T(8,128)(2,1)}, bf16[2,512,128]{2,1,0:T(8,128)(2,1)S(1)}, u32[]{:S(2)}, u32[]{:S(2)}) collective-permute-start(bf16[2,512,128]{2,1,0:T(8,128)(2,1)} %get-tuple-element.345), channel_id=1, source_target_pairs={{0,32},{32,64},{64,96},{96,128},{128,160},{160,192},{192,224},{224... | collective-permute-start | bytes 786440 | tf_op jit(solution)/shard_map/while/body/eval_jaxpr/ppermute | solution.py:21
  454.8 1.1 copy-start.3
  458.3 14.0 %collective-permute-start = (bf16[2,512,128]{2,1,0:T(8,128)(2,1)}, bf16[2,512,128]{2,1,0:T(8,128)(2,1)S(1)}, u32[]{:S(2)}, u32[]{:S(2)}) collective-permute-start(bf16[2,512,128]{2,1,0:T(8,128)(2,1)} %get-tuple-element.345), channel_id=1, source_target_pairs={{0,32},{32,64},{64,96},{96,128},{128,160},{160,192},{192,224},{224... | collective-permute-start | bytes 786440 | tf_op jit(solution)/shard_map/while/body/eval_jaxpr/ppermute | solution.py:21
  472.5 1.1 copy-start.3
  476.0 13.9 %collective-permute-start = (bf16[2,512,128]{2,1,0:T(8,128)(2,1)}, bf16[2,512,128]{2,1,0:T(8,128)(2,1)S(1)}, u32[]{:S(2)}, u32[]{:S(2)}) collective-permute-start(bf16[2,512,128]{2,1,0:T(8,128)(2,1)} %get-tuple-element.345), channel_id=1, source_target_pairs={{0,32},{32,64},{64,96},{96,128},{128,160},{160,192},{192,224},{224... | collective-permute-start | bytes 786440 | tf_op jit(solution)/shard_map/while/body/eval_jaxpr/ppermute | solution.py:21
  490.1 1.1 copy-start.3
  493.6 13.9 %collective-permute-start = (bf16[2,512,128]{2,1,0:T(8,128)(2,1)}, bf16[2,512,128]{2,1,0:T(8,128)(2,1)S(1)}, u32[]{:S(2)}, u32[]{:S(2)}) collective-permute-start(bf16[2,512,128]{2,1,0:T(8,128)(2,1)} %get-tuple-element.345), channel_id=1, source_target_pairs={{0,32},{32,64},{64,96},{96,128},{128,160},{160,192},{192,224},{224... | collective-permute-start | bytes 786440 | tf_op jit(solution)/shard_map/while/body/eval_jaxpr/ppermute | solution.py:21
  507.7 1.1 copy-start.3
  511.2 13.9 %collective-permute-start = (bf16[2,512,128]{2,1,0:T(8,128)(2,1)}, bf16[2,512,128]{2,1,0:T(8,128)(2,1)S(1)}, u32[]{:S(2)}, u32[]{:S(2)}) collective-permute-start(bf16[2,512,128]{2,1,0:T(8,128)(2,1)} %get-tuple-element.345), channel_id=1, source_target_pairs={{0,32},{32,64},{64,96},{96,128},{128,160},{160,192},{192,224},{224... | collective-permute-start | bytes 786440 | tf_op jit(solution)/shard_map/while/body/eval_jaxpr/ppermute | solution.py:21
  525.3 1.1 copy-start.3
  528.8 13.9 %collective-permute-start = (bf16[2,512,128]{2,1,0:T(8,128)(2,1)}, bf16[2,512,128]{2,1,0:T(8,128)(2,1)S(1)}, u32[]{:S(2)}, u32[]{:S(2)}) collective-permute-start(bf16[2,512,128]{2,1,0:T(8,128)(2,1)} %get-tuple-element.345), channel_id=1, source_target_pairs={{0,32},{32,64},{64,96},{96,128},{128,160},{160,192},{192,224},{224... | collective-permute-start | bytes 786440 | tf_op jit(solution)/shard_map/while/body/eval_jaxpr/ppermute | solution.py:21
  542.9 1.1 copy-start.3
  546.3 13.9 %collective-permute-start = (bf16[2,512,128]{2,1,0:T(8,128)(2,1)}, bf16[2,512,128]{2,1,0:T(8,128)(2,1)S(1)}, u32[]{:S(2)}, u32[]{:S(2)}) collective-permute-start(bf16[2,512,128]{2,1,0:T(8,128)(2,1)} %get-tuple-element.345), channel_id=1, source_target_pairs={{0,32},{32,64},{64,96},{96,128},{128,160},{160,192},{192,224},{224... | collective-permute-start | bytes 786440 | tf_op jit(solution)/shard_map/while/body/eval_jaxpr/ppermute | solution.py:21
  560.5 1.1 copy-start.3
  563.9 13.9 %collective-permute-start = (bf16[2,512,128]{2,1,0:T(8,128)(2,1)}, bf16[2,512,128]{2,1,0:T(8,128)(2,1)S(1)}, u32[]{:S(2)}, u32[]{:S(2)}) collective-permute-start(bf16[2,512,128]{2,1,0:T(8,128)(2,1)} %get-tuple-element.345), channel_id=1, source_target_pairs={{0,32},{32,64},{64,96},{96,128},{128,160},{160,192},{192,224},{224... | collective-permute-start | bytes 786440 | tf_op jit(solution)/shard_map/while/body/eval_jaxpr/ppermute | solution.py:21
  578.5 13.9 %collective-permute-start = (bf16[2,512,128]{2,1,0:T(8,128)(2,1)}, bf16[2,512,128]{2,1,0:T(8,128)(2,1)S(1)}, u32[]{:S(2)}, u32[]{:S(2)}) collective-permute-start(bf16[2,512,128]{2,1,0:T(8,128)(2,1)} %get-tuple-element.345), channel_id=1, source_target_pairs={{0,32},{32,64},{64,96},{96,128},{128,160},{160,192},{192,224},{224... | collective-permute-start | bytes 786440 | tf_op jit(solution)/shard_map/while/body/eval_jaxpr/ppermute | solution.py:21
  593.2 13.9 %collective-permute-start = (bf16[2,512,128]{2,1,0:T(8,128)(2,1)}, bf16[2,512,128]{2,1,0:T(8,128)(2,1)S(1)}, u32[]{:S(2)}, u32[]{:S(2)}) collective-permute-start(bf16[2,512,128]{2,1,0:T(8,128)(2,1)} %get-tuple-element.345), channel_id=1, source_target_pairs={{0,32},{32,64},{64,96},{96,128},{128,160},{160,192},{192,224},{224... | collective-permute-start | bytes 786440 | tf_op jit(solution)/shard_map/while/body/eval_jaxpr/ppermute | solution.py:21
  607.8 13.9 %collective-permute-start = (bf16[2,512,128]{2,1,0:T(8,128)(2,1)}, bf16[2,512,128]{2,1,0:T(8,128)(2,1)S(1)}, u32[]{:S(2)}, u32[]{:S(2)}) collective-permute-start(bf16[2,512,128]{2,1,0:T(8,128)(2,1)} %get-tuple-element.345), channel_id=1, source_target_pairs={{0,32},{32,64},{64,96},{96,128},{128,160},{160,192},{192,224},{224... | collective-permute-start | bytes 786440 | tf_op jit(solution)/shard_map/while/body/eval_jaxpr/ppermute | solution.py:21
  622.4 13.9 %collective-permute-start = (bf16[2,512,128]{2,1,0:T(8,128)(2,1)}, bf16[2,512,128]{2,1,0:T(8,128)(2,1)S(1)}, u32[]{:S(2)}, u32[]{:S(2)}) collective-permute-start(bf16[2,512,128]{2,1,0:T(8,128)(2,1)} %get-tuple-element.345), channel_id=1, source_target_pairs={{0,32},{32,64},{64,96},{96,128},{128,160},{160,192},{192,224},{224... | collective-permute-start | bytes 786440 | tf_op jit(solution)/shard_map/while/body/eval_jaxpr/ppermute | solution.py:21
  637.0 13.9 %collective-permute-start = (bf16[2,512,128]{2,1,0:T(8,128)(2,1)}, bf16[2,512,128]{2,1,0:T(8,128)(2,1)S(1)}, u32[]{:S(2)}, u32[]{:S(2)}) collective-permute-start(bf16[2,512,128]{2,1,0:T(8,128)(2,1)} %get-tuple-element.345), channel_id=1, source_target_pairs={{0,32},{32,64},{64,96},{96,128},{128,160},{160,192},{192,224},{224... | collective-permute-start | bytes 786440 | tf_op jit(solution)/shard_map/while/body/eval_jaxpr/ppermute | solution.py:21
  651.6 13.9 %collective-permute-start = (bf16[2,512,128]{2,1,0:T(8,128)(2,1)}, bf16[2,512,128]{2,1,0:T(8,128)(2,1)S(1)}, u32[]{:S(2)}, u32[]{:S(2)}) collective-permute-start(bf16[2,512,128]{2,1,0:T(8,128)(2,1)} %get-tuple-element.345), channel_id=1, source_target_pairs={{0,32},{32,64},{64,96},{96,128},{128,160},{160,192},{192,224},{224... | collective-permute-start | bytes 786440 | tf_op jit(solution)/shard_map/while/body/eval_jaxpr/ppermute | solution.py:21
  (7 other events, 5.5 us)
Sparse Core Ops, SparseCore 0:
  330.5 59.4 all-gather.2
where the time goes:
time: 680 us; the launch traced here: 678 us
  waiting for transfers between devices  239 us (35%)
  other arithmetic  164 us (24%)
  blocking collectives  114 us (17%)
  local copies, waits for them, and re-layouts  87.2 us (13%)
  starting transfers between devices  39.1 us (6%)
  matrix products  20.5 us (3%)
  between operations  14.2 us (2%)
    ppermute x15, waiting for transfers between devices, shifted(): return lax.ppermute(shard, axis, pairs)  185 us
    all_to_all x1, blocking collectives, body(): lax.all_to_all(both, 'ctx', split_axis=1, concat_axis=0, tiled=True)  89.6 us
    unnamed x3, other arithmetic  81.9 us
    convert_element_type x1, other arithmetic, body(): summed = jnp.sum(arrived.astype(jnp.float32), axis=0)  63.7 us
    all_gather x1, waiting for transfers between devices, body(): lax.all_gather(hidden_share, 'ctx', axis=0, tiled=True)  54.4 us
    concatenate x1, local copies, waits for them, and re-layouts, body(): both = jnp.concatenate([gate_part, up_part], axis=2).astype(jnp.bfloat16)  31 us
    unnamed x22, local copies, waits for them, and re-layouts  29 us
    ppermute x15, starting transfers between devices, shifted(): return lax.ppermute(shard, axis, pairs)  28.8 us
  transfers between devices with their start and end apart: 17, of which 16 were waited for; matrix products, arithmetic and copies ran while one was open for 6% of the time, Pallas kernels for 0%

commit v1 on v0

v1 whole, which is shorter than its diff:
```python
import functools

import jax
import jax.numpy as jnp
from jax import lax
from jax.experimental import pallas as pl
from jax.experimental.pallas import tpu as pltpu
from jax.sharding import Mesh
from jax.sharding import PartitionSpec as P

FF = 1536
HALF = FF // 2
HEADS = 64
KVH = 4
HD = 128
TOPK = 8
EXPERTS = 32
CAP = 18
ROOM = 24
ROWS = EXPERTS * CAP
F32 = jnp.float32
BF16 = jnp.bfloat16
CONTRACT_LAST = (((1,), (1,)), ((), ()))
CONTRACT_FIRST = (((0,), (0,)), ((), ()))
SMEM = pl.BlockSpec(memory_space=pltpu.SMEM)
VMEM = pl.BlockSpec(memory_space=pltpu.VMEM)


def call(kernel, outs, ins, flops, moved, limit=32, scratch=(), transcendentals=0, name=None):
    return pl.pallas_call(
        kernel,
        out_shape=outs,
        in_specs=[SMEM] + [VMEM] * (len(ins) - 1),
        out_specs=jax.tree.map(lambda _: VMEM, outs),
        scratch_shapes=scratch,
        compiler_params=pltpu.CompilerParams(vmem_limit_bytes=limit << 20),
        cost_estimate=pl.CostEstimate(
            flops=flops, bytes_accessed=moved, transcendentals=transcendentals
        ),
        name=name,
    )(*ins)


def shape(dims, dtype=BF16):
    return jax.ShapeDtypeStruct(dims, dtype)


def attention_kernel(place, q_ref, kv_ref, o_ref, q2, peak, acc, *, tile, keys):
    rows, heads = q_ref.shape[0], q_ref.shape[1] // HD
    shard = place[0]
    unit = 1.4426950408889634 * HD**-0.5
    for h in range(heads):
        q = q_ref[:, h * HD : (h + 1) * HD].astype(F32) * unit
        high = q.astype(BF16)
        q2[h * rows : (h + 1) * rows, :HD] = high
        q2[h * rows : (h + 1) * rows, HD:] = (q - high.astype(F32)).astype(BF16)

    def block(start, first):
        k = kv_ref[pl.ds(start, keys), :HD]
        v = kv_ref[pl.ds(start, keys), HD:]
        kk = jnp.concatenate([k, k], axis=1)
        v1 = jnp.concatenate([v, jnp.ones_like(v)], axis=1)
        for t in range(rows * heads // tile):
            sl = slice(t * tile, (t + 1) * tile)
            s = lax.dot_general(q2[sl, :], kk, CONTRACT_LAST, preferred_element_type=F32)
            if first:
                query = (t * tile) % rows + lax.broadcasted_iota(jnp.int32, (tile, keys), 0)
                key = lax.broadcasted_iota(jnp.int32, (tile, keys), 1)
                s = jnp.where(query >= key, s, -1e30)
            new = jnp.max(s, axis=1, keepdims=True)
            if not first:
                old = peak[sl, :1]
                new = jnp.maximum(old, new)
            peak[sl, :] = jnp.broadcast_to(new, (tile, HD))
            mixed = jnp.dot(jnp.exp2(s - new).astype(BF16), v1, preferred_element_type=F32)
            acc[sl, :] = mixed if first else acc[sl, :] * jnp.exp2(old - new) + mixed

    block(pl.multiple_of(shard * rows, rows), True)

    def earlier(j, carry):
        block(pl.multiple_of(j * keys, keys), False)
        return carry

    lax.fori_loop(0, shard * (rows // keys), earlier, 0)
    for h in range(heads):
        a = acc[h * rows : (h + 1) * rows, :]
        o_ref[:, h * HD : (h + 1) * HD] = (a[:, :HD] / a[:, HD:]).astype(o_ref.dtype)


def attention(place, q, kv):
    rows, cols = q.shape
    stacked = rows * cols // HD
    return call(
        functools.partial(attention_kernel, tile=256, keys=rows),
        shape(q.shape),
        (place, q, kv),
        flops=4 * stacked * kv.shape[0] * HD,
        moved=5 << 20,
        limit=40,
        transcendentals=stacked * kv.shape[0],
        scratch=[
            pltpu.VMEM((stacked, 2 * HD), BF16),
            pltpu.VMEM((stacked, HD), F32),
            pltpu.VMEM((stacked, 2 * HD), F32),
        ],
        name="attention",
    )


def dispatch_kernel(place, ids_ref, w_ref, tokens_ref, out_ref, combine_ref):
    ids, w = ids_ref[...], w_ref[...]
    count = ids.shape[0]
    expert = lax.broadcasted_iota(jnp.int32, (count, EXPERTS), 1)
    weight = jnp.zeros((count, EXPERTS), F32)
    chosen = jnp.zeros((count, EXPERTS), F32)
    for k in range(TOPK):
        hit = ids[:, k : k + 1] == expert
        weight = weight + jnp.where(hit, w[:, k : k + 1], 0.0)
        chosen = chosen + jnp.where(hit, 1.0, 0.0)
    earlier = lax.broadcasted_iota(jnp.int32, (count, count), 0) > lax.broadcasted_iota(
        jnp.int32, (count, count), 1
    )
    rank = jnp.dot(earlier.astype(BF16), chosen.astype(BF16), preferred_element_type=F32)
    slots = EXPERTS * ROOM
    column = lax.broadcasted_iota(jnp.int32, (EXPERTS, slots), 1)
    owner = lax.broadcasted_iota(jnp.int32, (EXPERTS, slots), 0)
    inside = column - owner * ROOM
    spread = jnp.where((inside >= 0) & (inside < ROOM), 1.0, 0.0)
    slot = jnp.sum(jnp.where(spread > 0, inside.astype(F32), 0.0), axis=0, keepdims=True)
    spread_low = spread.astype(BF16)
    hits = jnp.dot(chosen.astype(BF16), spread_low, preferred_element_type=F32)
    ranks = jnp.dot(rank.astype(BF16), spread_low, preferred_element_type=F32)
    weights = jnp.dot(weight, spread, precision=lax.Precision.HIGHEST)
    placed = (hits > 0.5) & (ranks == slot)
    combine_ref[...] = jnp.where(placed, weights, 0.0)
    onehot = jnp.where(placed, 1.0, 0.0).astype(BF16)
    out_ref[...] = lax.dot_general(
        onehot, tokens_ref[...], CONTRACT_FIRST, preferred_element_type=F32
    ).astype(BF16)


def packing(tall, wide, by_row):
    row = lax.broadcasted_iota(jnp.int32, (tall, wide), 0)
    column = lax.broadcasted_iota(jnp.int32, (tall, wide), 1)
    tight, loose = (row, column) if by_row else (column, row)
    block = lax.shift_right_logical(tight * 3641, 16)
    return jnp.where(loose == tight + block * (ROOM - CAP), 1.0, 0.0).astype(BF16)


def products_kernel(place, own_ref, sibling_ref, gate_ref, up_ref, swapped_ref, out_ref):
    start = pl.multiple_of(place[1] * HALF, HALF)
    pack = packing(ROWS, EXPERTS * ROOM, True)
    own = jnp.dot(pack, own_ref[...], preferred_element_type=F32).astype(BF16)
    sibling = jnp.dot(pack, sibling_ref[...], preferred_element_type=F32).astype(BF16)
    parts = out_ref.shape[0]
    rows = ROWS // parts
    for i in range(parts):
        a, b = own[i * rows : (i + 1) * rows], sibling[i * rows : (i + 1) * rows]
        for j, mine in enumerate((gate_ref, up_ref)):
            out_ref[i, :, j * HALF : (j + 1) * HALF] = (
                jnp.dot(a, mine[:, pl.ds(start, HALF)], preferred_element_type=F32)
                + jnp.dot(b, swapped_ref[j], preferred_element_type=F32)
            ).astype(BF16)


def sum_kernel(place, parts_ref, wide_ref, low_ref):
    total = parts_ref[0].astype(F32)
    for i in range(1, parts_ref.shape[0]):
        total = total + parts_ref[i].astype(F32)
    wide_ref[...] = total
    low_ref[...] = total.astype(BF16)


def hidden_kernel(place, wide_ref, other_ref, out_ref):
    total = wide_ref[...] + other_ref[...].astype(F32)
    gate, up = total[:, :HALF], total[:, HALF:]
    hidden = (gate / (1.0 + jnp.exp(-gate)) * up).astype(BF16)
    for i in range(out_ref.shape[0]):
        out_ref[i] = hidden


def project_kernel(place, hidden_ref, down_ref, swapped_ref, own_ref, sibling_ref):
    start = pl.multiple_of(place[1] * HALF, HALF)
    parts = hidden_ref.shape[0]
    rows = ROWS // parts
    for i in range(parts):
        sl = slice(i * rows, (i + 1) * rows)
        h = hidden_ref[i]
        sibling_ref[sl] = jnp.dot(h, swapped_ref[...], preferred_element_type=F32).astype(BF16)
        own_ref[sl] = jnp.dot(h, down_ref[pl.ds(start, HALF), :], preferred_element_type=F32)


def finish_kernel(place, own_ref, other_ref, out_ref):
    result = (own_ref[...] + other_ref[...].astype(F32)).astype(BF16)
    unpack = packing(EXPERTS * ROOM, ROWS, False)
    out_ref[...] = jnp.dot(unpack, result, preferred_element_type=F32).astype(BF16)


def combine_kernel(place, combine_ref, back_ref, out_ref):
    c = combine_ref[...]
    back = back_ref[...]
    total = jnp.zeros(out_ref.shape, F32)
    for _ in range(3):
        part = c.astype(BF16)
        total = total + jnp.dot(part, back, preferred_element_type=F32)
        c = c - part.astype(F32)
    out_ref[...] = total.astype(BF16)


def body(
    queries,
    key_states,
    value_states,
    token_states,
    expert_ids,
    combine_weights,
    gate_weight,
    up_weight,
    down_weight,
):
    core, z_lo = lax.axis_index("c"), lax.axis_index("z")
    shard = (lax.axis_index("w") * lax.axis_size("x") + lax.axis_index("x")) * 2 + core
    place = jnp.stack([shard, core]).astype(jnp.int32)
    head = z_lo * HD
    kv = jnp.concatenate(
        [
            lax.dynamic_slice_in_dim(key_states, head, HD, 1),
            lax.dynamic_slice_in_dim(value_states, head, HD, 1),
        ],
        axis=1,
    )
    gate, up, down = gate_weight[0], up_weight[0], down_weight[0]
    width = token_states.shape[1]
    swap = lambda a: lax.ppermute(a, "c", [(0, 1), (1, 0)])

    kv_all = lax.all_gather(kv, ("w", "x", "c"), axis=0, tiled=True)

    slots = EXPERTS * ROOM
    outbound, combine_map = call(
        dispatch_kernel,
        (shape((slots, width)), shape((token_states.shape[0], slots), F32)),
        (place, expert_ids, combine_weights, token_states),
        flops=2 * slots * 64 * 400,
        moved=1 << 20,
        name="dispatch",
    )
    received = lax.all_to_all(
        outbound.reshape(EXPERTS, ROOM, width), ("z", "y"), 0, 0, tiled=True
    ).reshape(slots, width)
    other_half = (1 - core) * HALF
    swapped = swap(
        jnp.stack(
            [
                lax.dynamic_slice_in_dim(gate, other_half, HALF, 1),
                lax.dynamic_slice_in_dim(up, other_half, HALF, 1),
            ]
        )
    )
    swapped_down = swap(lax.dynamic_slice_in_dim(down, other_half, HALF, 0))
    sibling = swap(received)
    lanes = lax.axis_size("x")
    rows = ROWS // lanes
    products = call(
        products_kernel,
        shape((lanes, rows, FF)),
        (place, received, sibling, gate, up, swapped),
        flops=2 * ROWS * 2 * width * FF,
        moved=4 << 20,
        name="products",
    )
    parts = lax.all_to_all(products, "x", 0, 0, tiled=True)
    wide, low = call(
        sum_kernel,
        (shape((rows, FF), F32), shape((rows, FF))),
        (place, parts),
        flops=rows * FF * 4,
        moved=3 << 20,
        name="sum_parts",
    )
    other = lax.ppermute(low, "w", [(0, 1), (1, 0)])
    hidden = call(
        hidden_kernel,
        shape((lanes, rows, HALF)),
        (place, wide, other),
        flops=rows * FF * 4,
        moved=2 << 20,
        transcendentals=rows * HALF,
        name="hidden",
    )
    hidden_all = lax.all_to_all(hidden, "x", 0, 0, tiled=True)
    own_part, sibling_part = call(
        project_kernel,
        (shape((ROWS, width), F32), shape((ROWS, width))),
        (place, hidden_all, down, swapped_down),
        flops=2 * ROWS * HALF * 2 * width,
        moved=3 << 20,
        name="project",
    )
    finished = call(
        finish_kernel,
        shape((slots, width)),
        (place, own_part, swap(sibling_part)),
        flops=2 * ROWS * slots * width,
        moved=2 << 20,
        name="finish",
    )
    back = lax.all_to_all(finished.reshape(EXPERTS, ROOM, width), ("z", "y"), 0, 0, tiled=True)
    moe_output = call(
        combine_kernel,
        shape(token_states.shape),
        (place, combine_map, back.reshape(slots, width)),
        flops=6 * slots * width * 64,
        moved=1 << 20,
        name="combine",
    )
    context = attention(place, queries, kv_all)
    return (context, moe_output)


def solution(mesh):
    fine = Mesh(mesh.devices.reshape(2, 4, 2, 4, 8), ("w", "x", "c", "z", "y"))
    ctx, exp = ("w", "x", "c"), ("z", "y")
    in_specs = (
        P(ctx, exp),
        P(ctx, None),
        P(ctx, None),
        P(exp, ctx),
        P(exp, None),
        P(exp, None),
        P(exp, ctx, None),
        P(exp, ctx, None),
        P(exp, None, ctx),
    )
    out_specs = (P(ctx, exp), P(exp, ctx))
    return jax.shard_map(body, mesh=fine, in_specs=in_specs, out_specs=out_specs, check_vma=False)
```

time: 680 us -> 188 us (0.28)
  the two profiles are of different devices: /device:TPU:320 before, /device:TPU:270 now
where the time goes in v1:
time: 188 us
  waiting for transfers between devices  56.1 us (30%)
  blocking collectives  52 us (28%)
  Pallas kernels  32.5 us (17%)
  starting transfers between devices  25.3 us (13%)
  between operations  14.2 us (8%)
  local copies, waits for them, and re-layouts  5.69 us (3%)
    pallas_call x8, Pallas kernels, call(): pl.pallas_call(kernel, out_shape=outs, in_specs=[SMEM] + [VMEM] * (len(in...  32.5 us
    ppermute x1, waiting for transfers between devices, body(): other = lax.ppermute(low, 'w', [(0, 1), (1, 0)])  31 us
    all_to_all x1, blocking collectives, body(): parts = lax.all_to_all(products, 'x', 0, 0, tiled=True)  29.3 us
    all_to_all x1, blocking collectives, body(): lax.all_to_all(finished.reshape(EXPERTS, ROOM, width), ('z', 'y'), 0, 0,...  22.8 us
    all_to_all x1, waiting for transfers between devices, body(): lax.all_to_all(outbound.reshape(EXPERTS, ROOM, width), ('z', 'y'), 0, 0,...  12.2 us
    all_to_all x1, starting transfers between devices, body(): lax.all_to_all(outbound.reshape(EXPERTS, ROOM, width), ('z', 'y'), 0, 0,...  10.4 us
    all_to_all x1, waiting for transfers between devices, body(): hidden_all = lax.all_to_all(hidden, 'x', 0, 0, tiled=True)  8.08 us
    ppermute x4, starting transfers between devices, body(): swap = lambda a: lax.ppermute(a, 'c', [(0, 1), (1, 0)])  7.79 us
  transfers between devices with their start and end apart: 8, of which 6 were waited for; matrix products, arithmetic and copies ran while one was open for 1% of the time, Pallas kernels for 5%

profile of v1, /device:TPU:270, one launch (start us, length us, event | category | flops | bytes accessed | tf_op | source)
XLA Modules:
  0.0 187.7 jit_solution(12578728103987054192)
XLA Ops:
  7.2 1.1 constant_dynamic-slice_fusion.2
  8.3 0.7 pad_maximum_fusion.1
  9.1 0.8 copy.11.ids_ref
  9.9 0.8 copy.12.w_ref
  10.6 0.1 pad_add_fusion.place
  10.7 0.8 copy-done.5
  11.5 2.1 %dispatch.1 = (bf16[768,256]{1,0:T(8,128)(2,1)}, f32[64,768]{1,0:T(8,128)S(1)}) custom-call(s32[2]{0:T(128)S(1)} %pad_add_fusion.place, s32[64,8]{1,0:T(8,128)S(1)} %copy.11.ids_ref, f32[64,8]{1,0:T(8,128)S(1)} %copy.12.w_ref, bf16[64,256]{1,0:T(8,128)(2,1)S(1)} %copy-done.5), custom_call_target="tpu_custom_call" | custom-call | flops 39321600 | bytes 1048576 | tf_op jit(solution)/shard_map/dispatch/pallas_call | solution.py:30
  13.6 10.4 %all-to-all-start = ((bf16[32,24,256]{2,1,0:T(8,128)(2,1)}), bf16[32,24,256]{2,1,0:T(8,128)(2,1)S(1)}, u32[]{:S(2)}, u32[]{:S(2)}) async-start(bf16[32,24,256]{2,1,0:T(8,128)(2,1)} %bitcast.2), calls=%async_computation | async-start | bytes 786432 | tf_op jit(solution)/shard_map/all_to_all | solution.py:247
  24.0 0.1 constant_dynamic-slice_fusion
  24.1 1.0 pad_maximum_fusion
  25.1 1.9 %collective-permute-start.1 = (bf16[2,256,768]{2,1,0:T(8,128)(2,1)}, bf16[2,256,768]{2,1,0:T(8,128)(2,1)S(1)}, u32[]{:S(2)}, u32[]{:S(2)}) collective-permute-start(bf16[2,256,768]{2,1,0:T(8,128)(2,1)} %pad_maximum_fusion), channel_id=1, source_target_pairs={{0,32},{32,0},{1,33},{33,1},{2,34},{34,2},{3,35},{35,3},{4,36},{36... | collective-permute-start | bytes 2359304 | tf_op jit(solution)/shard_map/ppermute | solution.py:234
  27.0 12.2 %all-to-all-done = bf16[32,24,256]{2,1,0:T(8,128)(2,1)S(1)} async-done(((bf16[32,24,256]{2,1,0:T(8,128)(2,1)}), bf16[32,24,256]{2,1,0:T(8,128)(2,1)S(1)}, u32[]{:S(2)}, u32[]{:S(2)}) %all-to-all-start) | async-done | bytes 393248 | tf_op jit(solution)/shard_map/all_to_all | solution.py:247
  39.1 1.9 %collective-permute-start = (bf16[768,256]{1,0:T(8,128)(2,1)S(1)}, bf16[768,256]{1,0:T(8,128)(2,1)S(1)}, u32[]{:S(2)}, u32[]{:S(2)}) collective-permute-start(bf16[768,256]{1,0:T(8,128)(2,1)S(1)} %bitcast.14), channel_id=1, source_target_pairs={{0,32},{32,0},{1,33},{33,1},{2,34},{34,2},{3,35},{35,3},{4,36},{36... | collective-permute-start | bytes 1179656 | tf_op jit(solution)/shard_map/ppermute | solution.py:234
  41.1 1.7 collective-permute-done.sibling_ref
  42.7 2.1 %products.1 = bf16[4,144,1536]{2,1,0:T(8,128)(2,1)S(1)} custom-call(s32[2]{0:T(128)S(1)} %pad_add_fusion.place, bf16[768,256]{1,0:T(8,128)(2,1)S(1)} %bitcast.15, bf16[768,256]{1,0:T(8,128)(2,1)S(1)} %collective-permute-done.sibling_ref, bf16[256,1536]{1,0:T(8,128)(2,1)S(1)} %bitcast.11, bf16[256,1536]{1,0:T(8,128)(2,1)S(1)} %bitcast.12, ...), custom_call_target="tpu_custom_call" | custom-call | flops 905969664 | bytes 4194304 | tf_op jit(solution)/shard_map/products/pallas_call | solution.py:30
  44.8 29.3 %all_to_all.20.parts_ref = bf16[4,144,1536]{2,1,0:T(8,128)(2,1)S(1)} all-to-all(bf16[4,144,1536]{2,1,0:T(8,128)(2,1)S(1)} %products.1), channel_id=1, replica_groups=mesh['w'=2,'x'=4,'c'=2,'z'=4,'y'=8] {'x'}, dimensions={0} | all-to-all | bytes 3538944 | tf_op jit(solution)/shard_map/all_to_all | solution.py:271
  74.1 0.8 sum_parts.1
  74.9 1.9 %collective-permute-start.2 = (bf16[144,1536]{1,0:T(8,128)(2,1)S(1)}, bf16[144,1536]{1,0:T(8,128)(2,1)S(1)}, u32[]{:S(2)}, u32[]{:S(2)}) collective-permute-start(bf16[144,1536]{1,0:T(8,128)(2,1)S(1)} %get-tuple-element.11), channel_id=1, source_target_pairs={{0,256},{256,0},{1,257},{257,1},{2,258},{258,2},{3,259},{259,3},{4... | collective-permute-start | bytes 1327112 | tf_op jit(solution)/shard_map/ppermute | solution.py:280
  76.8 31.0 %collective-permute-done.2.other_ref = bf16[144,1536]{1,0:T(8,128)(2,1)S(1)} collective-permute-done((bf16[144,1536]{1,0:T(8,128)(2,1)S(1)}, bf16[144,1536]{1,0:T(8,128)(2,1)S(1)}, u32[]{:S(2)}, u32[]{:S(2)}) %collective-permute-start.2) | collective-permute-done | bytes 442400 | tf_op jit(solution)/shard_map/ppermute | solution.py:280
  107.8 1.6 hidden.1
  109.4 5.1 %all-to-all-start.2 = ((bf16[4,144,768]{2,1,0:T(8,128)(2,1)}), bf16[4,144,768]{2,1,0:T(8,128)(2,1)S(1)}, u32[]{:S(2)}, u32[]{:S(2)}) async-start(bf16[4,144,768]{2,1,0:T(8,128)(2,1)} %hidden.1), calls=%async_computation.2 | async-start | bytes 1769472 | tf_op jit(solution)/shard_map/all_to_all | solution.py:290
  114.6 1.9 %collective-permute-start.3 = (bf16[768,256]{1,0:T(8,128)(2,1)S(1)}, bf16[768,256]{1,0:T(8,128)(2,1)S(1)}, u32[]{:S(2)}, u32[]{:S(2)}) collective-permute-start(bf16[768,256]{1,0:T(8,128)(2,1)S(1)} %dynamic-slice_bitcast_fusion), channel_id=1, source_target_pairs={{0,32},{32,0},{1,33},{33,1},{2,34},{34,2},{3,35},{35,3},{4,36},{36... | collective-permute-start | bytes 1179656 | tf_op jit(solution)/shard_map/ppermute | solution.py:234
  116.5 1.7 collective-permute-done.3.swapped_ref
  118.2 8.1 %all-to-all-done.2.hidden_ref = bf16[4,144,768]{2,1,0:T(8,128)(2,1)S(1)} async-done(((bf16[4,144,768]{2,1,0:T(8,128)(2,1)}), bf16[4,144,768]{2,1,0:T(8,128)(2,1)S(1)}, u32[]{:S(2)}, u32[]{:S(2)}) %all-to-all-start.2) | async-done | bytes 884768 | tf_op jit(solution)/shard_map/all_to_all | solution.py:290
  126.3 1.2 project.1
  127.5 2.1 %collective-permute-start.4 = (bf16[576,256]{1,0:T(8,128)(2,1)S(1)}, bf16[576,256]{1,0:T(8,128)(2,1)S(1)}, u32[]{:S(2)}, u32[]{:S(2)}) collective-permute-start(bf16[576,256]{1,0:T(8,128)(2,1)S(1)} %get-tuple-element.13), channel_id=1, source_target_pairs={{0,32},{32,0},{1,33},{33,1},{2,34},{34,2},{3,35},{35,3},{4,36},{36... | collective-permute-start | bytes 884744 | tf_op jit(solution)/shard_map/ppermute | solution.py:234
  129.6 1.5 collective-permute-done.4.other_ref
  131.1 1.0 finish.1
  132.1 22.8 %all_to_all.21 = bf16[32,24,256]{2,1,0:T(8,128)(2,1)S(1)} all-to-all(bf16[32,24,256]{2,1,0:T(8,128)(2,1)S(1)} %bitcast.17), channel_id=1, replica_groups=mesh['w'=2,'x'=4,'c'=2,'z'=4,'y'=8] {'z','y'}, dimensions={0} | all-to-all | bytes 786432 | tf_op jit(solution)/shard_map/all_to_all | solution.py:307
  154.9 1.5 combine.1
  156.4 2.2 %copy-done.3 = bf16[8192,256]{1,0:T(8,128)(2,1)S(1)} copy-done((bf16[8192,256]{1,0:T(8,128)(2,1)S(1)}, bf16[8192,256]{1,0:T(8,128)(2,1)}, u32[]{:S(2)}) %copy-start.3) | copy-done | bytes 4194328
  158.6 22.2 %attention.1 = bf16[512,256]{1,0:T(8,128)(2,1)} custom-call(s32[2]{0:T(128)S(1)} %pad_add_fusion.place, bf16[512,256]{1,0:T(8,128)(2,1)S(1)} %copy-done.4, bf16[8192,256]{1,0:T(8,128)(2,1)S(1)} %copy-done.3), custom_call_target="tpu_custom_call" | custom-call | flops 4294967296 | bytes 5242880 | tf_op jit(solution)/shard_map/attention/pallas_call | solution.py:30
  (15 shorter events, 0.1 us)
Async XLA Ops:
  7.2 16.9 %copy-start = (bf16[1,256,1536]{2,1,0:T(8,128)(2,1)S(1)}, bf16[1,256,1536]{2,1,0:T(8,128)(2,1)}, u32[]{:S(2)}) copy-start(bf16[1,256,1536]{2,1,0:T(8,128)(2,1)} %param.15) | copy-start | bytes 2359300
  7.2 16.9 %copy-start.1 = (bf16[1,256,1536]{2,1,0:T(8,128)(2,1)S(1)}, bf16[1,256,1536]{2,1,0:T(8,128)(2,1)}, u32[]{:S(2)}) copy-start(bf16[1,256,1536]{2,1,0:T(8,128)(2,1)} %param.16) | copy-start | bytes 2359300
  7.2 149.2 %all-gather.2.cloned.1.call-start = ((), (), s32[]{:S(2)}) async-start(), calls=%async_computation.4 | async-start | bytes 4456448 | tf_op jit(solution)/shard_map/all_gather | solution.py:236
  10.7 0.8 copy-start.5
  13.6 25.6 %all-to-all-start = ((bf16[32,24,256]{2,1,0:T(8,128)(2,1)}), bf16[32,24,256]{2,1,0:T(8,128)(2,1)S(1)}, u32[]{:S(2)}, u32[]{:S(2)}) async-start(bf16[32,24,256]{2,1,0:T(8,128)(2,1)} %bitcast.2), calls=%async_computation | async-start | bytes 786432 | tf_op jit(solution)/shard_map/all_to_all | solution.py:247
  25.1 16.0 %collective-permute-start.1 = (bf16[2,256,768]{2,1,0:T(8,128)(2,1)}, bf16[2,256,768]{2,1,0:T(8,128)(2,1)S(1)}, u32[]{:S(2)}, u32[]{:S(2)}) collective-permute-start(bf16[2,256,768]{2,1,0:T(8,128)(2,1)} %pad_maximum_fusion), channel_id=1, source_target_pairs={{0,32},{32,0},{1,33},{33,1},{2,34},{34,2},{3,35},{35,3},{4,36},{36... | collective-permute-start | bytes 2359304 | tf_op jit(solution)/shard_map/ppermute | solution.py:234
  39.1 3.6 %collective-permute-start = (bf16[768,256]{1,0:T(8,128)(2,1)S(1)}, bf16[768,256]{1,0:T(8,128)(2,1)S(1)}, u32[]{:S(2)}, u32[]{:S(2)}) collective-permute-start(bf16[768,256]{1,0:T(8,128)(2,1)S(1)} %bitcast.14), channel_id=1, source_target_pairs={{0,32},{32,0},{1,33},{33,1},{2,34},{34,2},{3,35},{35,3},{4,36},{36... | collective-permute-start | bytes 1179656 | tf_op jit(solution)/shard_map/ppermute | solution.py:234
  74.9 32.9 %collective-permute-start.2 = (bf16[144,1536]{1,0:T(8,128)(2,1)S(1)}, bf16[144,1536]{1,0:T(8,128)(2,1)S(1)}, u32[]{:S(2)}, u32[]{:S(2)}) collective-permute-start(bf16[144,1536]{1,0:T(8,128)(2,1)S(1)} %get-tuple-element.11), channel_id=1, source_target_pairs={{0,256},{256,0},{1,257},{257,1},{2,258},{258,2},{3,259},{259,3},{4... | collective-permute-start | bytes 1327112 | tf_op jit(solution)/shard_map/ppermute | solution.py:280
  107.8 6.8 %copy-start.2 = (bf16[1,1536,256]{2,1,0:T(8,128)(2,1)S(1)}, bf16[1,1536,256]{2,1,0:T(8,128)(2,1)}, u32[]{:S(2)}) copy-start(bf16[1,1536,256]{2,1,0:T(8,128)(2,1)} %param.17) | copy-start | bytes 2359300
  109.4 16.9 %all-to-all-start.2 = ((bf16[4,144,768]{2,1,0:T(8,128)(2,1)}), bf16[4,144,768]{2,1,0:T(8,128)(2,1)S(1)}, u32[]{:S(2)}, u32[]{:S(2)}) async-start(bf16[4,144,768]{2,1,0:T(8,128)(2,1)} %hidden.1), calls=%async_computation.2 | async-start | bytes 1769472 | tf_op jit(solution)/shard_map/all_to_all | solution.py:290
  114.6 3.6 %collective-permute-start.3 = (bf16[768,256]{1,0:T(8,128)(2,1)S(1)}, bf16[768,256]{1,0:T(8,128)(2,1)S(1)}, u32[]{:S(2)}, u32[]{:S(2)}) collective-permute-start(bf16[768,256]{1,0:T(8,128)(2,1)S(1)} %dynamic-slice_bitcast_fusion), channel_id=1, source_target_pairs={{0,32},{32,0},{1,33},{33,1},{2,34},{34,2},{3,35},{35,3},{4,36},{36... | collective-permute-start | bytes 1179656 | tf_op jit(solution)/shard_map/ppermute | solution.py:234
  127.5 28.9 %copy-start.4 = (bf16[512,256]{1,0:T(8,128)(2,1)S(1)}, bf16[512,256]{1,0:T(8,128)(2,1)}, u32[]{:S(2)}) copy-start(bf16[512,256]{1,0:T(8,128)(2,1)} %q_ref.1) | copy-start | bytes 786436
  127.5 3.6 %collective-permute-start.4 = (bf16[576,256]{1,0:T(8,128)(2,1)S(1)}, bf16[576,256]{1,0:T(8,128)(2,1)S(1)}, u32[]{:S(2)}, u32[]{:S(2)}) collective-permute-start(bf16[576,256]{1,0:T(8,128)(2,1)S(1)} %get-tuple-element.13), channel_id=1, source_target_pairs={{0,32},{32,0},{1,33},{33,1},{2,34},{34,2},{3,35},{35,3},{4,36},{36... | collective-permute-start | bytes 884744 | tf_op jit(solution)/shard_map/ppermute | solution.py:234
  156.4 2.2 %copy-start.3 = (bf16[8192,256]{1,0:T(8,128)(2,1)S(1)}, bf16[8192,256]{1,0:T(8,128)(2,1)}, u32[]{:S(2)}) copy-start(bf16[8192,256]{1,0:T(8,128)(2,1)} %all-gather.2.cloned.1.call-done.kv_ref) | copy-start | bytes 12582916
Sparse Core Ops, SparseCore 0:
  11.9 76.2 all-gather.1

commit v2 on v1

v2 whole, which is shorter than its diff:
```python
import jax
import jax.numpy as jnp
import numpy as np
from jax import lax
from jax.experimental import pallas as pl
from jax.experimental.pallas import tpu as pltpu
from jax.sharding import Mesh
from jax.sharding import PartitionSpec as P

FF = 1536
HEADS = 64
KVH = 4
HD = 128
TOPK = 8
EXPERTS = 32
CAP = 18
HALF_CAP = CAP // 2
GROUPS = 4
ROOM = 40
SLOTS = EXPERTS * ROOM
ROWS = EXPERTS * HALF_CAP
F32 = jnp.float32
BF16 = jnp.bfloat16
LOG2E = 1.4426950408889634
TILE = 256
CONTRACT_LAST = (((1,), (1,)), ((), ()))
CONTRACT_FIRST = (((0,), (0,)), ((), ()))
SMEM = pl.BlockSpec(memory_space=pltpu.SMEM)
VMEM = pl.BlockSpec(memory_space=pltpu.VMEM)


def call(
    kernel, outs, ins, flops, moved, limit=32, scratch=(), transcendentals=0, name=None, after=()
):
    count = len(ins)

    def run(*refs):
        kernel(*refs[:count], *refs[count + len(after) :])

    return pl.pallas_call(
        run,
        out_shape=outs,
        in_specs=[SMEM] + [VMEM] * (count - 1) + [pl.BlockSpec(memory_space=pl.ANY)] * len(after),
        out_specs=jax.tree.map(lambda _: VMEM, outs),
        scratch_shapes=scratch,
        compiler_params=pltpu.CompilerParams(vmem_limit_bytes=limit << 20),
        cost_estimate=pl.CostEstimate(
            flops=flops, bytes_accessed=moved, transcendentals=transcendentals
        ),
        name=name,
    )(*ins, *after)


def shape(dims, dtype=BF16):
    return jax.ShapeDtypeStruct(dims, dtype)


def spread_queries(q_ref, q2):
    rows, heads = q_ref.shape[0], q_ref.shape[1] // HD
    for h in range(heads):
        q = q_ref[:, h * HD : (h + 1) * HD].astype(F32) * (LOG2E * HD**-0.5)
        high = q.astype(BF16)
        q2[h * rows : (h + 1) * rows, :HD] = high
        q2[h * rows : (h + 1) * rows, HD:] = (q - high.astype(F32)).astype(BF16)


def key_block(kv_ref, i):
    k, v = kv_ref[i, :, :HD], kv_ref[i, :, HD:]
    return (
        jnp.concatenate([k, k], axis=1),
        jnp.concatenate([v, jnp.ones_like(v)], axis=1),
    )


def attend(q2, kk, v1, peak, acc, rows, diagonal):
    keys = kk.shape[0]
    for t in range(q2.shape[0] // TILE):
        sl = slice(t * TILE, (t + 1) * TILE)
        s = lax.dot_general(q2[sl, :], kk, CONTRACT_LAST, preferred_element_type=F32)
        if diagonal:
            query = (t * TILE) % rows + lax.broadcasted_iota(jnp.int32, (TILE, keys), 0)
            key = lax.broadcasted_iota(jnp.int32, (TILE, keys), 1)
            s = jnp.where(query >= key, s, -1e30)
        new = jnp.max(s, axis=1, keepdims=True)
        if not diagonal:
            old = peak[sl, :1]
            new = jnp.maximum(old, new)
        peak[sl, :] = jnp.broadcast_to(new, (TILE, HD))
        mixed = jnp.dot(jnp.exp2(s - new).astype(BF16), v1, preferred_element_type=F32)
        acc[sl, :] = mixed if diagonal else acc[sl, :] * jnp.exp2(old - new) + mixed


def attention_own_kernel(place, q_ref, kv_ref, sibling_ref, acc, peak, q2):
    rows = q_ref.shape[0]
    spread_queries(q_ref, q2)
    attend(q2, *key_block(kv_ref, 0), peak, acc, rows, True)

    def earlier(i, carry):
        attend(q2, *key_block(kv_ref, i), peak, acc, rows, False)
        return carry

    def earlier_sibling(i, carry):
        attend(q2, *key_block(sibling_ref, i), peak, acc, rows, False)
        return carry

    chip, core = place[0], place[1]
    lax.fori_loop(1, chip + 1, earlier, 0)
    lax.fori_loop(1 - core, chip + 1, earlier_sibling, 0)


def attention_far_kernel(place, q_ref, kv_ref, acc_in, peak_in, acc, peak, q2):
    spread_queries(q_ref, q2)
    acc[...] = acc_in[...]
    peak[...] = peak_in[...]

    def earlier(i, carry):
        attend(q2, *key_block(kv_ref, i), peak, acc, q_ref.shape[0], False)
        return carry

    lax.fori_loop(0, place[2] * kv_ref.shape[0], earlier, 0)


def attention_last_kernel(place, q_ref, kv_ref, acc_in, peak_in, o_ref, q2, acc, peak):
    rows, heads = q_ref.shape[0], q_ref.shape[1] // HD
    attention_far_kernel(place, q_ref, kv_ref, acc_in, peak_in, acc, peak, q2)
    for h in range(heads):
        a = acc[h * rows : (h + 1) * rows, :]
        o_ref[:, h * HD : (h + 1) * HD] = (a[:, :HD] / a[:, HD:]).astype(o_ref.dtype)


def attention(kernel, place, q, keys, state, last, name, after):
    stacked = q.shape[0] * q.shape[1] // HD
    results = (shape((stacked, 2 * HD), F32), shape((stacked, HD), F32))
    scratch = [pltpu.VMEM((stacked, 2 * HD), BF16)]
    if last:
        scratch = scratch + [pltpu.VMEM(r.shape, r.dtype) for r in results]
        results = shape(q.shape)
    count = sum(k.shape[0] * k.shape[1] for k in keys)
    return call(
        kernel,
        results,
        (place, q, *keys, *state),
        flops=4 * stacked * count * HD,
        moved=5 << 20,
        transcendentals=stacked * count,
        scratch=scratch,
        name=name,
        after=after,
    )


def places(ids_ref, core):
    count = ids_ref.shape[1]
    expert = lax.broadcasted_iota(jnp.int32, (EXPERTS, count), 0)
    chosen = jnp.zeros((EXPERTS, count), F32)
    for k in range(TOPK):
        chosen = chosen + jnp.where(ids_ref[k : k + 1, :] == expert, 1.0, 0.0)
    chosen = chosen.astype(BF16)
    earlier = lax.broadcasted_iota(jnp.int32, (count, count), 0) < lax.broadcasted_iota(
        jnp.int32, (count, count), 1
    )
    rank = jnp.dot(chosen, jnp.where(earlier, 1.0, 0.0).astype(BF16), preferred_element_type=F32)
    inside = lax.broadcasted_iota(jnp.int32, (SLOTS, EXPERTS), 0) - ROOM * lax.broadcasted_iota(
        jnp.int32, (SLOTS, EXPERTS), 1
    )
    own = (inside >= 0) & (inside < ROOM)
    spread = jnp.where(own, 1.0, 0.0).astype(BF16)
    row = jnp.sum(jnp.where(own, inside.astype(F32), 0.0), axis=1, keepdims=True)
    group = jnp.zeros_like(row)
    for g in range(1, GROUPS + 1):
        group = group + jnp.where(row >= g * HALF_CAP, 1.0, 0.0)
    wanted = row - group * HALF_CAP + (core * HALF_CAP).astype(F32)
    hits = jnp.dot(spread, chosen, preferred_element_type=F32)
    ranks = jnp.dot(spread, rank.astype(BF16), preferred_element_type=F32)
    placed = (hits > 0.5) & (ranks == wanted) & (group < GROUPS)
    return spread, placed, group


def dispatch_kernel(place, ids_ref, own_ref, sibling_ref, out_ref):
    core = place[1]
    _, placed, group = places(ids_ref, core)
    own, sibling = own_ref[...], sibling_ref[...]
    first, second = jnp.where(core == 0, own, sibling), jnp.where(core == 0, sibling, own)
    tokens = jnp.concatenate([first, second], axis=1)
    total = jnp.zeros(out_ref.shape, F32)
    for g in range(GROUPS):
        onehot = jnp.where(placed & (group == g), 1.0, 0.0).astype(BF16)
        total = total + jnp.dot(
            onehot, tokens[:, g * HD : (g + 1) * HD], preferred_element_type=F32
        )
    out_ref[...] = total.astype(BF16)


def combine_map_kernel(place, ids_ref, w_ref, out_ref):
    spread, placed, _ = places(ids_ref, place[1])
    expert = lax.broadcasted_iota(jnp.int32, (EXPERTS, ids_ref.shape[1]), 0)
    weight = jnp.zeros(expert.shape, F32)
    for k in range(TOPK):
        weight = weight + jnp.where(ids_ref[k : k + 1, :] == expert, w_ref[k : k + 1, :], 0.0)
    weights = jnp.dot(spread.astype(F32), weight, precision=lax.Precision.HIGHEST)
    out_ref[...] = jnp.where(placed, weights, 0.0)


def packing():
    row = np.arange(SLOTS)
    inside = row % ROOM
    tight = np.where(
        inside < GROUPS * HALF_CAP, row // ROOM * HALF_CAP + inside % HALF_CAP, -1
    )
    return jnp.asarray(np.arange(ROWS)[:, None] == tight[None, :], BF16)


def row_groups():
    row = lax.broadcasted_iota(jnp.int32, (SLOTS, 1), 0)
    inside = row - ROOM * lax.shift_right_logical(row * 1639, 16)
    group = jnp.zeros_like(row)
    for g in range(1, GROUPS + 1):
        group = group + jnp.where(inside >= g * HALF_CAP, 1, 0)
    return group


def widen(block):
    group = row_groups()
    return jnp.concatenate(
        [jnp.where(group == g, block, 0.0).astype(BF16) for g in range(GROUPS)], axis=1
    )


def products_kernel(
    place, pack_ref, rows_ref, gate_ref, up_ref, sibling_gate_ref, sibling_up_ref, out_ref
):
    rows = jnp.dot(pack_ref[...], widen(rows_ref[...]), preferred_element_type=F32)
    rows = rows.astype(BF16)
    half = rows.shape[1] // 2
    first, second = rows[:, :half], rows[:, half:]
    core = place[1]
    own, sibling = jnp.where(core == 0, first, second), jnp.where(core == 0, second, first)
    cols = out_ref.shape[2] // 2
    for i in range(out_ref.shape[0]):
        sl = slice(i * cols, (i + 1) * cols)
        for j, (mine, its) in enumerate(((gate_ref, sibling_gate_ref), (up_ref, sibling_up_ref))):
            out_ref[i, :, j * cols : (j + 1) * cols] = (
                jnp.dot(own, mine[:, sl], preferred_element_type=F32)
                + jnp.dot(sibling, its[:, sl], preferred_element_type=F32)
            ).astype(BF16)


def sum_kernel(place, parts_ref, wide_ref, low_ref):
    total = parts_ref[0].astype(F32)
    for i in range(1, parts_ref.shape[0]):
        total = total + parts_ref[i].astype(F32)
    wide_ref[...] = total
    low_ref[...] = total.astype(BF16)


def hidden_kernel(place, wide_ref, other_ref, out_ref):
    total = wide_ref[...] + other_ref[...].astype(F32)
    cols = total.shape[1] // 2
    gate, up = total[:, :cols], total[:, cols:]
    hidden = (gate / (1.0 + jnp.exp(-gate)) * up).astype(BF16)
    for i in range(out_ref.shape[0]):
        out_ref[i] = hidden


def project_kernel(place, pack_ref, hidden_ref, down_ref, swapped_ref, out_ref):
    hidden = jnp.concatenate([hidden_ref[i] for i in range(hidden_ref.shape[0])], axis=1)
    own = jnp.dot(hidden, down_ref[...], preferred_element_type=F32).astype(BF16)
    sibling = jnp.dot(hidden, swapped_ref[...], preferred_element_type=F32).astype(BF16)
    core = place[1]
    first, second = jnp.where(core == 0, own, sibling), jnp.where(core == 0, sibling, own)
    result = jnp.concatenate([first, second], axis=1)
    group = row_groups()
    wide = lax.dot_general(pack_ref[...], result, CONTRACT_FIRST, preferred_element_type=F32)
    total = jnp.zeros(out_ref.shape, F32)
    for g in range(GROUPS):
        total = jnp.where(group == g, wide[:, g * HD : (g + 1) * HD], total)
    out_ref[...] = total.astype(BF16)


def combine_kernel(place, combine_ref, back_ref, own_ref, sibling_ref):
    c, wide = combine_ref[...], widen(back_ref[...])
    total = jnp.zeros((c.shape[1], wide.shape[1]), F32)
    for _ in range(3):
        part = c.astype(BF16)
        total = total + lax.dot_general(part, wide, CONTRACT_FIRST, preferred_element_type=F32)
        c = c - part.astype(F32)
    half = total.shape[1] // 2
    core = place[1]
    own_ref[...] = jnp.where(core == 0, total[:, :half], total[:, half:])
    sibling_ref[...] = jnp.where(core == 0, total[:, half:], total[:, :half])


def add_kernel(place, own_ref, other_ref, out_ref):
    out_ref[...] = (own_ref[...] + other_ref[...]).astype(BF16)


def head_columns(heads, key_states, value_states, after):
    rows = key_states.shape[0]
    picks = [
        pl.BlockSpec((rows, HD), lambda i, at, n=n: (0, at[n])) for n in (0, 1) for _ in range(2)
    ]

    def run(place, key_ref, value_ref, other_key_ref, other_value_ref, *refs):
        out_ref, other_ref = refs[-2:]
        out_ref[:, :HD], out_ref[:, HD:] = key_ref[...], value_ref[...]
        other_ref[:, :HD], other_ref[:, HD:] = other_key_ref[...], other_value_ref[...]

    return pl.pallas_call(
        run,
        out_shape=[shape((rows, 2 * HD))] * 2,
        grid_spec=pltpu.PrefetchScalarGridSpec(
            num_scalar_prefetch=1,
            grid=(1,),
            in_specs=picks + [pl.BlockSpec(memory_space=pl.ANY)] * len(after),
            out_specs=[pl.BlockSpec((rows, 2 * HD), lambda i, at: (0, 0))] * 2,
        ),
        cost_estimate=pl.CostEstimate(flops=0, bytes_accessed=0, transcendentals=0),
        name="head_columns",
    )(
        jnp.stack(heads).astype(jnp.int32),
        key_states,
        value_states,
        key_states,
        value_states,
        *after,
    )


def stack_kernel(place, *refs):
    for i, ref in enumerate(refs[:-1]):
        refs[-1][i] = ref[...]


def stack(place, parts, after, name):
    return call(
        stack_kernel,
        shape((len(parts), *parts[0].shape)),
        (place, *parts),
        flops=0,
        moved=0,
        name=name,
        after=after,
    )


def body(
    queries,
    key_states,
    value_states,
    token_states,
    expert_ids,
    combine_weights,
    gate_weight,
    up_weight,
    down_weight,
):
    core, z_lo = lax.axis_index("c"), lax.axis_index("z")
    half = lax.axis_index("w")
    place = jnp.stack([lax.axis_index("x"), core, half]).astype(jnp.int32)
    swap = lambda a: lax.ppermute(a, "c", [(0, 1), (1, 0)])
    gate, up, down = gate_weight[0], up_weight[0], down_weight[0]
    count, width = token_states.shape
    ids = expert_ids.T
    block = (EXPERTS, ROOM, HD)
    pack = packing()

    outbound = call(
        dispatch_kernel,
        shape((SLOTS, HD)),
        (place, ids, token_states, swap(token_states)),
        flops=2 * SLOTS * 64 * 600,
        moved=1 << 20,
        name="dispatch",
    )
    received = lax.all_to_all(outbound.reshape(block), ("z", "y"), 0, 0, tiled=True)

    z_count, lanes = lax.axis_size("z"), lax.axis_size("x")
    kv, kv_near = head_columns(
        [z_lo, z_count - 1 - z_lo], key_states, value_states, (outbound,)
    )
    kv_far = lax.ppermute(
        kv_near, ("w", "z"), [(z, 2 * z_count - 1 - z) for z in range(z_count)]
    )
    near = [kv] + [
        lax.ppermute(kv, "x", [(x, x + k) for x in range(lanes - k)]) for k in range(1, lanes)
    ]
    far = [kv_far] + [
        lax.ppermute(
            kv_far, ("w", "x"), [(lanes + x, lanes + (x + k) % lanes) for x in range(lanes)]
        )
        for k in range(1, lanes)
    ]
    cols = 2 * FF // lanes
    products = call(
        products_kernel,
        shape((lanes, ROWS, cols)),
        (place, pack, received.reshape(SLOTS, HD), gate, up, swap(gate), swap(up)),
        flops=2 * ROWS * 4 * width * FF,
        moved=5 << 20,
        name="products",
    )
    parts = lax.all_to_all(products, "x", 0, 0, tiled=True)
    near = stack(place, near, (products,), "stack_near")
    acc, peak = attention(
        attention_own_kernel,
        place,
        queries,
        (near, swap(near)),
        (),
        False,
        "attention_near",
        (products,),
    )
    wide, low = call(
        sum_kernel,
        (shape((ROWS, cols), F32), shape((ROWS, cols))),
        (place, parts),
        flops=ROWS * cols * 4,
        moved=3 << 20,
        name="sum_parts",
        after=(acc, kv_far),
    )
    other = lax.ppermute(low, "w", [(0, 1), (1, 0)])
    combine_map = call(
        combine_map_kernel,
        shape((SLOTS, count), F32),
        (place, ids, combine_weights.T),
        flops=2 * SLOTS * 64 * 600,
        moved=1 << 20,
        name="combine_map",
        after=(low,),
    )
    hidden = call(
        hidden_kernel,
        shape((lanes, ROWS, cols // 2)),
        (place, wide, other),
        flops=ROWS * cols * 4,
        moved=2 << 20,
        transcendentals=ROWS * cols // 2,
        name="hidden",
    )
    hidden_all = lax.all_to_all(hidden, "x", 0, 0, tiled=True)
    far = stack(place, far, (hidden, combine_map), "stack_far")
    state = attention(
        attention_far_kernel,
        place,
        queries,
        (far,),
        (acc, peak),
        False,
        "attention_far",
        (hidden,),
    )
    finished = call(
        project_kernel,
        shape((SLOTS, HD)),
        (place, pack, hidden_all, down, swap(down)),
        flops=2 * ROWS * FF * 2 * width,
        moved=3 << 20,
        name="project",
        after=state,
    )
    back = lax.all_to_all(finished.reshape(block), ("z", "y"), 0, 0, tiled=True)
    context = attention(
        attention_last_kernel,
        place,
        queries,
        (swap(far),),
        state,
        True,
        "attention_last",
        (finished,),
    )
    own_sum, sibling_sum = call(
        combine_kernel,
        (shape((count, width), F32), shape((count, width), F32)),
        (place, combine_map, back.reshape(SLOTS, HD)),
        flops=6 * SLOTS * 2 * width * 64,
        moved=1 << 20,
        name="combine",
        after=(context,),
    )
    moe_output = call(
        add_kernel,
        shape((count, width)),
        (place, own_sum, swap(sibling_sum)),
        flops=count * width,
        moved=200 << 10,
        name="add_cores",
    )
    return (context, moe_output)


def solution(mesh):
    fine = Mesh(mesh.devices.reshape(2, 4, 2, 4, 8), ("w", "x", "c", "z", "y"))
    ctx, exp = ("w", "x", "c"), ("z", "y")
    in_specs = (
        P(ctx, exp),
        P(ctx, None),
        P(ctx, None),
        P(exp, ctx),
        P(exp, None),
        P(exp, None),
        P(exp, ctx, None),
        P(exp, ctx, None),
        P(exp, None, ctx),
    )
    out_specs = (P(ctx, exp), P(exp, ctx))
    return jax.shard_map(body, mesh=fine, in_specs=in_specs, out_specs=out_specs, check_vma=False)
```

time: 188 us -> 158 us (0.84)
  the two profiles are of different devices: /device:TPU:270 before, /device:TPU:1 now
where the time goes in v2:
time: 158 us; the launch traced here: 156 us
  starting transfers between devices  83.3 us (53%)
  Pallas kernels  30.9 us (20%)
  waiting for transfers between devices  27.2 us (17%)
  local copies, waits for them, and re-layouts  13.3 us (8%)
    ppermute x7, starting transfers between devices, body(): swap = lambda a: lax.ppermute(a, 'c', [(0, 1), (1, 0)])  29 us
    pallas_call x13, Pallas kernels, call(): pl.pallas_call(run, out_shape=outs, in_specs=[SMEM] + [VMEM] * (count - 1...  28.3 us
    unnamed x52, local copies, waits for them, and re-layouts  13.3 us
    ppermute x1, waiting for transfers between devices, body(): other = lax.ppermute(low, 'w', [(0, 1), (1, 0)])  11.2 us
    ppermute x3, starting transfers between devices, body(): lax.ppermute(kv, 'x', [(x, x + k) for x in range(lanes - k)])  10.2 us
    ppermute x1, starting transfers between devices, body(): lax.ppermute(kv_near, ('w', 'z'), [(z, 2 * z_count - 1 - z) for z in rang...  8.9 us
    all_to_all x1, starting transfers between devices, body(): hidden_all = lax.all_to_all(hidden, 'x', 0, 0, tiled=True)  7.72 us
    all_to_all x1, starting transfers between devices, body(): back = lax.all_to_all(finished.reshape(block), ('z', 'y'), 0, 0, tiled=True)  7.4 us
  transfers between devices with their start and end apart: 19, of which 6 were waited for; matrix products, arithmetic and copies ran while one was open for 0% of the time, Pallas kernels for 17%

profile of v2, /device:TPU:1, one launch (start us, length us, event | category | flops | bytes accessed | tf_op | source)
XLA Modules:
  0.0 156.4 jit_solution(13151451104916787089)
XLA Ops:
  0.7 8.9 %collective-permute-start.5 = (bf16[256,1536]{1,0:T(8,128)(2,1)}, bf16[256,1536]{1,0:T(8,128)(2,1)}, u32[]{:S(2)}, u32[]{:S(2)}) collective-permute-start(bf16[256,1536]{1,0:T(8,128)(2,1)} %bitcast.16), channel_id=1, source_target_pairs={{0,32},{32,0},{1,33},{33,1},{2,34},{34,2},{3,35},{35,3},{4,36},{36... | collective-permute-start | bytes 2359304 | tf_op jit(solution)/shard_map/ppermute | solution.py:360
  9.6 1.9 %collective-permute-start.6 = (bf16[256,1536]{1,0:T(8,128)(2,1)}, bf16[256,1536]{1,0:T(8,128)(2,1)}, u32[]{:S(2)}, u32[]{:S(2)}) collective-permute-start(bf16[256,1536]{1,0:T(8,128)(2,1)} %bitcast.18), channel_id=1, source_target_pairs={{0,32},{32,0},{1,33},{33,1},{2,34},{34,2},{3,35},{35,3},{4,36},{36... | collective-permute-start | bytes 2359304 | tf_op jit(solution)/shard_map/ppermute | solution.py:360
  11.5 2.4 %collective-permute-start = (bf16[64,256]{1,0:T(8,128)(2,1)}, bf16[64,256]{1,0:T(8,128)(2,1)S(1)}, u32[]{:S(2)}, u32[]{:S(2)}) collective-permute-start(bf16[64,256]{1,0:T(8,128)(2,1)} %refs_2_.1), channel_id=1, source_target_pairs={{0,32},{32,0},{1,33},{33,1},{2,34},{34,2},{3,35},{35,3},{4,36},{36... | collective-permute-start | bytes 98312 | tf_op jit(solution)/shard_map/ppermute | solution.py:360
  16.4 2.5 %dispatch.1.refs_0_ = bf16[1280,128]{1,0:T(8,128)(2,1)} custom-call(s32[3]{0:T(128)S(1)} %pad_add_fusion.refs_0_, s32[8,64]{1,0:T(8,128)S(1)} %bitcast.20, bf16[64,256]{1,0:T(8,128)(2,1)S(1)} %copy-done.17, bf16[64,256]{1,0:T(8,128)(2,1)S(1)} %collective-permute-done.refs_3_), custom_call_target="tpu_custom_call" | custom-call | flops 98304000 | bytes 1048576 | tf_op jit(solution)/shard_map/dispatch/pallas_call | solution.py:40
  18.9 7.3 %all-to-all-start = ((bf16[32,40,128]{2,1,0:T(8,128)(2,1)}), bf16[32,40,128]{2,1,0:T(8,128)(2,1)S(1)}, u32[]{:S(2)}, u32[]{:S(2)}) async-start(bf16[32,40,128]{2,1,0:T(8,128)(2,1)} %bitcast.6), calls=%async_computation | async-start | bytes 655360 | tf_op jit(solution)/shard_map/all_to_all | solution.py:375
  26.8 2.6 %head_columns.1 = (bf16[512,256]{1,0:T(8,128)(2,1)}, bf16[512,256]{1,0:T(8,128)(2,1)}) custom-call(s32[2]{0:T(128)} %pad_add_fusion.1.place, bf16[512,512]{1,0:T(8,128)(2,1)} %other_key_ref.1, bf16[512,512]{1,0:T(8,128)(2,1)} %other_value_ref.1, bf16[512,512]{1,0:T(8,128)(2,1)} %other_key_ref.1, bf16[512,512]{1,0:T(8,128)(2,1)} %other_value_ref.1, ...), custom_call_target="tpu_custom_call" | custom-call | tf_op jit(solution)/shard_map/head_columns/pallas_call | solution.py:308
  29.5 3.1 %collective-permute-start.7 = (bf16[512,256]{1,0:T(8,128)(2,1)}, bf16[512,256]{1,0:T(8,128)(2,1)S(1)}, u32[]{:S(2)}, u32[]{:S(2)}) collective-permute-start(bf16[512,256]{1,0:T(8,128)(2,1)} %get-tuple-element.13.refs_1_), channel_id=1, source_target_pairs={{0,64},{64,128},{128,192},{1,65},{65,129},{129,193},{2,66},{66,130... | collective-permute-start | bytes 786440 | tf_op jit(solution)/shard_map/ppermute | solution.py:385
  32.6 5.1 %collective-permute-start.8 = (bf16[512,256]{1,0:T(8,128)(2,1)}, bf16[512,256]{1,0:T(8,128)(2,1)}, u32[]{:S(2)}, u32[]{:S(2)}) collective-permute-start(bf16[512,256]{1,0:T(8,128)(2,1)} %get-tuple-element.13.refs_1_), channel_id=1, source_target_pairs={{0,128},{64,192},{1,129},{65,193},{2,130},{66,194},{3,131},{67,195... | collective-permute-start | bytes 786440 | tf_op jit(solution)/shard_map/ppermute | solution.py:385
  37.6 2.0 %collective-permute-start.9 = (bf16[512,256]{1,0:T(8,128)(2,1)}, bf16[512,256]{1,0:T(8,128)(2,1)}, u32[]{:S(2)}, u32[]{:S(2)}) collective-permute-start(bf16[512,256]{1,0:T(8,128)(2,1)} %get-tuple-element.13.refs_1_), channel_id=1, source_target_pairs={{0,192},{1,193},{2,194},{3,195},{4,196},{5,197},{6,198},{7,199},{8... | collective-permute-start | bytes 786440 | tf_op jit(solution)/shard_map/ppermute | solution.py:385
  39.7 4.8 %products.1.refs_5_.refs_4_ = bf16[4,288,768]{2,1,0:T(8,128)(2,1)} custom-call(s32[3]{0:T(128)S(1)} %pad_add_fusion.refs_0_, bf16[288,1280]{1,0:T(8,128)(2,1)S(1)} %copy-done, bf16[1280,128]{1,0:T(8,128)(2,1)S(1)} %bitcast.14, bf16[256,1536]{1,0:T(8,128)(2,1)S(1)} %bitcast.17, bf16[256,1536]{1,0:T(8,128)(2,1)S(1)} %bitcast.19, ...), custom_call_target="tpu_custom_call" | custom-call | flops 905969664 | bytes 5242880 | tf_op jit(solution)/shard_map/products/pallas_call | solution.py:40
  44.5 3.7 %all-to-all-start.1 = ((bf16[4,288,768]{2,1,0:T(8,128)(2,1)}), bf16[4,288,768]{2,1,0:T(8,128)(2,1)S(1)}, u32[]{:S(2)}, u32[]{:S(2)}) async-start(bf16[4,288,768]{2,1,0:T(8,128)(2,1)} %products.1.refs_5_.refs_4_), calls=%async_computation.1 | async-start | bytes 3538944 | tf_op jit(solution)/shard_map/all_to_all | solution.py:402
  50.0 3.2 %collective-permute-start.10 = (bf16[4,512,256]{2,1,0:T(8,128)(2,1)S(1)}, bf16[4,512,256]{2,1,0:T(8,128)(2,1)S(1)}, u32[]{:S(2)}, u32[]{:S(2)}) collective-permute-start(bf16[4,512,256]{2,1,0:T(8,128)(2,1)S(1)} %stack_near.1.refs_2_), channel_id=1, source_target_pairs={{0,32},{32,0},{1,33},{33,1},{2,34},{34,2},{3,35},{35,3},{4,36},{36... | collective-permute-start | bytes 3145736 | tf_op jit(solution)/shard_map/ppermute | solution.py:360
  53.2 8.9 %collective-permute-start.1 = (bf16[512,256]{1,0:T(8,128)(2,1)}, bf16[512,256]{1,0:T(8,128)(2,1)}, u32[]{:S(2)}, u32[]{:S(2)}) collective-permute-start(bf16[512,256]{1,0:T(8,128)(2,1)} %get-tuple-element.12), channel_id=1, source_target_pairs={{0,280},{8,272},{16,264},{24,256},{1,281},{9,273},{17,265},{25,257... | collective-permute-start | bytes 786440 | tf_op jit(solution)/shard_map/ppermute | solution.py:381
  63.1 3.0 %attention_near.1 = (f32[1024,256]{1,0:T(8,128)S(1)}, f32[1024,128]{1,0:T(8,128)S(1)}) custom-call(s32[3]{0:T(128)S(1)} %copy-done.14, bf16[512,256]{1,0:T(8,128)(2,1)S(1)} %copy-done.21, bf16[4,512,256]{2,1,0:T(8,128)(2,1)S(1)} %stack_near.1.refs_2_, bf16[4,512,256]{2,1,0:T(8,128)(2,1)S(1)} %collective-permute-done.10.refs_3_, ...), custom_call_target="tpu_custom_call" | custom-call | flops 2147483648 | bytes 5242880 | tf_op jit(solution)/shard_map/attention_near/pallas_call | solution.py:40
  66.9 6.2 %collective-permute-done.1.refs_3_.refs_1_ = bf16[512,256]{1,0:T(8,128)(2,1)} collective-permute-done((bf16[512,256]{1,0:T(8,128)(2,1)}, bf16[512,256]{1,0:T(8,128)(2,1)}, u32[]{:S(2)}, u32[]{:S(2)}) %collective-permute-start.1) | collective-permute-done | bytes 262176 | tf_op jit(solution)/shard_map/ppermute | solution.py:381
  74.5 5.1 %collective-permute-start.11 = (bf16[288,768]{1,0:T(8,128)(2,1)S(1)}, bf16[288,768]{1,0:T(8,128)(2,1)S(1)}, u32[]{:S(2)}, u32[]{:S(2)}) collective-permute-start(bf16[288,768]{1,0:T(8,128)(2,1)S(1)} %get-tuple-element.16.refs_3_), channel_id=1, source_target_pairs={{0,256},{256,0},{1,257},{257,1},{2,258},{258,2},{3,259},{259,3},{4... | collective-permute-start | bytes 1327112 | tf_op jit(solution)/shard_map/ppermute | solution.py:423
  80.4 3.9 %collective-permute-start.13 = (bf16[1536,256]{1,0:T(8,128)(2,1)}, bf16[1536,256]{1,0:T(8,128)(2,1)}, u32[]{:S(2)}, u32[]{:S(2)}) collective-permute-start(bf16[1536,256]{1,0:T(8,128)(2,1)} %bitcast.11.refs_3_), channel_id=1, source_target_pairs={{0,32},{32,0},{1,33},{33,1},{2,34},{34,2},{3,35},{35,3},{4,36},{36... | collective-permute-start | bytes 2359304 | tf_op jit(solution)/shard_map/ppermute | solution.py:360
  87.0 1.4 collective-permute-start.4
  88.4 11.2 %collective-permute-done.11.refs_2_ = bf16[288,768]{1,0:T(8,128)(2,1)S(1)} collective-permute-done((bf16[288,768]{1,0:T(8,128)(2,1)S(1)}, bf16[288,768]{1,0:T(8,128)(2,1)S(1)}, u32[]{:S(2)}, u32[]{:S(2)}) %collective-permute-start.11) | collective-permute-done | bytes 442400 | tf_op jit(solution)/shard_map/ppermute | solution.py:423
  99.6 1.7 %hidden.1.refs_5_ = bf16[4,288,384]{2,1,0:T(8,128)(2,1)} custom-call(s32[3]{0:T(128)S(1)} %copy-done.15, f32[288,768]{1,0:T(8,128)S(1)} %get-tuple-element.15.refs_1_, bf16[288,768]{1,0:T(8,128)(2,1)S(1)} %collective-permute-done.11.refs_2_), custom_call_target="tpu_custom_call" | custom-call | flops 884736 | bytes 2097152 | tf_op jit(solution)/shard_map/hidden/pallas_call | solution.py:40
  101.3 7.7 %all-to-all-start.2 = ((bf16[4,288,384]{2,1,0:T(8,128)(2,1)}), bf16[4,288,384]{2,1,0:T(8,128)(2,1)S(1)}, u32[]{:S(2)}, u32[]{:S(2)}) async-start(bf16[4,288,384]{2,1,0:T(8,128)(2,1)} %hidden.1.refs_5_), calls=%async_computation.2 | async-start | bytes 1769472 | tf_op jit(solution)/shard_map/all_to_all | solution.py:442
  110.0 1.6 %combine_map.1.refs_6_.refs_1_ = f32[1280,64]{1,0:T(8,128)S(1)} custom-call(s32[3]{0:T(128)S(1)} %copy-done.16, s32[8,64]{1,0:T(8,128)S(1)} %bitcast.21, f32[8,64]{1,0:T(8,128)S(1)} %bitcast.22, bf16[288,768]{1,0:T(8,128)(2,1)S(1)} %copy-done.10), custom_call_target="tpu_custom_call" | custom-call | flops 98304000 | bytes 1048576 | tf_op jit(solution)/shard_map/combine_map/pallas_call | solution.py:40
  111.7 2.3 %stack_far.1.refs_2_ = bf16[4,512,256]{2,1,0:T(8,128)(2,1)} custom-call(s32[3]{0:T(128)S(1)} %copy-done.16, bf16[512,256]{1,0:T(8,128)(2,1)} %collective-permute-done.1.refs_3_.refs_1_, bf16[512,256]{1,0:T(8,128)(2,1)} %collective-permute-done.2.refs_2_, bf16[512,256]{1,0:T(8,128)(2,1)} %collective-permute-done.3.refs_3_, ...), custom_call_target="tpu_custom_call" | custom-call | tf_op jit(solution)/shard_map/stack_far/pallas_call | solution.py:40
  114.0 2.6 %collective-permute-start.12 = (bf16[4,512,256]{2,1,0:T(8,128)(2,1)}, bf16[4,512,256]{2,1,0:T(8,128)(2,1)}, u32[]{:S(2)}, u32[]{:S(2)}) collective-permute-start(bf16[4,512,256]{2,1,0:T(8,128)(2,1)} %stack_far.1.refs_2_), channel_id=1, source_target_pairs={{0,32},{32,0},{1,33},{33,1},{2,34},{34,2},{3,35},{35,3},{4,36},{36... | collective-permute-start | bytes 3145736 | tf_op jit(solution)/shard_map/ppermute | solution.py:360
  116.6 1.6 %attention_far.1 = (f32[1024,256]{1,0:T(8,128)S(1)}, f32[1024,128]{1,0:T(8,128)S(1)}) custom-call(s32[3]{0:T(128)S(1)} %copy-done.16, bf16[512,256]{1,0:T(8,128)(2,1)S(1)} %copy-done.22, bf16[4,512,256]{2,1,0:T(8,128)(2,1)} %stack_far.1.refs_2_, f32[1024,256]{1,0:T(8,128)S(1)} %get-tuple-element.14.refs_2_.refs_3_, f32[1024,128]{1,0:T(8,128)S(1)} %copy-done.25, ...), custom_call_target="tpu_custom_call" | custom-call | flops 1073741824 | bytes 5242880 | tf_op jit(solution)/shard_map/attention_far/pallas_call | solution.py:40
  120.0 1.6 %all-to-all-done.2.refs_2_ = bf16[4,288,384]{2,1,0:T(8,128)(2,1)S(1)} async-done(((bf16[4,288,384]{2,1,0:T(8,128)(2,1)}), bf16[4,288,384]{2,1,0:T(8,128)(2,1)S(1)}, u32[]{:S(2)}, u32[]{:S(2)}) %all-to-all-start.2) | async-done | bytes 884768 | tf_op jit(solution)/shard_map/all_to_all | solution.py:442
  123.9 3.8 %project.1.refs_5_ = bf16[1280,128]{1,0:T(8,128)(2,1)} custom-call(s32[3]{0:T(128)S(1)} %copy-done.16, bf16[288,1280]{1,0:T(8,128)(2,1)S(1)} %copy-done, bf16[4,288,384]{2,1,0:T(8,128)(2,1)S(1)} %all-to-all-done.2.refs_2_, bf16[1536,256]{1,0:T(8,128)(2,1)} %bitcast.11.refs_3_, bf16[1536,256]{1,0:T(8,128)(2,1)} %collective-permute-done.13.refs_4_, ...), custom_call_target="tpu_custom_call" | custom-call | flops 452984832 | bytes 3145728 | tf_op jit(solution)/shard_map/project/pallas_call | solution.py:40
  127.7 7.4 %all-to-all-start.3 = ((bf16[32,40,128]{2,1,0:T(8,128)(2,1)}), bf16[32,40,128]{2,1,0:T(8,128)(2,1)S(1)}, u32[]{:S(2)}, u32[]{:S(2)}) async-start(bf16[32,40,128]{2,1,0:T(8,128)(2,1)} %bitcast.12), calls=%async_computation.3 | async-start | bytes 655360 | tf_op jit(solution)/shard_map/all_to_all | solution.py:463
  137.2 2.2 %attention_last.1.refs_3_ = bf16[512,256]{1,0:T(8,128)(2,1)} custom-call(s32[3]{0:T(128)S(1)} %copy-done.16, bf16[512,256]{1,0:T(8,128)(2,1)S(1)} %copy-done.23, bf16[4,512,256]{2,1,0:T(8,128)(2,1)} %collective-permute-done.12.refs_2_, f32[1024,256]{1,0:T(8,128)S(1)} %copy-done.3, f32[1024,128]{1,0:T(8,128)S(1)} %copy-done.8, bf16[1280,128]{1,0:T(8,128)(2,1)} %project.1.refs_5_), custom_call_target="tpu_custom_call" | custom-call | flops 1073741824 | bytes 5242880 | tf_op jit(solution)/shard_map/attention_last/pallas_call | solution.py:40
  139.4 6.2 %all-to-all-done.3 = bf16[32,40,128]{2,1,0:T(8,128)(2,1)S(1)} async-done(((bf16[32,40,128]{2,1,0:T(8,128)(2,1)}), bf16[32,40,128]{2,1,0:T(8,128)(2,1)S(1)}, u32[]{:S(2)}, u32[]{:S(2)}) %all-to-all-start.3) | async-done | bytes 327712 | tf_op jit(solution)/shard_map/all_to_all | solution.py:463
  146.6 1.8 %combine.1 = (f32[64,256]{1,0:T(8,128)S(1)}, f32[64,256]{1,0:T(8,128)S(1)}) custom-call(s32[3]{0:T(128)S(1)} %copy-done.16, f32[1280,64]{1,0:T(8,128)S(1)} %combine_map.1.refs_6_.refs_1_, bf16[1280,128]{1,0:T(8,128)(2,1)S(1)} %bitcast.15, bf16[512,256]{1,0:T(8,128)(2,1)S(1)} %copy-done.12), custom_call_target="tpu_custom_call" | custom-call | flops 251658240 | bytes 1048576 | tf_op jit(solution)/shard_map/combine/pallas_call | solution.py:40
  148.4 6.0 %collective-permute-start.14 = (f32[64,256]{1,0:T(8,128)S(1)}, f32[64,256]{1,0:T(8,128)S(1)}, u32[]{:S(2)}, u32[]{:S(2)}) collective-permute-start(f32[64,256]{1,0:T(8,128)S(1)} %get-tuple-element.21), channel_id=1, source_target_pairs={{0,32},{32,0},{1,33},{33,1},{2,34},{34,2},{3,35},{35,3},{4,36},{36... | collective-permute-start | bytes 196616 | tf_op jit(solution)/shard_map/ppermute | solution.py:360
  (74 shorter events, 21.6 us)
Async XLA Ops:
  0.6 39.0 %copy-start = (bf16[288,1280]{1,0:T(8,128)(2,1)S(1)}, bf16[288,1280]{1,0:T(8,128)(2,1)}, u32[]{:S(2)}) copy-start(bf16[288,1280]{1,0:T(8,128)(2,1)} %constant.23.clone.refs_1_) | copy-start | bytes 2211844
  0.6 39.0 %copy-start.4 = (bf16[1,256,1536]{2,1,0:T(8,128)(2,1)S(1)}, bf16[1,256,1536]{2,1,0:T(8,128)(2,1)}, u32[]{:S(2)}) copy-start(bf16[1,256,1536]{2,1,0:T(8,128)(2,1)} %param.16) | copy-start | bytes 2359300
  0.7 39.0 %copy-start.5 = (bf16[1,256,1536]{2,1,0:T(8,128)(2,1)S(1)}, bf16[1,256,1536]{2,1,0:T(8,128)(2,1)}, u32[]{:S(2)}) copy-start(bf16[1,256,1536]{2,1,0:T(8,128)(2,1)} %param.17) | copy-start | bytes 2359300
  0.7 39.0 %collective-permute-start.5 = (bf16[256,1536]{1,0:T(8,128)(2,1)}, bf16[256,1536]{1,0:T(8,128)(2,1)}, u32[]{:S(2)}, u32[]{:S(2)}) collective-permute-start(bf16[256,1536]{1,0:T(8,128)(2,1)} %bitcast.16), channel_id=1, source_target_pairs={{0,32},{32,0},{1,33},{33,1},{2,34},{34,2},{3,35},{35,3},{4,36},{36... | collective-permute-start | bytes 2359304 | tf_op jit(solution)/shard_map/ppermute | solution.py:360
  9.6 30.1 %collective-permute-start.6 = (bf16[256,1536]{1,0:T(8,128)(2,1)}, bf16[256,1536]{1,0:T(8,128)(2,1)}, u32[]{:S(2)}, u32[]{:S(2)}) collective-permute-start(bf16[256,1536]{1,0:T(8,128)(2,1)} %bitcast.18), channel_id=1, source_target_pairs={{0,32},{32,0},{1,33},{33,1},{2,34},{34,2},{3,35},{35,3},{4,36},{36... | collective-permute-start | bytes 2359304 | tf_op jit(solution)/shard_map/ppermute | solution.py:360
  11.5 3.5 %collective-permute-start = (bf16[64,256]{1,0:T(8,128)(2,1)}, bf16[64,256]{1,0:T(8,128)(2,1)S(1)}, u32[]{:S(2)}, u32[]{:S(2)}) collective-permute-start(bf16[64,256]{1,0:T(8,128)(2,1)} %refs_2_.1), channel_id=1, source_target_pairs={{0,32},{32,0},{1,33},{33,1},{2,34},{34,2},{3,35},{35,3},{4,36},{36... | collective-permute-start | bytes 98312 | tf_op jit(solution)/shard_map/ppermute | solution.py:360
  14.0 30.5 %copy-start.13 = (s32[3]{0:T(128)}, s32[3]{0:T(128)S(1)}, u32[]{:S(2)}) copy-start(s32[3]{0:T(128)S(1)} %pad_add_fusion.refs_0_) | copy-start | bytes 40
  18.9 20.7 %all-to-all-start = ((bf16[32,40,128]{2,1,0:T(8,128)(2,1)}), bf16[32,40,128]{2,1,0:T(8,128)(2,1)S(1)}, u32[]{:S(2)}, u32[]{:S(2)}) async-start(bf16[32,40,128]{2,1,0:T(8,128)(2,1)} %bitcast.6), calls=%async_computation | async-start | bytes 655360 | tf_op jit(solution)/shard_map/all_to_all | solution.py:375
  29.5 18.7 %collective-permute-start.7 = (bf16[512,256]{1,0:T(8,128)(2,1)}, bf16[512,256]{1,0:T(8,128)(2,1)S(1)}, u32[]{:S(2)}, u32[]{:S(2)}) collective-permute-start(bf16[512,256]{1,0:T(8,128)(2,1)} %get-tuple-element.13.refs_1_), channel_id=1, source_target_pairs={{0,64},{64,128},{128,192},{1,65},{65,129},{129,193},{2,66},{66,130... | collective-permute-start | bytes 786440 | tf_op jit(solution)/shard_map/ppermute | solution.py:385
  32.6 15.6 %collective-permute-start.8 = (bf16[512,256]{1,0:T(8,128)(2,1)}, bf16[512,256]{1,0:T(8,128)(2,1)}, u32[]{:S(2)}, u32[]{:S(2)}) collective-permute-start(bf16[512,256]{1,0:T(8,128)(2,1)} %get-tuple-element.13.refs_1_), channel_id=1, source_target_pairs={{0,128},{64,192},{1,129},{65,193},{2,130},{66,194},{3,131},{67,195... | collective-permute-start | bytes 786440 | tf_op jit(solution)/shard_map/ppermute | solution.py:385
  37.6 10.6 %collective-permute-start.9 = (bf16[512,256]{1,0:T(8,128)(2,1)}, bf16[512,256]{1,0:T(8,128)(2,1)}, u32[]{:S(2)}, u32[]{:S(2)}) collective-permute-start(bf16[512,256]{1,0:T(8,128)(2,1)} %get-tuple-element.13.refs_1_), channel_id=1, source_target_pairs={{0,192},{1,193},{2,194},{3,195},{4,196},{5,197},{6,198},{7,199},{8... | collective-permute-start | bytes 786440 | tf_op jit(solution)/shard_map/ppermute | solution.py:385
  44.5 3.8 %copy-start.11 = (bf16[512,256]{1,0:T(8,128)(2,1)S(1)}, bf16[512,256]{1,0:T(8,128)(2,1)}, u32[]{:S(2)}) copy-start(bf16[512,256]{1,0:T(8,128)(2,1)} %get-tuple-element.13.refs_1_) | copy-start | bytes 786436
  44.5 28.6 %all-to-all-start.1 = ((bf16[4,288,768]{2,1,0:T(8,128)(2,1)}), bf16[4,288,768]{2,1,0:T(8,128)(2,1)S(1)}, u32[]{:S(2)}, u32[]{:S(2)}) async-start(bf16[4,288,768]{2,1,0:T(8,128)(2,1)} %products.1.refs_5_.refs_4_), calls=%async_computation.1 | async-start | bytes 3538944 | tf_op jit(solution)/shard_map/all_to_all | solution.py:402
  50.0 12.1 %collective-permute-start.10 = (bf16[4,512,256]{2,1,0:T(8,128)(2,1)S(1)}, bf16[4,512,256]{2,1,0:T(8,128)(2,1)S(1)}, u32[]{:S(2)}, u32[]{:S(2)}) collective-permute-start(bf16[4,512,256]{2,1,0:T(8,128)(2,1)S(1)} %stack_near.1.refs_2_), channel_id=1, source_target_pairs={{0,32},{32,0},{1,33},{33,1},{2,34},{34,2},{3,35},{35,3},{4,36},{36... | collective-permute-start | bytes 3145736 | tf_op jit(solution)/shard_map/ppermute | solution.py:360
  53.2 19.8 %collective-permute-start.1 = (bf16[512,256]{1,0:T(8,128)(2,1)}, bf16[512,256]{1,0:T(8,128)(2,1)}, u32[]{:S(2)}, u32[]{:S(2)}) collective-permute-start(bf16[512,256]{1,0:T(8,128)(2,1)} %get-tuple-element.12), channel_id=1, source_target_pairs={{0,280},{8,272},{16,264},{24,256},{1,281},{9,273},{17,265},{25,257... | collective-permute-start | bytes 786440 | tf_op jit(solution)/shard_map/ppermute | solution.py:381
  74.5 25.1 %collective-permute-start.11 = (bf16[288,768]{1,0:T(8,128)(2,1)S(1)}, bf16[288,768]{1,0:T(8,128)(2,1)S(1)}, u32[]{:S(2)}, u32[]{:S(2)}) collective-permute-start(bf16[288,768]{1,0:T(8,128)(2,1)S(1)} %get-tuple-element.16.refs_3_), channel_id=1, source_target_pairs={{0,256},{256,0},{1,257},{257,1},{2,258},{258,2},{3,259},{259,3},{4... | collective-permute-start | bytes 1327112 | tf_op jit(solution)/shard_map/ppermute | solution.py:423
  80.4 39.7 %collective-permute-start.13 = (bf16[1536,256]{1,0:T(8,128)(2,1)}, bf16[1536,256]{1,0:T(8,128)(2,1)}, u32[]{:S(2)}, u32[]{:S(2)}) collective-permute-start(bf16[1536,256]{1,0:T(8,128)(2,1)} %bitcast.11.refs_3_), channel_id=1, source_target_pairs={{0,32},{32,0},{1,33},{33,1},{2,34},{34,2},{3,35},{35,3},{4,36},{36... | collective-permute-start | bytes 2359304 | tf_op jit(solution)/shard_map/ppermute | solution.py:360
  84.3 27.3 %collective-permute-start.2 = (bf16[512,256]{1,0:T(8,128)(2,1)}, bf16[512,256]{1,0:T(8,128)(2,1)}, u32[]{:S(2)}, u32[]{:S(2)}) collective-permute-start(bf16[512,256]{1,0:T(8,128)(2,1)} %collective-permute-done.1.refs_3_.refs_1_), channel_id=1, source_target_pairs={{256,320},{320,384},{384,448},{448,256},{257,321},{321,385},{385,4... | collective-permute-start | bytes 786440 | tf_op jit(solution)/shard_map/ppermute | solution.py:388
  85.6 26.0 %collective-permute-start.3 = (bf16[512,256]{1,0:T(8,128)(2,1)}, bf16[512,256]{1,0:T(8,128)(2,1)}, u32[]{:S(2)}, u32[]{:S(2)}) collective-permute-start(bf16[512,256]{1,0:T(8,128)(2,1)} %collective-permute-done.1.refs_3_.refs_1_), channel_id=1, source_target_pairs={{256,384},{320,448},{384,256},{448,320},{257,385},{321,449},{385,2... | collective-permute-start | bytes 786440 | tf_op jit(solution)/shard_map/ppermute | solution.py:388
  87.0 24.6 %collective-permute-start.4 = (bf16[512,256]{1,0:T(8,128)(2,1)}, bf16[512,256]{1,0:T(8,128)(2,1)}, u32[]{:S(2)}, u32[]{:S(2)}) collective-permute-start(bf16[512,256]{1,0:T(8,128)(2,1)} %collective-permute-done.1.refs_3_.refs_1_), channel_id=1, source_target_pairs={{256,448},{320,256},{384,320},{448,384},{257,449},{321,257},{385,3... | collective-permute-start | bytes 786440 | tf_op jit(solution)/shard_map/ppermute | solution.py:388
  99.6 9.4 %copy-start.16 = (s32[3]{0:T(128)S(1)}, s32[3]{0:T(128)}, u32[]{:S(2)}) copy-start(s32[3]{0:T(128)} %copy-done.13) | copy-start | bytes 40
  99.6 9.4 %copy-start.19 = (s32[64,8]{0,1:T(8,128)S(1)}, s32[64,8]{0,1:T(8,128)}, u32[]{:S(2)}) copy-start(s32[64,8]{0,1:T(8,128)} %param.14) | copy-start | bytes 6148
  99.6 9.4 %copy-start.20 = (f32[64,8]{0,1:T(8,128)S(1)}, f32[64,8]{0,1:T(8,128)}, u32[]{:S(2)}) copy-start(f32[64,8]{0,1:T(8,128)} %param.15) | copy-start | bytes 6148
  101.3 20.4 %all-to-all-start.2 = ((bf16[4,288,384]{2,1,0:T(8,128)(2,1)}), bf16[4,288,384]{2,1,0:T(8,128)(2,1)S(1)}, u32[]{:S(2)}, u32[]{:S(2)}) async-start(bf16[4,288,384]{2,1,0:T(8,128)(2,1)} %hidden.1.refs_5_), calls=%async_computation.2 | async-start | bytes 1769472 | tf_op jit(solution)/shard_map/all_to_all | solution.py:442
  111.6 5.0 %copy-start.22 = (bf16[512,256]{1,0:T(8,128)(2,1)S(1)}, bf16[512,256]{1,0:T(8,128)(2,1)}, u32[]{:S(2)}) copy-start(bf16[512,256]{1,0:T(8,128)(2,1)} %refs_1_.7) | copy-start | bytes 786436
  111.6 5.0 %copy-start.25 = (f32[1024,128]{1,0:T(8,128)S(1)}, f32[1024,128]{1,0:T(8,128)}, u32[]{:S(2)}) copy-start(f32[1024,128]{1,0:T(8,128)} %copy-done.24) | copy-start | bytes 1572868
  114.0 21.2 %collective-permute-start.12 = (bf16[4,512,256]{2,1,0:T(8,128)(2,1)}, bf16[4,512,256]{2,1,0:T(8,128)(2,1)}, u32[]{:S(2)}, u32[]{:S(2)}) collective-permute-start(bf16[4,512,256]{2,1,0:T(8,128)(2,1)} %stack_far.1.refs_2_), channel_id=1, source_target_pairs={{0,32},{32,0},{1,33},{33,1},{2,34},{34,2},{3,35},{35,3},{4,36},{36... | collective-permute-start | bytes 3145736 | tf_op jit(solution)/shard_map/ppermute | solution.py:360
  121.7 1.2 copy-start.2
  123.9 11.2 %copy-start.3 = (f32[1024,256]{1,0:T(8,128)S(1)}, f32[1024,256]{1,0:T(8,128)}, u32[]{:S(2)}) copy-start(f32[1024,256]{1,0:T(8,128)} %copy-done.1) | copy-start | bytes 3145732
  127.7 17.9 %all-to-all-start.3 = ((bf16[32,40,128]{2,1,0:T(8,128)(2,1)}), bf16[32,40,128]{2,1,0:T(8,128)(2,1)S(1)}, u32[]{:S(2)}, u32[]{:S(2)}) async-start(bf16[32,40,128]{2,1,0:T(8,128)(2,1)} %bitcast.12), calls=%async_computation.3 | async-start | bytes 655360 | tf_op jit(solution)/shard_map/all_to_all | solution.py:463
  135.2 1.0 copy-start.8
  148.4 6.9 %collective-permute-start.14 = (f32[64,256]{1,0:T(8,128)S(1)}, f32[64,256]{1,0:T(8,128)S(1)}, u32[]{:S(2)}, u32[]{:S(2)}) collective-permute-start(f32[64,256]{1,0:T(8,128)S(1)} %get-tuple-element.21), channel_id=1, source_target_pairs={{0,32},{32,0},{1,33},{33,1},{2,34},{34,2},{3,35},{35,3},{4,36},{36... | collective-permute-start | bytes 196616 | tf_op jit(solution)/shard_map/ppermute | solution.py:360
  (13 other events, 11.0 us)

commit v3 on v2

v3 whole, which is shorter than its diff:
```python
import jax
import jax.numpy as jnp
from jax import lax
from jax.experimental import pallas as pl
from jax.experimental.pallas import tpu as pltpu
from jax.sharding import Mesh
from jax.sharding import PartitionSpec as P

FF = 1536
HEADS = 64
KVH = 4
HD = 128
TOPK = 8
EXPERTS = 32
CAP = 18
HALF_CAP = CAP // 2
GROUPS = 4
ROOM = 40
SLOTS = EXPERTS * ROOM
ROWS = EXPERTS * HALF_CAP
F32 = jnp.float32
BF16 = jnp.bfloat16
LOG2E = 1.4426950408889634
TILE = 256
CONTRACT_LAST = (((1,), (1,)), ((), ()))
CONTRACT_FIRST = (((0,), (0,)), ((), ()))
VMEM = pl.BlockSpec(memory_space=pltpu.VMEM)
ANY = pl.BlockSpec(memory_space=pl.ANY)


def call(
    kernel, outs, ins, flops, moved, scratch=(), transcendentals=0, name=None, after=(),
    fetched=(), stored=(), bare=False,
):
    first = len(ins) + len(after)
    outs = [*outs, shape((8, HD), F32)]
    last = first + len(outs) - 1
    buffers = [] if bare else [ins[i] for i in fetched] + [outs[i] for i in stored]
    copies = len(buffers)

    def run(*refs):
        own = refs[last + 1 + copies :]
        if copies:
            *own, sems = own
            reads, writes = refs[: len(ins)], refs[first:last]
            near = refs[last + 1 : last + 1 + copies]
            into = dict(zip(fetched, near))
            out_of = dict(zip(stored, near[len(fetched) :]))
            moves = [
                pltpu.make_async_copy(reads[i], buffer, sems.at[k])
                for k, (i, buffer) in enumerate(into.items())
            ]
            for move in moves:
                move.start()
            for move in moves:
                move.wait()
            kernel(
                *[into.get(i, ref) for i, ref in enumerate(reads)],
                *[out_of.get(i, ref) for i, ref in enumerate(writes)],
                *own,
            )
            moves = [
                pltpu.make_async_copy(buffer, writes[i], sems.at[len(fetched) + k])
                for k, (i, buffer) in enumerate(out_of.items())
            ]
            for move in moves:
                move.start()
            for move in moves:
                move.wait()
        else:
            kernel(*refs[: len(ins)], *refs[first:last], *own)
        refs[last][...] = jnp.zeros(refs[last].shape, F32)

    return pl.pallas_call(
        run,
        out_shape=outs,
        in_specs=[ANY if i in fetched else VMEM for i in range(first)],
        out_specs=[ANY if i in stored else VMEM for i in range(len(outs))],
        scratch_shapes=[
            *[pltpu.VMEM(b.shape, b.dtype) for b in buffers],
            *scratch,
            *([pltpu.SemaphoreType.DMA((copies,))] if copies else []),
        ],
        compiler_params=pltpu.CompilerParams(vmem_limit_bytes=(60 if copies else 32) << 20),
        cost_estimate=pl.CostEstimate(
            flops=flops, bytes_accessed=moved, transcendentals=transcendentals
        ),
        name=name,
    )(*ins, *after)


def shape(dims, dtype=BF16):
    return jax.ShapeDtypeStruct(dims, dtype)


def spread_queries(q_ref, q2):
    rows, heads = q_ref.shape[0], q_ref.shape[1] // HD
    for h in range(heads):
        q = q_ref[:, h * HD : (h + 1) * HD].astype(F32) * (LOG2E * HD**-0.5)
        high = q.astype(BF16)
        q2[h * rows : (h + 1) * rows, :HD] = high
        q2[h * rows : (h + 1) * rows, HD:] = (q - high.astype(F32)).astype(BF16)


def key_block(kv_ref, i):
    k, v = kv_ref[i, :, :HD], kv_ref[i, :, HD:]
    return (
        jnp.concatenate([k, k], axis=1),
        jnp.concatenate([v, jnp.ones_like(v)], axis=1),
    )


def attend(q2, blocks, peak, acc, rows, diagonal=False):
    tiles = [slice(at, at + TILE) for at in range(0, q2.shape[0], TILE)]

    def scores_of(sl):
        out = []
        for kk, _ in blocks:
            s = lax.dot_general(q2[sl, :], kk, CONTRACT_LAST, preferred_element_type=F32)
            if diagonal:
                query = sl.start % rows + lax.broadcasted_iota(jnp.int32, s.shape, 0)
                key = lax.broadcasted_iota(jnp.int32, s.shape, 1)
                s = jnp.where(query >= key, s, -1e30)
            out.append(s)
        return out

    ahead = scores_of(tiles[0])
    for t, sl in enumerate(tiles):
        scores = ahead
        if t + 1 < len(tiles):
            ahead = scores_of(tiles[t + 1])
        highest = scores[0]
        for s in scores[1:]:
            highest = jnp.maximum(highest, s)
        new = jnp.max(highest, axis=1, keepdims=True)
        if not diagonal:
            old = peak[sl, :1]
            new = jnp.maximum(old, new)
        mixed = 0.0 if diagonal else acc[sl, :] * jnp.exp2(old - new)
        for s, (_, v1) in zip(scores, blocks):
            p = jnp.exp2(s - new).astype(BF16)
            mixed = mixed + jnp.dot(p, v1, preferred_element_type=F32)
        acc[sl, :] = mixed
        peak[sl, :] = jnp.broadcast_to(new, (TILE, HD))


def attention_near_kernel(q_ref, kv_ref, sibling_ref, acc, peak, q2):
    rows = q_ref.shape[0]
    spread_queries(q_ref, q2)
    attend(q2, [key_block(kv_ref, 0)], peak, acc, rows, True)

    def beside(i, carry):
        attend(q2, [key_block(sibling_ref, 0)], peak, acc, rows)
        return carry

    def earlier(i, carry):
        attend(q2, [key_block(kv_ref, i), key_block(sibling_ref, i)], peak, acc, rows)
        return carry

    chip, core = lax.axis_index("x"), lax.axis_index("c")
    lax.fori_loop(0, core, beside, 0)
    lax.fori_loop(1, chip + 1, earlier, 0)


def attention_far_kernel(q, kv, sibling, acc, peak, o_ref, q2):
    rows, heads = q.shape[0], q.shape[1] // HD
    spread_queries(q, q2)

    def earlier(i, carry):
        blocks = [key_block(ref, 2 * i + j) for j in (0, 1) for ref in (kv, sibling)]
        attend(q2, blocks, peak, acc, rows)
        return carry

    lax.fori_loop(0, lax.axis_index("w") * (kv.shape[0] // 2), earlier, 0)
    for h in range(heads):
        a = acc[h * rows : (h + 1) * rows, :]
        o_ref[:, h * HD : (h + 1) * HD] = (a[:, :HD] / a[:, HD:]).astype(o_ref.dtype)


def attention(kernel, outs, ins, fetched, name, after):
    stacked, keys = ins[0].shape[0] * ins[0].shape[1] // HD, 8 * ins[0].shape[0]
    return call(
        kernel,
        outs,
        ins,
        flops=4 * stacked * keys * HD,
        moved=5 << 20,
        transcendentals=stacked * keys,
        scratch=[pltpu.VMEM((stacked, 2 * HD), BF16)],
        name=name,
        after=after,
        fetched=fetched,
    )


def places(ids_ref, core):
    count = ids_ref.shape[1]
    expert = lax.broadcasted_iota(jnp.int32, (EXPERTS, count), 0)
    chosen = jnp.zeros((EXPERTS, count), F32)
    for k in range(TOPK):
        chosen = chosen + jnp.where(ids_ref[k : k + 1, :] == expert, 1.0, 0.0)
    chosen = chosen.astype(BF16)
    earlier = lax.broadcasted_iota(jnp.int32, (count, count), 0) < lax.broadcasted_iota(
        jnp.int32, (count, count), 1
    )
    rank = jnp.dot(chosen, jnp.where(earlier, 1.0, 0.0).astype(BF16), preferred_element_type=F32)
    inside = lax.broadcasted_iota(jnp.int32, (SLOTS, EXPERTS), 0) - ROOM * lax.broadcasted_iota(
        jnp.int32, (SLOTS, EXPERTS), 1
    )
    own = (inside >= 0) & (inside < ROOM)
    spread = jnp.where(own, 1.0, 0.0).astype(BF16)
    row = jnp.sum(jnp.where(own, inside.astype(F32), 0.0), axis=1, keepdims=True)
    group = jnp.zeros_like(row)
    for g in range(1, GROUPS + 1):
        group = group + jnp.where(row >= g * HALF_CAP, 1.0, 0.0)
    wanted = row - group * HALF_CAP + (core * HALF_CAP).astype(F32)
    hits = jnp.dot(spread, chosen, preferred_element_type=F32)
    ranks = jnp.dot(spread, rank.astype(BF16), preferred_element_type=F32)
    placed = (hits > 0.5) & (ranks == wanted) & (group < GROUPS)
    return spread, placed, group


def dispatch_kernel(ids_ref, own_ref, sibling_ref, out_ref):
    core = lax.axis_index("c")
    _, placed, group = places(ids_ref, core)
    own, sibling = own_ref[...], sibling_ref[...]
    first, second = jnp.where(core == 0, own, sibling), jnp.where(core == 0, sibling, own)
    tokens = jnp.concatenate([first, second], axis=1)
    total = jnp.zeros(out_ref.shape, F32)
    for g in range(GROUPS):
        onehot = jnp.where(placed & (group == g), 1.0, 0.0).astype(BF16)
        total = total + jnp.dot(
            onehot, tokens[:, g * HD : (g + 1) * HD], preferred_element_type=F32
        )
    out_ref[...] = total.astype(BF16)


def combine_map_kernel(ids_ref, w_ref, out_ref):
    spread, placed, _ = places(ids_ref, lax.axis_index("c"))
    expert = lax.broadcasted_iota(jnp.int32, (EXPERTS, ids_ref.shape[1]), 0)
    weight = jnp.zeros(expert.shape, F32)
    for k in range(TOPK):
        weight = weight + jnp.where(ids_ref[k : k + 1, :] == expert, w_ref[k : k + 1, :], 0.0)
    weights = jnp.dot(spread.astype(F32), weight, precision=lax.Precision.HIGHEST)
    out_ref[...] = jnp.where(placed, weights, 0.0)


def block_rows(dims, axis):
    row = lax.broadcasted_iota(jnp.int32, dims, axis)
    expert = lax.shift_right_logical(row * 1639, 16)
    inside = row - ROOM * expert
    group = jnp.zeros_like(row)
    for g in range(1, GROUPS + 1):
        group = group + jnp.where(inside >= g * HALF_CAP, 1, 0)
    tight = expert * HALF_CAP + inside - HALF_CAP * group
    return jnp.where(group < GROUPS, tight, -1), group


def widen(block):
    _, group = block_rows((SLOTS, 1), 0)
    return jnp.concatenate(
        [jnp.where(group == g, block, 0.0).astype(BF16) for g in range(GROUPS)], axis=1
    )


def products_kernel(
    rows_ref, gate_ref, up_ref, sibling_gate_ref, sibling_up_ref, out_ref
):
    tight, _ = block_rows((1, SLOTS), 1)
    pack = jnp.where(tight == lax.broadcasted_iota(jnp.int32, (ROWS, SLOTS), 0), 1.0, 0.0)
    rows = jnp.dot(pack.astype(BF16), widen(rows_ref[...]), preferred_element_type=F32)
    rows = rows.astype(BF16)
    half = rows.shape[1] // 2
    first, second = rows[:, :half], rows[:, half:]
    core = lax.axis_index("c")
    own, sibling = jnp.where(core == 0, first, second), jnp.where(core == 0, second, first)
    cols = out_ref.shape[2] // 2
    for i in range(out_ref.shape[0]):
        sl = slice(i * cols, (i + 1) * cols)
        for j, (mine, its) in enumerate(((gate_ref, sibling_gate_ref), (up_ref, sibling_up_ref))):
            out_ref[i, :, j * cols : (j + 1) * cols] = (
                jnp.dot(own, mine[:, sl], preferred_element_type=F32)
                + jnp.dot(sibling, its[:, sl], preferred_element_type=F32)
            ).astype(BF16)


def sum_kernel(parts_ref, wide_ref, low_ref):
    total = parts_ref[0].astype(F32)
    for i in range(1, parts_ref.shape[0]):
        total = total + parts_ref[i].astype(F32)
    wide_ref[...] = total
    low_ref[...] = total.astype(BF16)


def hidden_kernel(wide_ref, other_ref, out_ref):
    total = wide_ref[...] + other_ref[...].astype(F32)
    cols = total.shape[1] // 2
    gate, up = total[:, :cols], total[:, cols:]
    out_ref[...] = (gate / (1.0 + jnp.exp(-gate)) * up).astype(BF16)


def project_kernel(hidden_ref, down_ref, swapped_ref, out_ref):
    hidden = jnp.concatenate([hidden_ref[i] for i in range(hidden_ref.shape[0])], axis=1)
    own = jnp.dot(hidden, down_ref[...], preferred_element_type=F32).astype(BF16)
    sibling = jnp.dot(hidden, swapped_ref[...], preferred_element_type=F32).astype(BF16)
    core = lax.axis_index("c")
    first, second = jnp.where(core == 0, own, sibling), jnp.where(core == 0, sibling, own)
    result = jnp.concatenate([first, second], axis=1)
    tight, group = block_rows((SLOTS, 1), 0)
    unpack = jnp.where(tight == lax.broadcasted_iota(jnp.int32, (SLOTS, ROWS), 1), 1.0, 0.0)
    wide = jnp.dot(unpack.astype(BF16), result, preferred_element_type=F32)
    total = jnp.zeros(out_ref.shape, F32)
    for g in range(GROUPS):
        total = jnp.where(group == g, wide[:, g * HD : (g + 1) * HD], total)
    out_ref[...] = total.astype(BF16)


def combine_kernel(combine_ref, back_ref, own_ref, sibling_ref):
    c, wide = combine_ref[...], widen(back_ref[...])
    total = jnp.zeros((c.shape[1], wide.shape[1]), F32)
    for _ in range(3):
        part = c.astype(BF16)
        total = total + lax.dot_general(part, wide, CONTRACT_FIRST, preferred_element_type=F32)
        c = c - part.astype(F32)
    half = total.shape[1] // 2
    core = lax.axis_index("c")
    own_ref[...] = jnp.where(core == 0, total[:, :half], total[:, half:])
    sibling_ref[...] = jnp.where(core == 0, total[:, half:], total[:, :half])


def add_kernel(own_ref, other_ref, out_ref):
    out_ref[...] = (own_ref[...] + other_ref[...]).astype(BF16)


def head_columns_kernel(key_ref, value_ref, kv_ref, near_ref, sems):
    z = lax.axis_index("z")
    copies = []
    for i, (out, head) in enumerate(((kv_ref, z), (near_ref, KVH - 1 - z))):
        columns = pl.ds(pl.multiple_of(head * HD, HD), HD)
        for j, source in enumerate((key_ref, value_ref)):
            copies.append(
                pltpu.make_async_copy(
                    source.at[:, columns], out.at[:, j * HD : (j + 1) * HD], sems.at[2 * i + j]
                )
            )
    for copy in copies:
        copy.start()
    for copy in copies:
        copy.wait()


def stack_kernel(*refs):
    for i, ref in enumerate(refs[:-1]):
        refs[-1][i] = ref[...]


def stack(parts, after, name):
    return call(
        stack_kernel,
        [shape((len(parts), *parts[0].shape))],
        parts,
        flops=0,
        moved=0,
        name=name,
        after=after,
    )[0]


def body(
    queries,
    key_states,
    value_states,
    token_states,
    expert_ids,
    combine_weights,
    gate_weight,
    up_weight,
    down_weight,
):
    swap = lambda a: lax.ppermute(a, "c", [(0, 1), (1, 0)])
    gate, up, down = gate_weight[0], up_weight[0], down_weight[0]
    count, width = token_states.shape
    ids = expert_ids.T
    block = (EXPERTS, ROOM, HD)

    outbound, sent = call(
        dispatch_kernel,
        [shape((SLOTS, HD))],
        (ids, token_states, swap(token_states)),
        flops=2 * SLOTS * 64 * 600,
        moved=1 << 20,
        name="dispatch",
    )
    received = lax.all_to_all(outbound.reshape(block), ("z", "y"), 0, 0, tiled=True)

    z_count, lanes = lax.axis_size("z"), lax.axis_size("x")
    kv, kv_near, _ = call(
        head_columns_kernel,
        [shape((key_states.shape[0], 2 * HD))] * 2,
        (key_states, value_states),
        flops=0,
        moved=0,
        scratch=[pltpu.SemaphoreType.DMA((4,))],
        name="head_columns",
        after=(sent,),
        fetched=(0, 1),
        bare=True,
    )
    kv_far = lax.ppermute(
        kv_near, ("w", "z"), [(z, 2 * z_count - 1 - z) for z in range(z_count)]
    )
    near = [kv] + [
        lax.ppermute(kv, "x", [(x, x + k) for x in range(lanes - k)]) for k in range(1, lanes)
    ]
    far = [kv_far] + [
        lax.ppermute(
            kv_far, ("w", "x"), [(lanes + x, lanes + (x + k) % lanes) for x in range(lanes)]
        )
        for k in range(1, lanes)
    ]
    cols = 2 * FF // lanes
    products, multiplied = call(
        products_kernel,
        [shape((lanes, ROWS, cols))],
        (received.reshape(SLOTS, HD), gate, up, swap(gate), swap(up)),
        flops=2 * ROWS * 4 * width * FF,
        moved=5 << 20,
        name="products",
    )
    parts = lax.all_to_all(products, "x", 0, 0, tiled=True)
    near = stack(near, (multiplied,), "stack_near")
    stacked = queries.shape[0] * queries.shape[1] // HD
    spread = shape((stacked, 2 * HD))
    running = [shape((stacked, 2 * HD), F32), shape((stacked, HD), F32)]
    stacked = queries.shape[0] * queries.shape[1] // HD
    *state, seen = attention(
        attention_near_kernel,
        [shape((stacked, 2 * HD), F32), shape((stacked, HD), F32)],
        (queries, near, swap(near)),
        (),
        "attention_near",
        (multiplied,),
    )
    wide, low, summed = call(
        sum_kernel,
        [shape((ROWS, cols), F32), shape((ROWS, cols))],
        (parts,),
        flops=ROWS * cols * 4,
        moved=3 << 20,
        name="sum_parts",
        after=(seen, kv_far),
    )
    other = lax.ppermute(low, "w", [(0, 1), (1, 0)])
    combine_map, mapped = call(
        combine_map_kernel,
        [shape((SLOTS, count), F32)],
        (ids, combine_weights.T),
        flops=0,
        moved=0,
        name="combine_map",
        after=(summed,),
    )
    hidden, ready = call(
        hidden_kernel,
        [shape((ROWS, cols // 2))],
        (wide, other),
        flops=ROWS * cols * 4,
        moved=2 << 20,
        transcendentals=ROWS * cols // 2,
        name="hidden",
        after=(mapped,),
    )
    hidden_all = lax.all_gather(hidden, "x", axis=0)
    far = stack(far, (ready,), "stack_far")
    finished, projected = call(
        project_kernel,
        [shape((SLOTS, HD))],
        (hidden_all, down, swap(down)),
        flops=2 * ROWS * FF * 2 * width,
        moved=3 << 20,
        name="project",
    )
    back = lax.all_to_all(finished.reshape(block), ("z", "y"), 0, 0, tiled=True)
    context, seen = attention(
        attention_far_kernel,
        [shape(queries.shape)],
        (queries, far, swap(far), *state),
        range(5),
        "attention_far",
        (projected,),
    )
    own_sum, sibling_sum, _ = call(
        combine_kernel,
        [shape((count, width), F32), shape((count, width), F32)],
        (combine_map, back.reshape(SLOTS, HD)),
        flops=6 * SLOTS * 2 * width * 64,
        moved=1 << 20,
        name="combine",
        after=(seen,),
    )
    moe_output, _ = call(
        add_kernel,
        [shape((count, width))],
        (own_sum, swap(sibling_sum)),
        flops=count * width,
        moved=200 << 10,
        name="add_cores",
    )
    return (context, moe_output)


def solution(mesh):
    fine = Mesh(mesh.devices.reshape(2, 4, 2, 4, 8), ("w", "x", "c", "z", "y"))
    ctx, exp = ("w", "x", "c"), ("z", "y")
    in_specs = (
        P(ctx, exp),
        P(ctx, None),
        P(ctx, None),
        P(exp, ctx),
        P(exp, None),
        P(exp, None),
        P(exp, ctx, None),
        P(exp, ctx, None),
        P(exp, None, ctx),
    )
    out_specs = (P(ctx, exp), P(exp, ctx))
    return jax.shard_map(body, mesh=fine, in_specs=in_specs, out_specs=out_specs, check_vma=False)
```

time: 158 us -> 147 us (0.930)
  blocking collectives: 0 us -> 14.8 us
  Pallas kernels: 30.9 us -> 20.3 us
  starting transfers between devices: 83.3 us -> 73.2 us
  local copies, waits for them, and re-layouts: 13.3 us -> 7.44 us
  waiting for transfers between devices: 27.2 us -> 29.2 us
    all_gather x0 -> x1, blocking collectives: none -> 14.8 us  [body(): hidden_all = lax.all_gather(hidden, 'x', axis=0)]
    pallas_call x14 -> x13, Pallas kernels: 30.9 us -> 20.3 us  [call(): pl.pallas_call(run, out_shape=outs, in_specs=[ANY if i in fetched else VM...]
    all_to_all x1 -> x0, starting transfers between devices: 7.72 us -> none  [body(): hidden_all = lax.all_to_all(hidden, 'x', 0, 0, tiled=True)]
    unnamed x52 -> x34, local copies, waits for them, and re-layouts: 13.3 us -> 7.44 us
    ppermute x3, starting transfers between devices: 4.09 us -> 2.03 us  [body(): lax.ppermute(kv_far, ('w', 'x'), [(lanes + x, lanes + (x + k) % lanes) fo...]
    all_to_all x1 -> x0, waiting for transfers between devices: 1.64 us -> none  [body(): hidden_all = lax.all_to_all(hidden, 'x', 0, 0, tiled=True)]
  transfers between devices with their start and end apart: 19 -> 18, of which waited for: 6 -> 6; matrix products, arithmetic and copies ran while one was open for 0% -> 0% of each run, Pallas kernels for 17% -> 12%
where the time goes in v3:
time: 147 us; the launch traced here: 146 us
  starting transfers between devices  73.2 us (50%)
  waiting for transfers between devices  29.2 us (20%)
  Pallas kernels  20.3 us (14%)
  blocking collectives  14.8 us (10%)
  local copies, waits for them, and re-layouts  7.44 us (5%)
    ppermute x7, starting transfers between devices, body(): swap = lambda a: lax.ppermute(a, 'c', [(0, 1), (1, 0)])  29.7 us
    pallas_call x13, Pallas kernels, call(): pl.pallas_call(run, out_shape=outs, in_specs=[ANY if i in fetched else VM...  20.3 us
    all_gather x1, blocking collectives, body(): hidden_all = lax.all_gather(hidden, 'x', axis=0)  14.8 us
    ppermute x1, waiting for transfers between devices, body(): other = lax.ppermute(low, 'w', [(0, 1), (1, 0)])  12.7 us
    ppermute x3, starting transfers between devices, body(): lax.ppermute(kv, 'x', [(x, x + k) for x in range(lanes - k)])  10.2 us
    ppermute x1, starting transfers between devices, body(): lax.ppermute(kv_near, ('w', 'z'), [(z, 2 * z_count - 1 - z) for z in rang...  8.32 us
    unnamed x34, local copies, waits for them, and re-layouts  7.44 us
    ppermute x1, waiting for transfers between devices, body(): lax.ppermute(kv_near, ('w', 'z'), [(z, 2 * z_count - 1 - z) for z in rang...  7.39 us
  transfers between devices with their start and end apart: 18, of which 6 were waited for; matrix products, arithmetic and copies ran while one was open for 0% of the time, Pallas kernels for 12%

profile of v3, /device:TPU:1, one launch (start us, length us, event | category | flops | bytes accessed | tf_op | source)
XLA Modules:
  0.0 145.9 jit_solution(17891436453215613935)
XLA Ops:
  0.7 8.9 %collective-permute-start.5 = (bf16[256,1536]{1,0:T(8,128)(2,1)}, bf16[256,1536]{1,0:T(8,128)(2,1)S(1)}, u32[]{:S(2)}, u32[]{:S(2)}) collective-permute-start(bf16[256,1536]{1,0:T(8,128)(2,1)} %bitcast.13), channel_id=1, source_target_pairs={{0,32},{32,0},{1,33},{33,1},{2,34},{34,2},{3,35},{35,3},{4,36},{36... | collective-permute-start | bytes 2359304 | tf_op jit(solution)/shard_map/ppermute | solution.py:380
  9.6 1.9 %collective-permute-start.6 = (bf16[256,1536]{1,0:T(8,128)(2,1)}, bf16[256,1536]{1,0:T(8,128)(2,1)S(1)}, u32[]{:S(2)}, u32[]{:S(2)}) collective-permute-start(bf16[256,1536]{1,0:T(8,128)(2,1)} %bitcast.15), channel_id=1, source_target_pairs={{0,32},{32,0},{1,33},{33,1},{2,34},{34,2},{3,35},{35,3},{4,36},{36... | collective-permute-start | bytes 2359304 | tf_op jit(solution)/shard_map/ppermute | solution.py:380
  11.5 2.4 %collective-permute-start = (bf16[64,256]{1,0:T(8,128)(2,1)}, bf16[64,256]{1,0:T(8,128)(2,1)S(1)}, u32[]{:S(2)}, u32[]{:S(2)}) collective-permute-start(bf16[64,256]{1,0:T(8,128)(2,1)} %refs_1_.2), channel_id=1, source_target_pairs={{0,32},{32,0},{1,33},{33,1},{2,34},{34,2},{3,35},{35,3},{4,36},{36... | collective-permute-start | bytes 98312 | tf_op jit(solution)/shard_map/ppermute | solution.py:380
  13.9 1.0 collective-permute-done.refs_2_
  16.4 1.2 dispatch.1
  18.4 7.3 %all-to-all-start = ((bf16[32,40,128]{2,1,0:T(8,128)(2,1)}), bf16[32,40,128]{2,1,0:T(8,128)(2,1)S(1)}, u32[]{:S(2)}, u32[]{:S(2)}) async-start(bf16[32,40,128]{2,1,0:T(8,128)(2,1)} %bitcast.19), calls=%async_computation | async-start | bytes 655360 | tf_op jit(solution)/shard_map/all_to_all | solution.py:394
  25.7 1.0 copy-done.3
  26.7 1.0 copy-done.4
  29.3 3.8 %collective-permute-start.7 = (bf16[512,256]{1,0:T(8,128)(2,1)}, bf16[512,256]{1,0:T(8,128)(2,1)}, u32[]{:S(2)}, u32[]{:S(2)}) collective-permute-start(bf16[512,256]{1,0:T(8,128)(2,1)} %get-tuple-element.31.refs_0_), channel_id=1, source_target_pairs={{0,64},{64,128},{128,192},{1,65},{65,129},{129,193},{2,66},{66,130... | collective-permute-start | bytes 786440 | tf_op jit(solution)/shard_map/ppermute | solution.py:413
  33.1 4.4 %collective-permute-start.8 = (bf16[512,256]{1,0:T(8,128)(2,1)}, bf16[512,256]{1,0:T(8,128)(2,1)}, u32[]{:S(2)}, u32[]{:S(2)}) collective-permute-start(bf16[512,256]{1,0:T(8,128)(2,1)} %get-tuple-element.31.refs_0_), channel_id=1, source_target_pairs={{0,128},{64,192},{1,129},{65,193},{2,130},{66,194},{3,131},{67,195... | collective-permute-start | bytes 786440 | tf_op jit(solution)/shard_map/ppermute | solution.py:413
  37.5 2.0 %collective-permute-start.9 = (bf16[512,256]{1,0:T(8,128)(2,1)}, bf16[512,256]{1,0:T(8,128)(2,1)}, u32[]{:S(2)}, u32[]{:S(2)}) collective-permute-start(bf16[512,256]{1,0:T(8,128)(2,1)} %get-tuple-element.31.refs_0_), channel_id=1, source_target_pairs={{0,192},{1,193},{2,194},{3,195},{4,196},{5,197},{6,198},{7,199},{8... | collective-permute-start | bytes 786440 | tf_op jit(solution)/shard_map/ppermute | solution.py:413
  39.5 3.5 %products.1 = (bf16[4,288,768]{2,1,0:T(8,128)(2,1)}, f32[8,128]{1,0:T(8,128)S(1)}) custom-call(bf16[1280,128]{1,0:T(8,128)(2,1)S(1)} %bitcast.12, bf16[256,1536]{1,0:T(8,128)(2,1)S(1)} %bitcast.14, bf16[256,1536]{1,0:T(8,128)(2,1)S(1)} %bitcast.16, bf16[256,1536]{1,0:T(8,128)(2,1)S(1)} %collective-permute-done.5.refs_3_, ...), custom_call_target="tpu_custom_call" | custom-call | flops 905969664 | bytes 5242880 | tf_op jit(solution)/shard_map/products/pallas_call | solution.py:74
  43.0 3.7 %all-to-all-start.1 = ((bf16[4,288,768]{2,1,0:T(8,128)(2,1)}), bf16[4,288,768]{2,1,0:T(8,128)(2,1)S(1)}, u32[]{:S(2)}, u32[]{:S(2)}) async-start(bf16[4,288,768]{2,1,0:T(8,128)(2,1)} %get-tuple-element.30), calls=%async_computation.1 | async-start | bytes 3538944 | tf_op jit(solution)/shard_map/all_to_all | solution.py:430
  47.2 1.8 %stack_near.1 = (bf16[4,512,256]{2,1,0:T(8,128)(2,1)S(1)}, f32[8,128]{1,0:T(8,128)}) custom-call(bf16[512,256]{1,0:T(8,128)(2,1)} %get-tuple-element.31.refs_0_, bf16[512,256]{1,0:T(8,128)(2,1)} %collective-permute-done.7.refs_1_, bf16[512,256]{1,0:T(8,128)(2,1)} %collective-permute-done.8.refs_2_, bf16[512,256]{1,0:T(8,128)(2,1)} %collective-permute-done.9.refs_3_, ...), custom_call_target="tpu_custom_call" | custom-call | tf_op jit(solution)/shard_map/stack_near/pallas_call | solution.py:74
  49.0 2.6 %collective-permute-start.10 = (bf16[4,512,256]{2,1,0:T(8,128)(2,1)S(1)}, bf16[4,512,256]{2,1,0:T(8,128)(2,1)S(1)}, u32[]{:S(2)}, u32[]{:S(2)}) collective-permute-start(bf16[4,512,256]{2,1,0:T(8,128)(2,1)S(1)} %get-tuple-element.33.refs_1_), channel_id=1, source_target_pairs={{0,32},{32,0},{1,33},{33,1},{2,34},{34,2},{3,35},{35,3},{4,36},{36... | collective-permute-start | bytes 3145736 | tf_op jit(solution)/shard_map/ppermute | solution.py:380
  51.6 8.3 %collective-permute-start.1 = (bf16[512,256]{1,0:T(8,128)(2,1)}, bf16[512,256]{1,0:T(8,128)(2,1)S(1)}, u32[]{:S(2)}, u32[]{:S(2)}) collective-permute-start(bf16[512,256]{1,0:T(8,128)(2,1)} %copy-done.12), channel_id=1, source_target_pairs={{0,280},{8,272},{16,264},{24,256},{1,281},{9,273},{17,265},{25,257... | collective-permute-start | bytes 786440 | tf_op jit(solution)/shard_map/ppermute | solution.py:409
  59.9 2.4 %attention_near.1 = (f32[1024,256]{1,0:T(8,128)S(1)}, f32[1024,128]{1,0:T(8,128)S(1)}, f32[8,128]{1,0:T(8,128)S(1)}) custom-call(bf16[512,256]{1,0:T(8,128)(2,1)S(1)} %copy-done.11, bf16[4,512,256]{2,1,0:T(8,128)(2,1)S(1)} %get-tuple-element.33.refs_1_, bf16[4,512,256]{2,1,0:T(8,128)(2,1)S(1)} %collective-permute-done.10.refs_2_, ...), custom_call_target="tpu_custom_call" | custom-call | flops 2147483648 | bytes 5242880 | tf_op jit(solution)/shard_map/attention_near/pallas_call | solution.py:74
  62.3 1.0 copy-done.15
  64.1 7.4 %collective-permute-done.1.refs_2_.refs_0_ = bf16[512,256]{1,0:T(8,128)(2,1)S(1)} collective-permute-done((bf16[512,256]{1,0:T(8,128)(2,1)}, bf16[512,256]{1,0:T(8,128)(2,1)S(1)}, u32[]{:S(2)}, u32[]{:S(2)}) %collective-permute-start.1) | collective-permute-done | bytes 262176 | tf_op jit(solution)/shard_map/ppermute | solution.py:409
  71.8 4.8 %collective-permute-start.11 = (bf16[288,768]{1,0:T(8,128)(2,1)S(1)}, bf16[288,768]{1,0:T(8,128)(2,1)S(1)}, u32[]{:S(2)}, u32[]{:S(2)}) collective-permute-start(bf16[288,768]{1,0:T(8,128)(2,1)S(1)} %get-tuple-element.36), channel_id=1, source_target_pairs={{0,256},{256,0},{1,257},{257,1},{2,258},{258,2},{3,259},{259,3},{4... | collective-permute-start | bytes 1327112 | tf_op jit(solution)/shard_map/ppermute | solution.py:453
  78.7 4.2 %collective-permute-start.13 = (bf16[1536,256]{1,0:T(8,128)(2,1)S(1)}, bf16[1536,256]{1,0:T(8,128)(2,1)S(1)}, u32[]{:S(2)}, u32[]{:S(2)}) collective-permute-start(bf16[1536,256]{1,0:T(8,128)(2,1)S(1)} %bitcast.17), channel_id=1, source_target_pairs={{0,32},{32,0},{1,33},{33,1},{2,34},{34,2},{3,35},{35,3},{4,36},{36... | collective-permute-start | bytes 2359304 | tf_op jit(solution)/shard_map/ppermute | solution.py:380
  82.9 1.0 combine_map.1
  83.9 12.7 %collective-permute-done.11.refs_1_ = bf16[288,768]{1,0:T(8,128)(2,1)S(1)} collective-permute-done((bf16[288,768]{1,0:T(8,128)(2,1)S(1)}, bf16[288,768]{1,0:T(8,128)(2,1)S(1)}, u32[]{:S(2)}, u32[]{:S(2)}) %collective-permute-start.11) | collective-permute-done | bytes 442400 | tf_op jit(solution)/shard_map/ppermute | solution.py:453
  97.5 3.6 %collective-permute-start.12 = (bf16[4,512,256]{2,1,0:T(8,128)(2,1)S(1)}, bf16[4,512,256]{2,1,0:T(8,128)(2,1)}, u32[]{:S(2)}, u32[]{:S(2)}) collective-permute-start(bf16[4,512,256]{2,1,0:T(8,128)(2,1)S(1)} %get-tuple-element.40.refs_1_), channel_id=1, source_target_pairs={{0,32},{32,0},{1,33},{33,1},{2,34},{34,2},{3,35},{35,3},{4,36},{36... | collective-permute-start | bytes 3145736 | tf_op jit(solution)/shard_map/ppermute | solution.py:380
  101.2 14.8 %all-gather = bf16[1152,384]{1,0:T(8,128)(2,1)S(1)} all-gather(bf16[288,384]{1,0:T(8,128)(2,1)S(1)} %get-tuple-element.43), channel_id=2, replica_groups=mesh['w'=2,'x'=4,'c'=2,'z'=4,'y'=8] {'x'}, dimensions={0}, use_global_device_ids=true | all-gather | bytes 1105920 | tf_op jit(solution)/shard_map/all_gather | solution.py:473
  116.0 2.4 %project.1 = (bf16[1280,128]{1,0:T(8,128)(2,1)}, f32[8,128]{1,0:T(8,128)S(1)}) custom-call(bf16[4,288,384]{2,1,0:T(8,128)(2,1)S(1)} %bitcast.10, bf16[1536,256]{1,0:T(8,128)(2,1)S(1)} %bitcast.18, bf16[1536,256]{1,0:T(8,128)(2,1)S(1)} %collective-permute-done.13.refs_2_), custom_call_target="tpu_custom_call" | custom-call | flops 452984832 | bytes 3145728 | tf_op jit(solution)/shard_map/project/pallas_call | solution.py:74
  118.5 7.1 %all-to-all-start.2 = ((bf16[32,40,128]{2,1,0:T(8,128)(2,1)}), bf16[32,40,128]{2,1,0:T(8,128)(2,1)S(1)}, u32[]{:S(2)}, u32[]{:S(2)}) async-start(bf16[32,40,128]{2,1,0:T(8,128)(2,1)} %bitcast.8), calls=%async_computation.2 | async-start | bytes 655360 | tf_op jit(solution)/shard_map/all_to_all | solution.py:483
  125.6 3.7 %attention_far.1 = (bf16[512,256]{1,0:T(8,128)(2,1)}, f32[8,128]{1,0:T(8,128)}) custom-call(bf16[512,256]{1,0:T(8,128)(2,1)} %refs_0_.5, bf16[4,512,256]{2,1,0:T(8,128)(2,1)} %copy-done.10, bf16[4,512,256]{2,1,0:T(8,128)(2,1)} %collective-permute-done.12.refs_2_, f32[1024,256]{1,0:T(8,128)} %copy-done.15, f32[1024,128]{1,0:T(8,128)} %copy-done.16, ...), custom_call_target="tpu_custom_call" | custom-call | flops 2147483648 | bytes 5242880 | tf_op jit(solution)/shard_map/attention_far/pallas_call | solution.py:74
  129.4 6.6 %all-to-all-done.2 = bf16[32,40,128]{2,1,0:T(8,128)(2,1)S(1)} async-done(((bf16[32,40,128]{2,1,0:T(8,128)(2,1)}), bf16[32,40,128]{2,1,0:T(8,128)(2,1)S(1)}, u32[]{:S(2)}, u32[]{:S(2)}) %all-to-all-start.2) | async-done | bytes 327712 | tf_op jit(solution)/shard_map/all_to_all | solution.py:483
  136.6 1.7 %combine.1 = (f32[64,256]{1,0:T(8,128)S(1)}, f32[64,256]{1,0:T(8,128)S(1)}, f32[8,128]{1,0:T(8,128)}) custom-call(f32[1280,64]{1,0:T(8,128)S(1)} %get-tuple-element.46.refs_0_, bf16[1280,128]{1,0:T(8,128)(2,1)S(1)} %bitcast.11, f32[8,128]{1,0:T(8,128)S(1)} %copy-done.6), custom_call_target="tpu_custom_call" | custom-call | flops 251658240 | bytes 1048576 | tf_op jit(solution)/shard_map/combine/pallas_call | solution.py:74
  138.3 6.1 %collective-permute-start.14 = (f32[64,256]{1,0:T(8,128)S(1)}, f32[64,256]{1,0:T(8,128)S(1)}, u32[]{:S(2)}, u32[]{:S(2)}) collective-permute-start(f32[64,256]{1,0:T(8,128)S(1)} %get-tuple-element.50), channel_id=1, source_target_pairs={{0,32},{32,0},{1,33},{33,1},{2,34},{34,2},{3,35},{35,3},{4,36},{36... | collective-permute-start | bytes 196616 | tf_op jit(solution)/shard_map/ppermute | solution.py:380
  144.4 0.9 collective-permute-done.14.refs_1_
  (52 shorter events, 9.5 us)
Async XLA Ops:
  0.6 38.8 %copy-start = (bf16[1,256,1536]{2,1,0:T(8,128)(2,1)S(1)}, bf16[1,256,1536]{2,1,0:T(8,128)(2,1)}, u32[]{:S(2)}) copy-start(bf16[1,256,1536]{2,1,0:T(8,128)(2,1)} %param.15) | copy-start | bytes 2359300
  0.6 38.8 %copy-start.1 = (bf16[1,256,1536]{2,1,0:T(8,128)(2,1)S(1)}, bf16[1,256,1536]{2,1,0:T(8,128)(2,1)}, u32[]{:S(2)}) copy-start(bf16[1,256,1536]{2,1,0:T(8,128)(2,1)} %param.16) | copy-start | bytes 2359300
  0.7 38.8 %collective-permute-start.5 = (bf16[256,1536]{1,0:T(8,128)(2,1)}, bf16[256,1536]{1,0:T(8,128)(2,1)S(1)}, u32[]{:S(2)}, u32[]{:S(2)}) collective-permute-start(bf16[256,1536]{1,0:T(8,128)(2,1)} %bitcast.13), channel_id=1, source_target_pairs={{0,32},{32,0},{1,33},{33,1},{2,34},{34,2},{3,35},{35,3},{4,36},{36... | collective-permute-start | bytes 2359304 | tf_op jit(solution)/shard_map/ppermute | solution.py:380
  9.6 29.9 %collective-permute-start.6 = (bf16[256,1536]{1,0:T(8,128)(2,1)}, bf16[256,1536]{1,0:T(8,128)(2,1)S(1)}, u32[]{:S(2)}, u32[]{:S(2)}) collective-permute-start(bf16[256,1536]{1,0:T(8,128)(2,1)} %bitcast.15), channel_id=1, source_target_pairs={{0,32},{32,0},{1,33},{33,1},{2,34},{34,2},{3,35},{35,3},{4,36},{36... | collective-permute-start | bytes 2359304 | tf_op jit(solution)/shard_map/ppermute | solution.py:380
  11.5 3.5 %collective-permute-start = (bf16[64,256]{1,0:T(8,128)(2,1)}, bf16[64,256]{1,0:T(8,128)(2,1)S(1)}, u32[]{:S(2)}, u32[]{:S(2)}) collective-permute-start(bf16[64,256]{1,0:T(8,128)(2,1)} %refs_1_.2), channel_id=1, source_target_pairs={{0,32},{32,0},{1,33},{33,1},{2,34},{34,2},{3,35},{35,3},{4,36},{36... | collective-permute-start | bytes 98312 | tf_op jit(solution)/shard_map/ppermute | solution.py:380
  15.7 0.8 copy-start.13
  17.7 0.7 copy-start.5
  18.4 21.1 %all-to-all-start = ((bf16[32,40,128]{2,1,0:T(8,128)(2,1)}), bf16[32,40,128]{2,1,0:T(8,128)(2,1)S(1)}, u32[]{:S(2)}, u32[]{:S(2)}) async-start(bf16[32,40,128]{2,1,0:T(8,128)(2,1)} %bitcast.19), calls=%async_computation | async-start | bytes 655360 | tf_op jit(solution)/shard_map/all_to_all | solution.py:394
  25.7 1.0 copy-start.3
  26.7 1.0 copy-start.4
  29.3 17.4 %collective-permute-start.7 = (bf16[512,256]{1,0:T(8,128)(2,1)}, bf16[512,256]{1,0:T(8,128)(2,1)}, u32[]{:S(2)}, u32[]{:S(2)}) collective-permute-start(bf16[512,256]{1,0:T(8,128)(2,1)} %get-tuple-element.31.refs_0_), channel_id=1, source_target_pairs={{0,64},{64,128},{128,192},{1,65},{65,129},{129,193},{2,66},{66,130... | collective-permute-start | bytes 786440 | tf_op jit(solution)/shard_map/ppermute | solution.py:413
  33.1 13.6 %collective-permute-start.8 = (bf16[512,256]{1,0:T(8,128)(2,1)}, bf16[512,256]{1,0:T(8,128)(2,1)}, u32[]{:S(2)}, u32[]{:S(2)}) collective-permute-start(bf16[512,256]{1,0:T(8,128)(2,1)} %get-tuple-element.31.refs_0_), channel_id=1, source_target_pairs={{0,128},{64,192},{1,129},{65,193},{2,130},{66,194},{3,131},{67,195... | collective-permute-start | bytes 786440 | tf_op jit(solution)/shard_map/ppermute | solution.py:413
  37.5 9.7 %collective-permute-start.9 = (bf16[512,256]{1,0:T(8,128)(2,1)}, bf16[512,256]{1,0:T(8,128)(2,1)}, u32[]{:S(2)}, u32[]{:S(2)}) collective-permute-start(bf16[512,256]{1,0:T(8,128)(2,1)} %get-tuple-element.31.refs_0_), channel_id=1, source_target_pairs={{0,192},{1,193},{2,194},{3,195},{4,196},{5,197},{6,198},{7,199},{8... | collective-permute-start | bytes 786440 | tf_op jit(solution)/shard_map/ppermute | solution.py:413
  43.0 17.0 %copy-start.11 = (bf16[512,256]{1,0:T(8,128)(2,1)S(1)}, bf16[512,256]{1,0:T(8,128)(2,1)}, u32[]{:S(2)}) copy-start(bf16[512,256]{1,0:T(8,128)(2,1)} %refs_0_.5) | copy-start | bytes 786436
  43.0 28.6 %all-to-all-start.1 = ((bf16[4,288,768]{2,1,0:T(8,128)(2,1)}), bf16[4,288,768]{2,1,0:T(8,128)(2,1)S(1)}, u32[]{:S(2)}, u32[]{:S(2)}) async-start(bf16[4,288,768]{2,1,0:T(8,128)(2,1)} %get-tuple-element.30), calls=%async_computation.1 | async-start | bytes 3538944 | tf_op jit(solution)/shard_map/all_to_all | solution.py:430
  49.0 10.9 %collective-permute-start.10 = (bf16[4,512,256]{2,1,0:T(8,128)(2,1)S(1)}, bf16[4,512,256]{2,1,0:T(8,128)(2,1)S(1)}, u32[]{:S(2)}, u32[]{:S(2)}) collective-permute-start(bf16[4,512,256]{2,1,0:T(8,128)(2,1)S(1)} %get-tuple-element.33.refs_1_), channel_id=1, source_target_pairs={{0,32},{32,0},{1,33},{33,1},{2,34},{34,2},{3,35},{35,3},{4,36},{36... | collective-permute-start | bytes 3145736 | tf_op jit(solution)/shard_map/ppermute | solution.py:380
  51.6 20.0 %collective-permute-start.1 = (bf16[512,256]{1,0:T(8,128)(2,1)}, bf16[512,256]{1,0:T(8,128)(2,1)S(1)}, u32[]{:S(2)}, u32[]{:S(2)}) collective-permute-start(bf16[512,256]{1,0:T(8,128)(2,1)} %copy-done.12), channel_id=1, source_target_pairs={{0,280},{8,272},{16,264},{24,256},{1,281},{9,273},{17,265},{25,257... | collective-permute-start | bytes 786440 | tf_op jit(solution)/shard_map/ppermute | solution.py:409
  62.3 1.0 copy-start.15
  63.3 0.8 copy-start.16
  64.1 14.6 %copy-start.2 = (bf16[1,1536,256]{2,1,0:T(8,128)(2,1)S(1)}, bf16[1,1536,256]{2,1,0:T(8,128)(2,1)}, u32[]{:S(2)}) copy-start(bf16[1,1536,256]{2,1,0:T(8,128)(2,1)} %param.17) | copy-start | bytes 2359300
  64.1 18.7 %copy-start.8 = (s32[64,8]{0,1:T(8,128)S(1)}, s32[64,8]{0,1:T(8,128)}, u32[]{:S(2)}) copy-start(s32[64,8]{0,1:T(8,128)} %param.13) | copy-start | bytes 6148
  64.1 18.7 %copy-start.9 = (f32[64,8]{0,1:T(8,128)S(1)}, f32[64,8]{0,1:T(8,128)}, u32[]{:S(2)}) copy-start(f32[64,8]{0,1:T(8,128)} %param.14) | copy-start | bytes 6148
  71.8 24.9 %collective-permute-start.11 = (bf16[288,768]{1,0:T(8,128)(2,1)S(1)}, bf16[288,768]{1,0:T(8,128)(2,1)S(1)}, u32[]{:S(2)}, u32[]{:S(2)}) collective-permute-start(bf16[288,768]{1,0:T(8,128)(2,1)S(1)} %get-tuple-element.36), channel_id=1, source_target_pairs={{0,256},{256,0},{1,257},{257,1},{2,258},{258,2},{3,259},{259,3},{4... | collective-permute-start | bytes 1327112 | tf_op jit(solution)/shard_map/ppermute | solution.py:453
  76.6 20.2 %collective-permute-start.2 = (bf16[512,256]{1,0:T(8,128)(2,1)S(1)}, bf16[512,256]{1,0:T(8,128)(2,1)S(1)}, u32[]{:S(2)}, u32[]{:S(2)}) collective-permute-start(bf16[512,256]{1,0:T(8,128)(2,1)S(1)} %collective-permute-done.1.refs_2_.refs_0_), channel_id=1, source_target_pairs={{256,320},{320,384},{384,448},{448,256},{257,321},{321,385},{385,4... | collective-permute-start | bytes 786440 | tf_op jit(solution)/shard_map/ppermute | solution.py:416
  77.3 19.5 %collective-permute-start.3 = (bf16[512,256]{1,0:T(8,128)(2,1)S(1)}, bf16[512,256]{1,0:T(8,128)(2,1)S(1)}, u32[]{:S(2)}, u32[]{:S(2)}) collective-permute-start(bf16[512,256]{1,0:T(8,128)(2,1)S(1)} %collective-permute-done.1.refs_2_.refs_0_), channel_id=1, source_target_pairs={{256,384},{320,448},{384,256},{448,320},{257,385},{321,449},{385,2... | collective-permute-start | bytes 786440 | tf_op jit(solution)/shard_map/ppermute | solution.py:416
  78.0 18.9 %collective-permute-start.4 = (bf16[512,256]{1,0:T(8,128)(2,1)S(1)}, bf16[512,256]{1,0:T(8,128)(2,1)S(1)}, u32[]{:S(2)}, u32[]{:S(2)}) collective-permute-start(bf16[512,256]{1,0:T(8,128)(2,1)S(1)} %collective-permute-done.1.refs_2_.refs_0_), channel_id=1, source_target_pairs={{256,448},{320,256},{384,320},{448,384},{257,449},{321,257},{385,3... | collective-permute-start | bytes 786440 | tf_op jit(solution)/shard_map/ppermute | solution.py:416
  78.7 37.3 %collective-permute-start.13 = (bf16[1536,256]{1,0:T(8,128)(2,1)S(1)}, bf16[1536,256]{1,0:T(8,128)(2,1)S(1)}, u32[]{:S(2)}, u32[]{:S(2)}) collective-permute-start(bf16[1536,256]{1,0:T(8,128)(2,1)S(1)} %bitcast.17), channel_id=1, source_target_pairs={{0,32},{32,0},{1,33},{33,1},{2,34},{34,2},{3,35},{35,3},{4,36},{36... | collective-permute-start | bytes 2359304 | tf_op jit(solution)/shard_map/ppermute | solution.py:380
  97.5 20.9 %copy-start.10 = (bf16[4,512,256]{2,1,0:T(8,128)(2,1)}, bf16[4,512,256]{2,1,0:T(8,128)(2,1)S(1)}, u32[]{:S(2)}) copy-start(bf16[4,512,256]{2,1,0:T(8,128)(2,1)S(1)} %get-tuple-element.40.refs_1_) | copy-start | bytes 3145732
  97.5 28.1 %collective-permute-start.12 = (bf16[4,512,256]{2,1,0:T(8,128)(2,1)S(1)}, bf16[4,512,256]{2,1,0:T(8,128)(2,1)}, u32[]{:S(2)}, u32[]{:S(2)}) collective-permute-start(bf16[4,512,256]{2,1,0:T(8,128)(2,1)S(1)} %get-tuple-element.40.refs_1_), channel_id=1, source_target_pairs={{0,32},{32,0},{1,33},{33,1},{2,34},{34,2},{3,35},{35,3},{4,36},{36... | collective-permute-start | bytes 3145736 | tf_op jit(solution)/shard_map/ppermute | solution.py:380
  118.5 7.2 %copy-start.14 = (f32[8,128]{1,0:T(8,128)}, f32[8,128]{1,0:T(8,128)S(1)}, u32[]{:S(2)}) copy-start(f32[8,128]{1,0:T(8,128)S(1)} %get-tuple-element.44.refs_5_) | copy-start | bytes 12292
  118.5 17.5 %all-to-all-start.2 = ((bf16[32,40,128]{2,1,0:T(8,128)(2,1)}), bf16[32,40,128]{2,1,0:T(8,128)(2,1)S(1)}, u32[]{:S(2)}, u32[]{:S(2)}) async-start(bf16[32,40,128]{2,1,0:T(8,128)(2,1)} %bitcast.8), calls=%async_computation.2 | async-start | bytes 655360 | tf_op jit(solution)/shard_map/all_to_all | solution.py:483
  138.3 7.0 %collective-permute-start.14 = (f32[64,256]{1,0:T(8,128)S(1)}, f32[64,256]{1,0:T(8,128)S(1)}, u32[]{:S(2)}, u32[]{:S(2)}) collective-permute-start(f32[64,256]{1,0:T(8,128)S(1)} %get-tuple-element.50), channel_id=1, source_target_pairs={{0,32},{32,0},{1,33},{33,1},{2,34},{34,2},{3,35},{35,3},{4,36},{36... | collective-permute-start | bytes 196616 | tf_op jit(solution)/shard_map/ppermute | solution.py:380
  (3 other events, 2.1 us)

commit v4 on v3

--- a/solution.py
+++ b/solution.py
@@ -81,7 +81,7 @@
             *scratch,
             *([pltpu.SemaphoreType.DMA((copies,))] if copies else []),
         ],
-        compiler_params=pltpu.CompilerParams(vmem_limit_bytes=(60 if copies else 32) << 20),
+        compiler_params=pltpu.CompilerParams(vmem_limit_bytes=(60 if fetched else 32) << 20),
         cost_estimate=pl.CostEstimate(
             flops=flops, bytes_accessed=moved, transcendentals=transcendentals
         ),
@@ -263,9 +263,7 @@
     )
 
 
-def products_kernel(
-    rows_ref, gate_ref, up_ref, sibling_gate_ref, sibling_up_ref, out_ref
-):
+def products_kernel(rows_ref, own_ref, sibling_ref, out_ref):
     tight, _ = block_rows((1, SLOTS), 1)
     pack = jnp.where(tight == lax.broadcasted_iota(jnp.int32, (ROWS, SLOTS), 0), 1.0, 0.0)
     rows = jnp.dot(pack.astype(BF16), widen(rows_ref[...]), preferred_element_type=F32)
@@ -277,10 +275,10 @@
     cols = out_ref.shape[2] // 2
     for i in range(out_ref.shape[0]):
         sl = slice(i * cols, (i + 1) * cols)
-        for j, (mine, its) in enumerate(((gate_ref, sibling_gate_ref), (up_ref, sibling_up_ref))):
+        for j in range(2):
             out_ref[i, :, j * cols : (j + 1) * cols] = (
-                jnp.dot(own, mine[:, sl], preferred_element_type=F32)
-                + jnp.dot(sibling, its[:, sl], preferred_element_type=F32)
+                jnp.dot(own, own_ref[j, :, sl], preferred_element_type=F32)
+                + jnp.dot(sibling, sibling_ref[j, :, sl], preferred_element_type=F32)
             ).astype(BF16)
 
 
@@ -363,7 +361,7 @@
         moved=0,
         name=name,
         after=after,
-    )[0]
+    )
 
 
 def body(
@@ -383,7 +381,7 @@
     ids = expert_ids.T
     block = (EXPERTS, ROOM, HD)
 
-    outbound, sent = call(
+    outbound, _ = call(
         dispatch_kernel,
         [shape((SLOTS, HD))],
         (ids, token_states, swap(token_states)),
@@ -402,7 +400,6 @@
         moved=0,
         scratch=[pltpu.SemaphoreType.DMA((4,))],
         name="head_columns",
-        after=(sent,),
         fetched=(0, 1),
         bare=True,
     )
@@ -419,16 +416,17 @@
         for k in range(1, lanes)
     ]
     cols = 2 * FF // lanes
+    gate_up, _ = stack((gate, up), (), "pair_weights")
     products, multiplied = call(
         products_kernel,
         [shape((lanes, ROWS, cols))],
-        (received.reshape(SLOTS, HD), gate, up, swap(gate), swap(up)),
+        (received.reshape(SLOTS, HD), gate_up, swap(gate_up)),
         flops=2 * ROWS * 4 * width * FF,
         moved=5 << 20,
         name="products",
     )
     parts = lax.all_to_all(products, "x", 0, 0, tiled=True)
-    near = stack(near, (multiplied,), "stack_near")
+    near, _ = stack(near, (multiplied,), "stack_near")
     stacked = queries.shape[0] * queries.shape[1] // HD
     spread = shape((stacked, 2 * HD))
     running = [shape((stacked, 2 * HD), F32), shape((stacked, HD), F32)]
@@ -471,7 +469,7 @@
         after=(mapped,),
     )
     hidden_all = lax.all_gather(hidden, "x", axis=0)
-    far = stack(far, (ready,), "stack_far")
+    far, _ = stack(far, (ready,), "stack_far")
     finished, projected = call(
         project_kernel,
         [shape((SLOTS, HD))],

time: 147 us -> 146 us (level)
  starting transfers between devices: 73.2 us -> 71.2 us
  Pallas kernels: 20.3 us -> 22 us
  blocking collectives: 14.8 us -> 13.3 us
    ppermute x7 -> x6, starting transfers between devices: 29.7 us -> 27.3 us  [body(): swap = lambda a: lax.ppermute(a, 'c', [(0, 1), (1, 0)])]
    pallas_call x13 -> x14, Pallas kernels: 20.3 us -> 22 us  [call(): pl.pallas_call(run, out_shape=outs, in_specs=[ANY if i in fetched else VM...]
    all_gather x1, blocking collectives: 14.8 us -> 13.3 us  [body(): hidden_all = lax.all_gather(hidden, 'x', axis=0)]
    unnamed x34 -> x30, local copies, waits for them, and re-layouts: 7.44 us -> 7.88 us
  transfers between devices with their start and end apart: 18 -> 17, of which waited for: 6 -> 6; matrix products, arithmetic and copies ran while one was open for 0% -> 0% of each run, Pallas kernels for 12% -> 13%
where the time goes in v4:
time: 146 us; the launch traced here: 145 us
  starting transfers between devices  71.2 us (49%)
  waiting for transfers between devices  29.6 us (20%)
  Pallas kernels  22 us (15%)
  blocking collectives  13.3 us (9%)
  local copies, waits for them, and re-layouts  7.88 us (5%)
    ppermute x6, starting transfers between devices, body(): swap = lambda a: lax.ppermute(a, 'c', [(0, 1), (1, 0)])  27.3 us
    pallas_call x14, Pallas kernels, call(): pl.pallas_call(run, out_shape=outs, in_specs=[ANY if i in fetched else VM...  22 us
    ppermute x1, waiting for transfers between devices, body(): other = lax.ppermute(low, 'w', [(0, 1), (1, 0)])  13.7 us
    all_gather x1, blocking collectives, body(): hidden_all = lax.all_gather(hidden, 'x', axis=0)  13.3 us
    ppermute x3, starting transfers between devices, body(): lax.ppermute(kv, 'x', [(x, x + k) for x in range(lanes - k)])  10.2 us
    unnamed x30, local copies, waits for them, and re-layouts  7.88 us
    all_to_all x1, starting transfers between devices, body(): back = lax.all_to_all(finished.reshape(block), ('z', 'y'), 0, 0, tiled=True)  7.54 us
    all_to_all x1, starting transfers between devices, body(): lax.all_to_all(outbound.reshape(block), ('z', 'y'), 0, 0, tiled=True)  7.26 us
  transfers between devices with their start and end apart: 17, of which 6 were waited for; matrix products, arithmetic and copies ran while one was open for 0% of the time, Pallas kernels for 13%

profile of v4, /device:TPU:1, one launch (start us, length us, event | category | flops | bytes accessed | tf_op | source)
XLA Modules:
  0.0 144.9 jit_solution(9263797877570397816)
XLA Ops:
  0.6 1.1 copy-done
  1.8 1.1 copy-done.1
  3.6 8.8 %collective-permute-start.5 = (bf16[2,256,1536]{2,1,0:T(8,128)(2,1)S(1)}, bf16[2,256,1536]{2,1,0:T(8,128)(2,1)S(1)}, u32[]{:S(2)}, u32[]{:S(2)}) collective-permute-start(bf16[2,256,1536]{2,1,0:T(8,128)(2,1)S(1)} %get-tuple-element.29.refs_1_), channel_id=1, source_target_pairs={{0,32},{32,0},{1,33},{33,1},{2,34},{34,2},{3,35},{35,3},{4,36},{36... | collective-permute-start | bytes 4718600 | tf_op jit(solution)/shard_map/ppermute | solution.py:378
  12.4 1.9 %collective-permute-start.4 = (bf16[64,256]{1,0:T(8,128)(2,1)}, bf16[64,256]{1,0:T(8,128)(2,1)S(1)}, u32[]{:S(2)}, u32[]{:S(2)}) collective-permute-start(bf16[64,256]{1,0:T(8,128)(2,1)} %refs_1_.3), channel_id=1, source_target_pairs={{0,32},{32,0},{1,33},{33,1},{2,34},{34,2},{3,35},{35,3},{4,36},{36... | collective-permute-start | bytes 98312 | tf_op jit(solution)/shard_map/ppermute | solution.py:378
  14.3 1.4 collective-permute-done.4.refs_2_
  17.1 1.2 dispatch.1
  19.1 7.3 %all-to-all-start = ((bf16[32,40,128]{2,1,0:T(8,128)(2,1)}), bf16[32,40,128]{2,1,0:T(8,128)(2,1)S(1)}, u32[]{:S(2)}, u32[]{:S(2)}) async-start(bf16[32,40,128]{2,1,0:T(8,128)(2,1)} %bitcast.17), calls=%async_computation | async-start | bytes 655360 | tf_op jit(solution)/shard_map/all_to_all | solution.py:392
  26.4 1.9 %head_columns.1 = (bf16[512,256]{1,0:T(8,128)(2,1)}, bf16[512,256]{1,0:T(8,128)(2,1)}, f32[8,128]{1,0:T(8,128)}) custom-call(bf16[512,512]{1,0:T(8,128)(2,1)} %refs_0_.3, bf16[512,512]{1,0:T(8,128)(2,1)} %refs_1_.2), custom_call_target="tpu_custom_call" | custom-call | tf_op jit(solution)/shard_map/head_columns/pallas_call | solution.py:74
  28.3 3.8 %collective-permute-start.6 = (bf16[512,256]{1,0:T(8,128)(2,1)}, bf16[512,256]{1,0:T(8,128)(2,1)}, u32[]{:S(2)}, u32[]{:S(2)}) collective-permute-start(bf16[512,256]{1,0:T(8,128)(2,1)} %get-tuple-element.31.refs_0_), channel_id=1, source_target_pairs={{0,64},{64,128},{128,192},{1,65},{65,129},{129,193},{2,66},{66,130... | collective-permute-start | bytes 786440 | tf_op jit(solution)/shard_map/ppermute | solution.py:410
  32.2 4.3 %collective-permute-start.7 = (bf16[512,256]{1,0:T(8,128)(2,1)}, bf16[512,256]{1,0:T(8,128)(2,1)}, u32[]{:S(2)}, u32[]{:S(2)}) collective-permute-start(bf16[512,256]{1,0:T(8,128)(2,1)} %get-tuple-element.31.refs_0_), channel_id=1, source_target_pairs={{0,128},{64,192},{1,129},{65,193},{2,130},{66,194},{3,131},{67,195... | collective-permute-start | bytes 786440 | tf_op jit(solution)/shard_map/ppermute | solution.py:410
  36.5 2.0 %collective-permute-start.8 = (bf16[512,256]{1,0:T(8,128)(2,1)}, bf16[512,256]{1,0:T(8,128)(2,1)}, u32[]{:S(2)}, u32[]{:S(2)}) collective-permute-start(bf16[512,256]{1,0:T(8,128)(2,1)} %get-tuple-element.31.refs_0_), channel_id=1, source_target_pairs={{0,192},{1,193},{2,194},{3,195},{4,196},{5,197},{6,198},{7,199},{8... | collective-permute-start | bytes 786440 | tf_op jit(solution)/shard_map/ppermute | solution.py:410
  38.5 3.5 %products.1 = (bf16[4,288,768]{2,1,0:T(8,128)(2,1)}, f32[8,128]{1,0:T(8,128)S(1)}) custom-call(bf16[1280,128]{1,0:T(8,128)(2,1)S(1)} %bitcast.12, bf16[2,256,1536]{2,1,0:T(8,128)(2,1)S(1)} %get-tuple-element.29.refs_1_, bf16[2,256,1536]{2,1,0:T(8,128)(2,1)S(1)} %collective-permute-done.5.refs_2_), custom_call_target="tpu_custom_call" | custom-call | flops 905969664 | bytes 5242880 | tf_op jit(solution)/shard_map/products/pallas_call | solution.py:74
  42.0 3.7 %all-to-all-start.1 = ((bf16[4,288,768]{2,1,0:T(8,128)(2,1)}), bf16[4,288,768]{2,1,0:T(8,128)(2,1)S(1)}, u32[]{:S(2)}, u32[]{:S(2)}) async-start(bf16[4,288,768]{2,1,0:T(8,128)(2,1)} %get-tuple-element.30), calls=%async_computation.1 | async-start | bytes 3538944 | tf_op jit(solution)/shard_map/all_to_all | solution.py:428
  46.3 1.7 %stack_near.1 = (bf16[4,512,256]{2,1,0:T(8,128)(2,1)S(1)}, f32[8,128]{1,0:T(8,128)}) custom-call(bf16[512,256]{1,0:T(8,128)(2,1)S(1)} %copy-done.4, bf16[512,256]{1,0:T(8,128)(2,1)} %collective-permute-done.6.refs_1_, bf16[512,256]{1,0:T(8,128)(2,1)} %collective-permute-done.7.refs_2_, bf16[512,256]{1,0:T(8,128)(2,1)} %collective-permute-done.8.refs_3_, ...), custom_call_target="tpu_custom_call" | custom-call | tf_op jit(solution)/shard_map/stack_near/pallas_call | solution.py:74
  48.0 4.0 %collective-permute-start.9 = (bf16[4,512,256]{2,1,0:T(8,128)(2,1)S(1)}, bf16[4,512,256]{2,1,0:T(8,128)(2,1)S(1)}, u32[]{:S(2)}, u32[]{:S(2)}) collective-permute-start(bf16[4,512,256]{2,1,0:T(8,128)(2,1)S(1)} %get-tuple-element.33.refs_1_), channel_id=1, source_target_pairs={{0,32},{32,0},{1,33},{33,1},{2,34},{34,2},{3,35},{35,3},{4,36},{36... | collective-permute-start | bytes 3145736 | tf_op jit(solution)/shard_map/ppermute | solution.py:378
  52.0 6.9 %collective-permute-start = (bf16[512,256]{1,0:T(8,128)(2,1)}, bf16[512,256]{1,0:T(8,128)(2,1)S(1)}, u32[]{:S(2)}, u32[]{:S(2)}) collective-permute-start(bf16[512,256]{1,0:T(8,128)(2,1)} %get-tuple-element.27), channel_id=1, source_target_pairs={{0,280},{8,272},{16,264},{24,256},{1,281},{9,273},{17,265},{25,257... | collective-permute-start | bytes 786440 | tf_op jit(solution)/shard_map/ppermute | solution.py:406
  58.9 0.9 copy-done.10
  59.8 2.4 %attention_near.1 = (f32[1024,256]{1,0:T(8,128)S(1)}, f32[1024,128]{1,0:T(8,128)S(1)}, f32[8,128]{1,0:T(8,128)S(1)}) custom-call(bf16[512,256]{1,0:T(8,128)(2,1)S(1)} %copy-done.10, bf16[4,512,256]{2,1,0:T(8,128)(2,1)S(1)} %get-tuple-element.33.refs_1_, bf16[4,512,256]{2,1,0:T(8,128)(2,1)S(1)} %collective-permute-done.9.refs_2_, ...), custom_call_target="tpu_custom_call" | custom-call | flops 2147483648 | bytes 5242880 | tf_op jit(solution)/shard_map/attention_near/pallas_call | solution.py:74
  62.2 1.0 copy-done.13
  64.0 6.4 %collective-permute-done.refs_2_.refs_0_ = bf16[512,256]{1,0:T(8,128)(2,1)S(1)} collective-permute-done((bf16[512,256]{1,0:T(8,128)(2,1)}, bf16[512,256]{1,0:T(8,128)(2,1)S(1)}, u32[]{:S(2)}, u32[]{:S(2)}) %collective-permute-start) | collective-permute-done | bytes 262176 | tf_op jit(solution)/shard_map/ppermute | solution.py:406
  70.7 6.3 %collective-permute-start.10 = (bf16[288,768]{1,0:T(8,128)(2,1)S(1)}, bf16[288,768]{1,0:T(8,128)(2,1)S(1)}, u32[]{:S(2)}, u32[]{:S(2)}) collective-permute-start(bf16[288,768]{1,0:T(8,128)(2,1)S(1)} %get-tuple-element.36), channel_id=1, source_target_pairs={{0,256},{256,0},{1,257},{257,1},{2,258},{258,2},{3,259},{259,3},{4... | collective-permute-start | bytes 1327112 | tf_op jit(solution)/shard_map/ppermute | solution.py:451
  79.1 3.0 %collective-permute-start.12 = (bf16[1536,256]{1,0:T(8,128)(2,1)S(1)}, bf16[1536,256]{1,0:T(8,128)(2,1)S(1)}, u32[]{:S(2)}, u32[]{:S(2)}) collective-permute-start(bf16[1536,256]{1,0:T(8,128)(2,1)S(1)} %bitcast.15), channel_id=1, source_target_pairs={{0,32},{32,0},{1,33},{33,1},{2,34},{34,2},{3,35},{35,3},{4,36},{36... | collective-permute-start | bytes 2359304 | tf_op jit(solution)/shard_map/ppermute | solution.py:378
  82.1 1.0 combine_map.1
  83.1 13.7 %collective-permute-done.10.refs_1_ = bf16[288,768]{1,0:T(8,128)(2,1)S(1)} collective-permute-done((bf16[288,768]{1,0:T(8,128)(2,1)S(1)}, bf16[288,768]{1,0:T(8,128)(2,1)S(1)}, u32[]{:S(2)}, u32[]{:S(2)}) %collective-permute-start.10) | collective-permute-done | bytes 442400 | tf_op jit(solution)/shard_map/ppermute | solution.py:451
  97.7 3.6 %collective-permute-start.11 = (bf16[4,512,256]{2,1,0:T(8,128)(2,1)S(1)}, bf16[4,512,256]{2,1,0:T(8,128)(2,1)}, u32[]{:S(2)}, u32[]{:S(2)}) collective-permute-start(bf16[4,512,256]{2,1,0:T(8,128)(2,1)S(1)} %get-tuple-element.40.refs_1_), channel_id=1, source_target_pairs={{0,32},{32,0},{1,33},{33,1},{2,34},{34,2},{3,35},{35,3},{4,36},{36... | collective-permute-start | bytes 3145736 | tf_op jit(solution)/shard_map/ppermute | solution.py:378
  101.4 13.3 %all-gather = bf16[1152,384]{1,0:T(8,128)(2,1)S(1)} all-gather(bf16[288,384]{1,0:T(8,128)(2,1)S(1)} %get-tuple-element.43), channel_id=2, replica_groups=mesh['w'=2,'x'=4,'c'=2,'z'=4,'y'=8] {'x'}, dimensions={0}, use_global_device_ids=true | all-gather | bytes 1105920 | tf_op jit(solution)/shard_map/all_gather | solution.py:471
  114.7 2.4 %project.1 = (bf16[1280,128]{1,0:T(8,128)(2,1)}, f32[8,128]{1,0:T(8,128)S(1)}) custom-call(bf16[4,288,384]{2,1,0:T(8,128)(2,1)S(1)} %bitcast.10, bf16[1536,256]{1,0:T(8,128)(2,1)S(1)} %bitcast.16, bf16[1536,256]{1,0:T(8,128)(2,1)S(1)} %collective-permute-done.12.refs_2_), custom_call_target="tpu_custom_call" | custom-call | flops 452984832 | bytes 3145728 | tf_op jit(solution)/shard_map/project/pallas_call | solution.py:74
  117.1 7.5 %all-to-all-start.2 = ((bf16[32,40,128]{2,1,0:T(8,128)(2,1)}), bf16[32,40,128]{2,1,0:T(8,128)(2,1)S(1)}, u32[]{:S(2)}, u32[]{:S(2)}) async-start(bf16[32,40,128]{2,1,0:T(8,128)(2,1)} %bitcast.8), calls=%async_computation.2 | async-start | bytes 655360 | tf_op jit(solution)/shard_map/all_to_all | solution.py:481
  124.6 3.7 %attention_far.1 = (bf16[512,256]{1,0:T(8,128)(2,1)}, f32[8,128]{1,0:T(8,128)}) custom-call(bf16[512,256]{1,0:T(8,128)(2,1)} %refs_0_.5, bf16[4,512,256]{2,1,0:T(8,128)(2,1)} %copy-done.9, bf16[4,512,256]{2,1,0:T(8,128)(2,1)} %collective-permute-done.11.refs_2_, f32[1024,256]{1,0:T(8,128)} %copy-done.13, f32[1024,128]{1,0:T(8,128)} %copy-done.14, ...), custom_call_target="tpu_custom_call" | custom-call | flops 2147483648 | bytes 5242880 | tf_op jit(solution)/shard_map/attention_far/pallas_call | solution.py:74
  128.4 6.7 %all-to-all-done.2 = bf16[32,40,128]{2,1,0:T(8,128)(2,1)S(1)} async-done(((bf16[32,40,128]{2,1,0:T(8,128)(2,1)}), bf16[32,40,128]{2,1,0:T(8,128)(2,1)S(1)}, u32[]{:S(2)}, u32[]{:S(2)}) %all-to-all-start.2) | async-done | bytes 327712 | tf_op jit(solution)/shard_map/all_to_all | solution.py:481
  135.7 1.7 %combine.1 = (f32[64,256]{1,0:T(8,128)S(1)}, f32[64,256]{1,0:T(8,128)S(1)}, f32[8,128]{1,0:T(8,128)}) custom-call(f32[1280,64]{1,0:T(8,128)S(1)} %get-tuple-element.46.refs_0_, bf16[1280,128]{1,0:T(8,128)(2,1)S(1)} %bitcast.11, f32[8,128]{1,0:T(8,128)S(1)} %copy-done.5), custom_call_target="tpu_custom_call" | custom-call | flops 251658240 | bytes 1048576 | tf_op jit(solution)/shard_map/combine/pallas_call | solution.py:74
  137.4 6.0 %collective-permute-start.13 = (f32[64,256]{1,0:T(8,128)S(1)}, f32[64,256]{1,0:T(8,128)S(1)}, u32[]{:S(2)}, u32[]{:S(2)}) collective-permute-start(f32[64,256]{1,0:T(8,128)S(1)} %get-tuple-element.50), channel_id=1, source_target_pairs={{0,32},{32,0},{1,33},{33,1},{2,34},{34,2},{3,35},{35,3},{4,36},{36... | collective-permute-start | bytes 196616 | tf_op jit(solution)/shard_map/ppermute | solution.py:378
  (47 shorter events, 9.5 us)
Async XLA Ops:
  0.6 1.1 copy-start
  1.8 1.1 copy-start.1
  3.6 34.9 %collective-permute-start.5 = (bf16[2,256,1536]{2,1,0:T(8,128)(2,1)S(1)}, bf16[2,256,1536]{2,1,0:T(8,128)(2,1)S(1)}, u32[]{:S(2)}, u32[]{:S(2)}) collective-permute-start(bf16[2,256,1536]{2,1,0:T(8,128)(2,1)S(1)} %get-tuple-element.29.refs_1_), channel_id=1, source_target_pairs={{0,32},{32,0},{1,33},{33,1},{2,34},{34,2},{3,35},{35,3},{4,36},{36... | collective-permute-start | bytes 4718600 | tf_op jit(solution)/shard_map/ppermute | solution.py:378
  12.4 3.3 %collective-permute-start.4 = (bf16[64,256]{1,0:T(8,128)(2,1)}, bf16[64,256]{1,0:T(8,128)(2,1)S(1)}, u32[]{:S(2)}, u32[]{:S(2)}) collective-permute-start(bf16[64,256]{1,0:T(8,128)(2,1)} %refs_1_.3), channel_id=1, source_target_pairs={{0,32},{32,0},{1,33},{33,1},{2,34},{34,2},{3,35},{35,3},{4,36},{36... | collective-permute-start | bytes 98312 | tf_op jit(solution)/shard_map/ppermute | solution.py:378
  15.7 0.7 copy-start.6
  16.4 0.8 copy-start.11
  18.4 0.7 copy-start.3
  19.1 19.4 %all-to-all-start = ((bf16[32,40,128]{2,1,0:T(8,128)(2,1)}), bf16[32,40,128]{2,1,0:T(8,128)(2,1)S(1)}, u32[]{:S(2)}, u32[]{:S(2)}) async-start(bf16[32,40,128]{2,1,0:T(8,128)(2,1)} %bitcast.17), calls=%async_computation | async-start | bytes 655360 | tf_op jit(solution)/shard_map/all_to_all | solution.py:392
  28.3 17.4 %collective-permute-start.6 = (bf16[512,256]{1,0:T(8,128)(2,1)}, bf16[512,256]{1,0:T(8,128)(2,1)}, u32[]{:S(2)}, u32[]{:S(2)}) collective-permute-start(bf16[512,256]{1,0:T(8,128)(2,1)} %get-tuple-element.31.refs_0_), channel_id=1, source_target_pairs={{0,64},{64,128},{128,192},{1,65},{65,129},{129,193},{2,66},{66,130... | collective-permute-start | bytes 786440 | tf_op jit(solution)/shard_map/ppermute | solution.py:410
  32.2 13.5 %collective-permute-start.7 = (bf16[512,256]{1,0:T(8,128)(2,1)}, bf16[512,256]{1,0:T(8,128)(2,1)}, u32[]{:S(2)}, u32[]{:S(2)}) collective-permute-start(bf16[512,256]{1,0:T(8,128)(2,1)} %get-tuple-element.31.refs_0_), channel_id=1, source_target_pairs={{0,128},{64,192},{1,129},{65,193},{2,130},{66,194},{3,131},{67,195... | collective-permute-start | bytes 786440 | tf_op jit(solution)/shard_map/ppermute | solution.py:410
  36.5 9.7 %collective-permute-start.8 = (bf16[512,256]{1,0:T(8,128)(2,1)}, bf16[512,256]{1,0:T(8,128)(2,1)}, u32[]{:S(2)}, u32[]{:S(2)}) collective-permute-start(bf16[512,256]{1,0:T(8,128)(2,1)} %get-tuple-element.31.refs_0_), channel_id=1, source_target_pairs={{0,192},{1,193},{2,194},{3,195},{4,196},{5,197},{6,198},{7,199},{8... | collective-permute-start | bytes 786440 | tf_op jit(solution)/shard_map/ppermute | solution.py:410
  42.0 4.3 %copy-start.4 = (bf16[512,256]{1,0:T(8,128)(2,1)S(1)}, bf16[512,256]{1,0:T(8,128)(2,1)}, u32[]{:S(2)}) copy-start(bf16[512,256]{1,0:T(8,128)(2,1)} %get-tuple-element.31.refs_0_) | copy-start | bytes 786436
  42.0 28.5 %all-to-all-start.1 = ((bf16[4,288,768]{2,1,0:T(8,128)(2,1)}), bf16[4,288,768]{2,1,0:T(8,128)(2,1)S(1)}, u32[]{:S(2)}, u32[]{:S(2)}) async-start(bf16[4,288,768]{2,1,0:T(8,128)(2,1)} %get-tuple-element.30), calls=%async_computation.1 | async-start | bytes 3538944 | tf_op jit(solution)/shard_map/all_to_all | solution.py:428
  48.0 10.9 %collective-permute-start.9 = (bf16[4,512,256]{2,1,0:T(8,128)(2,1)S(1)}, bf16[4,512,256]{2,1,0:T(8,128)(2,1)S(1)}, u32[]{:S(2)}, u32[]{:S(2)}) collective-permute-start(bf16[4,512,256]{2,1,0:T(8,128)(2,1)S(1)} %get-tuple-element.33.refs_1_), channel_id=1, source_target_pairs={{0,32},{32,0},{1,33},{33,1},{2,34},{34,2},{3,35},{35,3},{4,36},{36... | collective-permute-start | bytes 3145736 | tf_op jit(solution)/shard_map/ppermute | solution.py:378
  52.0 18.5 %collective-permute-start = (bf16[512,256]{1,0:T(8,128)(2,1)}, bf16[512,256]{1,0:T(8,128)(2,1)S(1)}, u32[]{:S(2)}, u32[]{:S(2)}) collective-permute-start(bf16[512,256]{1,0:T(8,128)(2,1)} %get-tuple-element.27), channel_id=1, source_target_pairs={{0,280},{8,272},{16,264},{24,256},{1,281},{9,273},{17,265},{25,257... | collective-permute-start | bytes 786440 | tf_op jit(solution)/shard_map/ppermute | solution.py:406
  58.9 1.0 copy-start.10
  62.2 1.0 copy-start.13
  63.2 0.8 copy-start.14
  64.0 15.0 %copy-start.2 = (bf16[1,1536,256]{2,1,0:T(8,128)(2,1)S(1)}, bf16[1,1536,256]{2,1,0:T(8,128)(2,1)}, u32[]{:S(2)}) copy-start(bf16[1,1536,256]{2,1,0:T(8,128)(2,1)} %param.17) | copy-start | bytes 2359300
  64.0 18.0 %copy-start.7 = (s32[64,8]{0,1:T(8,128)S(1)}, s32[64,8]{0,1:T(8,128)}, u32[]{:S(2)}) copy-start(s32[64,8]{0,1:T(8,128)} %param.13) | copy-start | bytes 6148
  64.0 18.1 %copy-start.8 = (f32[64,8]{0,1:T(8,128)S(1)}, f32[64,8]{0,1:T(8,128)}, u32[]{:S(2)}) copy-start(f32[64,8]{0,1:T(8,128)} %param.14) | copy-start | bytes 6148
  70.7 26.1 %collective-permute-start.10 = (bf16[288,768]{1,0:T(8,128)(2,1)S(1)}, bf16[288,768]{1,0:T(8,128)(2,1)S(1)}, u32[]{:S(2)}, u32[]{:S(2)}) collective-permute-start(bf16[288,768]{1,0:T(8,128)(2,1)S(1)} %get-tuple-element.36), channel_id=1, source_target_pairs={{0,256},{256,0},{1,257},{257,1},{2,258},{258,2},{3,259},{259,3},{4... | collective-permute-start | bytes 1327112 | tf_op jit(solution)/shard_map/ppermute | solution.py:451
  77.0 20.0 %collective-permute-start.1 = (bf16[512,256]{1,0:T(8,128)(2,1)S(1)}, bf16[512,256]{1,0:T(8,128)(2,1)S(1)}, u32[]{:S(2)}, u32[]{:S(2)}) collective-permute-start(bf16[512,256]{1,0:T(8,128)(2,1)S(1)} %collective-permute-done.refs_2_.refs_0_), channel_id=1, source_target_pairs={{256,320},{320,384},{384,448},{448,256},{257,321},{321,385},{385,4... | collective-permute-start | bytes 786440 | tf_op jit(solution)/shard_map/ppermute | solution.py:413
  77.7 19.3 %collective-permute-start.2 = (bf16[512,256]{1,0:T(8,128)(2,1)S(1)}, bf16[512,256]{1,0:T(8,128)(2,1)S(1)}, u32[]{:S(2)}, u32[]{:S(2)}) collective-permute-start(bf16[512,256]{1,0:T(8,128)(2,1)S(1)} %collective-permute-done.refs_2_.refs_0_), channel_id=1, source_target_pairs={{256,384},{320,448},{384,256},{448,320},{257,385},{321,449},{385,2... | collective-permute-start | bytes 786440 | tf_op jit(solution)/shard_map/ppermute | solution.py:413
  78.4 18.7 %collective-permute-start.3 = (bf16[512,256]{1,0:T(8,128)(2,1)S(1)}, bf16[512,256]{1,0:T(8,128)(2,1)S(1)}, u32[]{:S(2)}, u32[]{:S(2)}) collective-permute-start(bf16[512,256]{1,0:T(8,128)(2,1)S(1)} %collective-permute-done.refs_2_.refs_0_), channel_id=1, source_target_pairs={{256,448},{320,256},{384,320},{448,384},{257,449},{321,257},{385,3... | collective-permute-start | bytes 786440 | tf_op jit(solution)/shard_map/ppermute | solution.py:413
  79.1 35.6 %collective-permute-start.12 = (bf16[1536,256]{1,0:T(8,128)(2,1)S(1)}, bf16[1536,256]{1,0:T(8,128)(2,1)S(1)}, u32[]{:S(2)}, u32[]{:S(2)}) collective-permute-start(bf16[1536,256]{1,0:T(8,128)(2,1)S(1)} %bitcast.15), channel_id=1, source_target_pairs={{0,32},{32,0},{1,33},{33,1},{2,34},{34,2},{3,35},{35,3},{4,36},{36... | collective-permute-start | bytes 2359304 | tf_op jit(solution)/shard_map/ppermute | solution.py:378
  97.7 19.3 %copy-start.9 = (bf16[4,512,256]{2,1,0:T(8,128)(2,1)}, bf16[4,512,256]{2,1,0:T(8,128)(2,1)S(1)}, u32[]{:S(2)}) copy-start(bf16[4,512,256]{2,1,0:T(8,128)(2,1)S(1)} %get-tuple-element.40.refs_1_) | copy-start | bytes 3145732
  97.7 26.9 %collective-permute-start.11 = (bf16[4,512,256]{2,1,0:T(8,128)(2,1)S(1)}, bf16[4,512,256]{2,1,0:T(8,128)(2,1)}, u32[]{:S(2)}, u32[]{:S(2)}) collective-permute-start(bf16[4,512,256]{2,1,0:T(8,128)(2,1)S(1)} %get-tuple-element.40.refs_1_), channel_id=1, source_target_pairs={{0,32},{32,0},{1,33},{33,1},{2,34},{34,2},{3,35},{35,3},{4,36},{36... | collective-permute-start | bytes 3145736 | tf_op jit(solution)/shard_map/ppermute | solution.py:378
  117.1 7.6 %copy-start.12 = (f32[8,128]{1,0:T(8,128)}, f32[8,128]{1,0:T(8,128)S(1)}, u32[]{:S(2)}) copy-start(f32[8,128]{1,0:T(8,128)S(1)} %get-tuple-element.44.refs_5_) | copy-start | bytes 12292
  117.1 18.0 %all-to-all-start.2 = ((bf16[32,40,128]{2,1,0:T(8,128)(2,1)}), bf16[32,40,128]{2,1,0:T(8,128)(2,1)S(1)}, u32[]{:S(2)}, u32[]{:S(2)}) async-start(bf16[32,40,128]{2,1,0:T(8,128)(2,1)} %bitcast.8), calls=%async_computation.2 | async-start | bytes 655360 | tf_op jit(solution)/shard_map/all_to_all | solution.py:481
  135.1 0.7 copy-start.5
  137.4 6.9 %collective-permute-start.13 = (f32[64,256]{1,0:T(8,128)S(1)}, f32[64,256]{1,0:T(8,128)S(1)}, u32[]{:S(2)}, u32[]{:S(2)}) collective-permute-start(f32[64,256]{1,0:T(8,128)S(1)} %get-tuple-element.50), channel_id=1, source_target_pairs={{0,32},{32,0},{1,33},{33,1},{2,34},{34,2},{3,35},{35,3},{4,36},{36... | collective-permute-start | bytes 196616 | tf_op jit(solution)/shard_map/ppermute | solution.py:378

commit v5 on v4

--- a/solution.py
+++ b/solution.py
@@ -263,7 +263,7 @@
     )
 
 
-def products_kernel(rows_ref, own_ref, sibling_ref, out_ref):
+def products_kernel(rows_ref, gate_ref, up_ref, sibling_gate_ref, sibling_up_ref, out_ref):
     tight, _ = block_rows((1, SLOTS), 1)
     pack = jnp.where(tight == lax.broadcasted_iota(jnp.int32, (ROWS, SLOTS), 0), 1.0, 0.0)
     rows = jnp.dot(pack.astype(BF16), widen(rows_ref[...]), preferred_element_type=F32)
@@ -275,10 +275,10 @@
     cols = out_ref.shape[2] // 2
     for i in range(out_ref.shape[0]):
         sl = slice(i * cols, (i + 1) * cols)
-        for j in range(2):
+        for j, (mine, its) in enumerate(((gate_ref, sibling_gate_ref), (up_ref, sibling_up_ref))):
             out_ref[i, :, j * cols : (j + 1) * cols] = (
-                jnp.dot(own, own_ref[j, :, sl], preferred_element_type=F32)
-                + jnp.dot(sibling, sibling_ref[j, :, sl], preferred_element_type=F32)
+                jnp.dot(own, mine[:, sl], preferred_element_type=F32)
+                + jnp.dot(sibling, its[:, sl], preferred_element_type=F32)
             ).astype(BF16)
 
 
@@ -416,11 +416,10 @@
         for k in range(1, lanes)
     ]
     cols = 2 * FF // lanes
-    gate_up, _ = stack((gate, up), (), "pair_weights")
     products, multiplied = call(
         products_kernel,
         [shape((lanes, ROWS, cols))],
-        (received.reshape(SLOTS, HD), gate_up, swap(gate_up)),
+        (received.reshape(SLOTS, HD), gate, up, swap(gate), swap(up)),
         flops=2 * ROWS * 4 * width * FF,
         moved=5 << 20,
         name="products",

time: 146 us -> 145 us (level)
  starting transfers between devices: 71.2 us -> 73.7 us
  local copies, waits for them, and re-layouts: 7.88 us -> 5.63 us
    ppermute x6 -> x7, starting transfers between devices: 27.3 us -> 29.9 us  [body(): swap = lambda a: lax.ppermute(a, 'c', [(0, 1), (1, 0)])]
    unnamed x30, local copies, waits for them, and re-layouts: 7.88 us -> 5.63 us
    pallas_call x14 -> x13, Pallas kernels: 22 us -> 21.3 us  [call(): pl.pallas_call(run, out_shape=outs, in_specs=[ANY if i in fetched else VM...]
  transfers between devices with their start and end apart: 17 -> 18, of which waited for: 6 -> 6; matrix products, arithmetic and copies ran while one was open for 0% -> 0% of each run, Pallas kernels for 13% -> 13%
where the time goes in v5:
time: 145 us; the launch traced here: 144 us
  starting transfers between devices  73.7 us (51%)
  waiting for transfers between devices  29.3 us (20%)
  Pallas kernels  21.3 us (15%)
  blocking collectives  13.3 us (9%)
  local copies, waits for them, and re-layouts  5.63 us (4%)
    ppermute x7, starting transfers between devices, body(): swap = lambda a: lax.ppermute(a, 'c', [(0, 1), (1, 0)])  29.9 us
    pallas_call x13, Pallas kernels, call(): pl.pallas_call(run, out_shape=outs, in_specs=[ANY if i in fetched else VM...  21.3 us
    ppermute x1, waiting for transfers between devices, body(): other = lax.ppermute(low, 'w', [(0, 1), (1, 0)])  13.7 us
    all_gather x1, blocking collectives, body(): hidden_all = lax.all_gather(hidden, 'x', axis=0)  13.3 us
    ppermute x3, starting transfers between devices, body(): lax.ppermute(kv, 'x', [(x, x + k) for x in range(lanes - k)])  10.2 us
    all_to_all x1, starting transfers between devices, body(): back = lax.all_to_all(finished.reshape(block), ('z', 'y'), 0, 0, tiled=True)  7.48 us
    all_to_all x1, starting transfers between devices, body(): lax.all_to_all(outbound.reshape(block), ('z', 'y'), 0, 0, tiled=True)  7.26 us
    ppermute x1, starting transfers between devices, body(): lax.ppermute(kv_near, ('w', 'z'), [(z, 2 * z_count - 1 - z) for z in rang...  6.88 us
  transfers between devices with their start and end apart: 18, of which 6 were waited for; matrix products, arithmetic and copies ran while one was open for 0% of the time, Pallas kernels for 13%

profile of v5, /device:TPU:1, one launch (start us, length us, event | category | flops | bytes accessed | tf_op | source)
XLA Modules:
  0.0 144.2 jit_solution(18089823979513997698)
XLA Ops:
  0.7 8.9 %collective-permute-start.5 = (bf16[256,1536]{1,0:T(8,128)(2,1)}, bf16[256,1536]{1,0:T(8,128)(2,1)S(1)}, u32[]{:S(2)}, u32[]{:S(2)}) collective-permute-start(bf16[256,1536]{1,0:T(8,128)(2,1)} %bitcast.13), channel_id=1, source_target_pairs={{0,32},{32,0},{1,33},{33,1},{2,34},{34,2},{3,35},{35,3},{4,36},{36... | collective-permute-start | bytes 2359304 | tf_op jit(solution)/shard_map/ppermute | solution.py:378
  9.6 1.9 %collective-permute-start.6 = (bf16[256,1536]{1,0:T(8,128)(2,1)}, bf16[256,1536]{1,0:T(8,128)(2,1)S(1)}, u32[]{:S(2)}, u32[]{:S(2)}) collective-permute-start(bf16[256,1536]{1,0:T(8,128)(2,1)} %bitcast.15), channel_id=1, source_target_pairs={{0,32},{32,0},{1,33},{33,1},{2,34},{34,2},{3,35},{35,3},{4,36},{36... | collective-permute-start | bytes 2359304 | tf_op jit(solution)/shard_map/ppermute | solution.py:378
  11.5 2.4 %collective-permute-start.4 = (bf16[64,256]{1,0:T(8,128)(2,1)}, bf16[64,256]{1,0:T(8,128)(2,1)S(1)}, u32[]{:S(2)}, u32[]{:S(2)}) collective-permute-start(bf16[64,256]{1,0:T(8,128)(2,1)} %refs_1_.3), channel_id=1, source_target_pairs={{0,32},{32,0},{1,33},{33,1},{2,34},{34,2},{3,35},{35,3},{4,36},{36... | collective-permute-start | bytes 98312 | tf_op jit(solution)/shard_map/ppermute | solution.py:378
  13.9 1.0 collective-permute-done.4.refs_2_
  16.4 1.2 dispatch.1
  18.4 7.3 %all-to-all-start = ((bf16[32,40,128]{2,1,0:T(8,128)(2,1)}), bf16[32,40,128]{2,1,0:T(8,128)(2,1)S(1)}, u32[]{:S(2)}, u32[]{:S(2)}) async-start(bf16[32,40,128]{2,1,0:T(8,128)(2,1)} %bitcast.19), calls=%async_computation | async-start | bytes 655360 | tf_op jit(solution)/shard_map/all_to_all | solution.py:392
  25.7 1.9 %head_columns.1 = (bf16[512,256]{1,0:T(8,128)(2,1)}, bf16[512,256]{1,0:T(8,128)(2,1)}, f32[8,128]{1,0:T(8,128)}) custom-call(bf16[512,512]{1,0:T(8,128)(2,1)} %refs_0_.3, bf16[512,512]{1,0:T(8,128)(2,1)} %refs_1_.2), custom_call_target="tpu_custom_call" | custom-call | tf_op jit(solution)/shard_map/head_columns/pallas_call | solution.py:74
  27.6 3.8 %collective-permute-start.7 = (bf16[512,256]{1,0:T(8,128)(2,1)}, bf16[512,256]{1,0:T(8,128)(2,1)}, u32[]{:S(2)}, u32[]{:S(2)}) collective-permute-start(bf16[512,256]{1,0:T(8,128)(2,1)} %get-tuple-element.29.refs_0_), channel_id=1, source_target_pairs={{0,64},{64,128},{128,192},{1,65},{65,129},{129,193},{2,66},{66,130... | collective-permute-start | bytes 786440 | tf_op jit(solution)/shard_map/ppermute | solution.py:410
  31.5 4.3 %collective-permute-start.8 = (bf16[512,256]{1,0:T(8,128)(2,1)}, bf16[512,256]{1,0:T(8,128)(2,1)}, u32[]{:S(2)}, u32[]{:S(2)}) collective-permute-start(bf16[512,256]{1,0:T(8,128)(2,1)} %get-tuple-element.29.refs_0_), channel_id=1, source_target_pairs={{0,128},{64,192},{1,129},{65,193},{2,130},{66,194},{3,131},{67,195... | collective-permute-start | bytes 786440 | tf_op jit(solution)/shard_map/ppermute | solution.py:410
  35.8 2.0 %collective-permute-start.9 = (bf16[512,256]{1,0:T(8,128)(2,1)}, bf16[512,256]{1,0:T(8,128)(2,1)}, u32[]{:S(2)}, u32[]{:S(2)}) collective-permute-start(bf16[512,256]{1,0:T(8,128)(2,1)} %get-tuple-element.29.refs_0_), channel_id=1, source_target_pairs={{0,192},{1,193},{2,194},{3,195},{4,196},{5,197},{6,198},{7,199},{8... | collective-permute-start | bytes 786440 | tf_op jit(solution)/shard_map/ppermute | solution.py:410
  37.8 3.4 %products.1 = (bf16[4,288,768]{2,1,0:T(8,128)(2,1)}, f32[8,128]{1,0:T(8,128)S(1)}) custom-call(bf16[1280,128]{1,0:T(8,128)(2,1)S(1)} %bitcast.12, bf16[256,1536]{1,0:T(8,128)(2,1)S(1)} %bitcast.14, bf16[256,1536]{1,0:T(8,128)(2,1)S(1)} %bitcast.16, bf16[256,1536]{1,0:T(8,128)(2,1)S(1)} %collective-permute-done.5.refs_3_, ...), custom_call_target="tpu_custom_call" | custom-call | flops 905969664 | bytes 5242880 | tf_op jit(solution)/shard_map/products/pallas_call | solution.py:74
  41.3 3.7 %all-to-all-start.1 = ((bf16[4,288,768]{2,1,0:T(8,128)(2,1)}), bf16[4,288,768]{2,1,0:T(8,128)(2,1)S(1)}, u32[]{:S(2)}, u32[]{:S(2)}) async-start(bf16[4,288,768]{2,1,0:T(8,128)(2,1)} %get-tuple-element.28), calls=%async_computation.1 | async-start | bytes 3538944 | tf_op jit(solution)/shard_map/all_to_all | solution.py:427
  45.5 1.7 %stack_near.1 = (bf16[4,512,256]{2,1,0:T(8,128)(2,1)S(1)}, f32[8,128]{1,0:T(8,128)}) custom-call(bf16[512,256]{1,0:T(8,128)(2,1)S(1)} %copy-done.4, bf16[512,256]{1,0:T(8,128)(2,1)} %collective-permute-done.7.refs_1_, bf16[512,256]{1,0:T(8,128)(2,1)} %collective-permute-done.8.refs_2_, bf16[512,256]{1,0:T(8,128)(2,1)} %collective-permute-done.9.refs_3_, ...), custom_call_target="tpu_custom_call" | custom-call | tf_op jit(solution)/shard_map/stack_near/pallas_call | solution.py:74
  47.2 4.0 %collective-permute-start.10 = (bf16[4,512,256]{2,1,0:T(8,128)(2,1)S(1)}, bf16[4,512,256]{2,1,0:T(8,128)(2,1)S(1)}, u32[]{:S(2)}, u32[]{:S(2)}) collective-permute-start(bf16[4,512,256]{2,1,0:T(8,128)(2,1)S(1)} %get-tuple-element.31.refs_1_), channel_id=1, source_target_pairs={{0,32},{32,0},{1,33},{33,1},{2,34},{34,2},{3,35},{35,3},{4,36},{36... | collective-permute-start | bytes 3145736 | tf_op jit(solution)/shard_map/ppermute | solution.py:378
  51.3 6.9 %collective-permute-start = (bf16[512,256]{1,0:T(8,128)(2,1)}, bf16[512,256]{1,0:T(8,128)(2,1)S(1)}, u32[]{:S(2)}, u32[]{:S(2)}) collective-permute-start(bf16[512,256]{1,0:T(8,128)(2,1)} %get-tuple-element.26), channel_id=1, source_target_pairs={{0,280},{8,272},{16,264},{24,256},{1,281},{9,273},{17,265},{25,257... | collective-permute-start | bytes 786440 | tf_op jit(solution)/shard_map/ppermute | solution.py:406
  58.2 0.9 copy-done.10
  59.1 2.4 %attention_near.1 = (f32[1024,256]{1,0:T(8,128)S(1)}, f32[1024,128]{1,0:T(8,128)S(1)}, f32[8,128]{1,0:T(8,128)S(1)}) custom-call(bf16[512,256]{1,0:T(8,128)(2,1)S(1)} %copy-done.10, bf16[4,512,256]{2,1,0:T(8,128)(2,1)S(1)} %get-tuple-element.31.refs_1_, bf16[4,512,256]{2,1,0:T(8,128)(2,1)S(1)} %collective-permute-done.10.refs_2_, ...), custom_call_target="tpu_custom_call" | custom-call | flops 2147483648 | bytes 5242880 | tf_op jit(solution)/shard_map/attention_near/pallas_call | solution.py:74
  61.5 1.0 copy-done.13
  63.4 6.4 %collective-permute-done.refs_2_.refs_0_ = bf16[512,256]{1,0:T(8,128)(2,1)S(1)} collective-permute-done((bf16[512,256]{1,0:T(8,128)(2,1)}, bf16[512,256]{1,0:T(8,128)(2,1)S(1)}, u32[]{:S(2)}, u32[]{:S(2)}) %collective-permute-start) | collective-permute-done | bytes 262176 | tf_op jit(solution)/shard_map/ppermute | solution.py:406
  70.0 6.3 %collective-permute-start.11 = (bf16[288,768]{1,0:T(8,128)(2,1)S(1)}, bf16[288,768]{1,0:T(8,128)(2,1)S(1)}, u32[]{:S(2)}, u32[]{:S(2)}) collective-permute-start(bf16[288,768]{1,0:T(8,128)(2,1)S(1)} %get-tuple-element.34), channel_id=1, source_target_pairs={{0,256},{256,0},{1,257},{257,1},{2,258},{258,2},{3,259},{259,3},{4... | collective-permute-start | bytes 1327112 | tf_op jit(solution)/shard_map/ppermute | solution.py:450
  78.4 3.0 %collective-permute-start.13 = (bf16[1536,256]{1,0:T(8,128)(2,1)S(1)}, bf16[1536,256]{1,0:T(8,128)(2,1)S(1)}, u32[]{:S(2)}, u32[]{:S(2)}) collective-permute-start(bf16[1536,256]{1,0:T(8,128)(2,1)S(1)} %bitcast.17), channel_id=1, source_target_pairs={{0,32},{32,0},{1,33},{33,1},{2,34},{34,2},{3,35},{35,3},{4,36},{36... | collective-permute-start | bytes 2359304 | tf_op jit(solution)/shard_map/ppermute | solution.py:378
  81.4 1.0 combine_map.1
  82.4 13.7 %collective-permute-done.11.refs_1_ = bf16[288,768]{1,0:T(8,128)(2,1)S(1)} collective-permute-done((bf16[288,768]{1,0:T(8,128)(2,1)S(1)}, bf16[288,768]{1,0:T(8,128)(2,1)S(1)}, u32[]{:S(2)}, u32[]{:S(2)}) %collective-permute-start.11) | collective-permute-done | bytes 442400 | tf_op jit(solution)/shard_map/ppermute | solution.py:450
  97.0 3.6 %collective-permute-start.12 = (bf16[4,512,256]{2,1,0:T(8,128)(2,1)S(1)}, bf16[4,512,256]{2,1,0:T(8,128)(2,1)}, u32[]{:S(2)}, u32[]{:S(2)}) collective-permute-start(bf16[4,512,256]{2,1,0:T(8,128)(2,1)S(1)} %get-tuple-element.38.refs_1_), channel_id=1, source_target_pairs={{0,32},{32,0},{1,33},{33,1},{2,34},{34,2},{3,35},{35,3},{4,36},{36... | collective-permute-start | bytes 3145736 | tf_op jit(solution)/shard_map/ppermute | solution.py:378
  100.7 13.3 %all-gather = bf16[1152,384]{1,0:T(8,128)(2,1)S(1)} all-gather(bf16[288,384]{1,0:T(8,128)(2,1)S(1)} %get-tuple-element.41), channel_id=2, replica_groups=mesh['w'=2,'x'=4,'c'=2,'z'=4,'y'=8] {'x'}, dimensions={0}, use_global_device_ids=true | all-gather | bytes 1105920 | tf_op jit(solution)/shard_map/all_gather | solution.py:470
  114.0 2.4 %project.1 = (bf16[1280,128]{1,0:T(8,128)(2,1)}, f32[8,128]{1,0:T(8,128)S(1)}) custom-call(bf16[4,288,384]{2,1,0:T(8,128)(2,1)S(1)} %bitcast.10, bf16[1536,256]{1,0:T(8,128)(2,1)S(1)} %bitcast.18, bf16[1536,256]{1,0:T(8,128)(2,1)S(1)} %collective-permute-done.13.refs_2_), custom_call_target="tpu_custom_call" | custom-call | flops 452984832 | bytes 3145728 | tf_op jit(solution)/shard_map/project/pallas_call | solution.py:74
  116.4 7.5 %all-to-all-start.2 = ((bf16[32,40,128]{2,1,0:T(8,128)(2,1)}), bf16[32,40,128]{2,1,0:T(8,128)(2,1)S(1)}, u32[]{:S(2)}, u32[]{:S(2)}) async-start(bf16[32,40,128]{2,1,0:T(8,128)(2,1)} %bitcast.8), calls=%async_computation.2 | async-start | bytes 655360 | tf_op jit(solution)/shard_map/all_to_all | solution.py:480
  123.9 3.7 %attention_far.1 = (bf16[512,256]{1,0:T(8,128)(2,1)}, f32[8,128]{1,0:T(8,128)}) custom-call(bf16[512,256]{1,0:T(8,128)(2,1)} %refs_0_.5, bf16[4,512,256]{2,1,0:T(8,128)(2,1)} %copy-done.9, bf16[4,512,256]{2,1,0:T(8,128)(2,1)} %collective-permute-done.12.refs_2_, f32[1024,256]{1,0:T(8,128)} %copy-done.13, f32[1024,128]{1,0:T(8,128)} %copy-done.14, ...), custom_call_target="tpu_custom_call" | custom-call | flops 2147483648 | bytes 5242880 | tf_op jit(solution)/shard_map/attention_far/pallas_call | solution.py:74
  127.6 6.7 %all-to-all-done.2 = bf16[32,40,128]{2,1,0:T(8,128)(2,1)S(1)} async-done(((bf16[32,40,128]{2,1,0:T(8,128)(2,1)}), bf16[32,40,128]{2,1,0:T(8,128)(2,1)S(1)}, u32[]{:S(2)}, u32[]{:S(2)}) %all-to-all-start.2) | async-done | bytes 327712 | tf_op jit(solution)/shard_map/all_to_all | solution.py:480
  135.0 1.7 %combine.1 = (f32[64,256]{1,0:T(8,128)S(1)}, f32[64,256]{1,0:T(8,128)S(1)}, f32[8,128]{1,0:T(8,128)}) custom-call(f32[1280,64]{1,0:T(8,128)S(1)} %get-tuple-element.44.refs_0_, bf16[1280,128]{1,0:T(8,128)(2,1)S(1)} %bitcast.11, f32[8,128]{1,0:T(8,128)S(1)} %copy-done.5), custom_call_target="tpu_custom_call" | custom-call | flops 251658240 | bytes 1048576 | tf_op jit(solution)/shard_map/combine/pallas_call | solution.py:74
  136.7 6.0 %collective-permute-start.14 = (f32[64,256]{1,0:T(8,128)S(1)}, f32[64,256]{1,0:T(8,128)S(1)}, u32[]{:S(2)}, u32[]{:S(2)}) collective-permute-start(f32[64,256]{1,0:T(8,128)S(1)} %get-tuple-element.48), channel_id=1, source_target_pairs={{0,32},{32,0},{1,33},{33,1},{2,34},{34,2},{3,35},{35,3},{4,36},{36... | collective-permute-start | bytes 196616 | tf_op jit(solution)/shard_map/ppermute | solution.py:378
  142.6 0.9 collective-permute-done.14.refs_1_
  (48 shorter events, 8.0 us)
Async XLA Ops:
  0.6 37.2 %copy-start = (bf16[1,256,1536]{2,1,0:T(8,128)(2,1)S(1)}, bf16[1,256,1536]{2,1,0:T(8,128)(2,1)}, u32[]{:S(2)}) copy-start(bf16[1,256,1536]{2,1,0:T(8,128)(2,1)} %param.15) | copy-start | bytes 2359300
  0.6 37.2 %copy-start.1 = (bf16[1,256,1536]{2,1,0:T(8,128)(2,1)S(1)}, bf16[1,256,1536]{2,1,0:T(8,128)(2,1)}, u32[]{:S(2)}) copy-start(bf16[1,256,1536]{2,1,0:T(8,128)(2,1)} %param.16) | copy-start | bytes 2359300
  0.7 37.1 %collective-permute-start.5 = (bf16[256,1536]{1,0:T(8,128)(2,1)}, bf16[256,1536]{1,0:T(8,128)(2,1)S(1)}, u32[]{:S(2)}, u32[]{:S(2)}) collective-permute-start(bf16[256,1536]{1,0:T(8,128)(2,1)} %bitcast.13), channel_id=1, source_target_pairs={{0,32},{32,0},{1,33},{33,1},{2,34},{34,2},{3,35},{35,3},{4,36},{36... | collective-permute-start | bytes 2359304 | tf_op jit(solution)/shard_map/ppermute | solution.py:378
  9.6 28.2 %collective-permute-start.6 = (bf16[256,1536]{1,0:T(8,128)(2,1)}, bf16[256,1536]{1,0:T(8,128)(2,1)S(1)}, u32[]{:S(2)}, u32[]{:S(2)}) collective-permute-start(bf16[256,1536]{1,0:T(8,128)(2,1)} %bitcast.15), channel_id=1, source_target_pairs={{0,32},{32,0},{1,33},{33,1},{2,34},{34,2},{3,35},{35,3},{4,36},{36... | collective-permute-start | bytes 2359304 | tf_op jit(solution)/shard_map/ppermute | solution.py:378
  11.5 3.5 %collective-permute-start.4 = (bf16[64,256]{1,0:T(8,128)(2,1)}, bf16[64,256]{1,0:T(8,128)(2,1)S(1)}, u32[]{:S(2)}, u32[]{:S(2)}) collective-permute-start(bf16[64,256]{1,0:T(8,128)(2,1)} %refs_1_.3), channel_id=1, source_target_pairs={{0,32},{32,0},{1,33},{33,1},{2,34},{34,2},{3,35},{35,3},{4,36},{36... | collective-permute-start | bytes 98312 | tf_op jit(solution)/shard_map/ppermute | solution.py:378
  15.0 0.7 copy-start.6
  15.7 0.8 copy-start.11
  17.7 0.7 copy-start.3
  18.4 19.4 %all-to-all-start = ((bf16[32,40,128]{2,1,0:T(8,128)(2,1)}), bf16[32,40,128]{2,1,0:T(8,128)(2,1)S(1)}, u32[]{:S(2)}, u32[]{:S(2)}) async-start(bf16[32,40,128]{2,1,0:T(8,128)(2,1)} %bitcast.19), calls=%async_computation | async-start | bytes 655360 | tf_op jit(solution)/shard_map/all_to_all | solution.py:392
  27.6 17.4 %collective-permute-start.7 = (bf16[512,256]{1,0:T(8,128)(2,1)}, bf16[512,256]{1,0:T(8,128)(2,1)}, u32[]{:S(2)}, u32[]{:S(2)}) collective-permute-start(bf16[512,256]{1,0:T(8,128)(2,1)} %get-tuple-element.29.refs_0_), channel_id=1, source_target_pairs={{0,64},{64,128},{128,192},{1,65},{65,129},{129,193},{2,66},{66,130... | collective-permute-start | bytes 786440 | tf_op jit(solution)/shard_map/ppermute | solution.py:410
  31.5 13.6 %collective-permute-start.8 = (bf16[512,256]{1,0:T(8,128)(2,1)}, bf16[512,256]{1,0:T(8,128)(2,1)}, u32[]{:S(2)}, u32[]{:S(2)}) collective-permute-start(bf16[512,256]{1,0:T(8,128)(2,1)} %get-tuple-element.29.refs_0_), channel_id=1, source_target_pairs={{0,128},{64,192},{1,129},{65,193},{2,130},{66,194},{3,131},{67,195... | collective-permute-start | bytes 786440 | tf_op jit(solution)/shard_map/ppermute | solution.py:410
  35.8 9.7 %collective-permute-start.9 = (bf16[512,256]{1,0:T(8,128)(2,1)}, bf16[512,256]{1,0:T(8,128)(2,1)}, u32[]{:S(2)}, u32[]{:S(2)}) collective-permute-start(bf16[512,256]{1,0:T(8,128)(2,1)} %get-tuple-element.29.refs_0_), channel_id=1, source_target_pairs={{0,192},{1,193},{2,194},{3,195},{4,196},{5,197},{6,198},{7,199},{8... | collective-permute-start | bytes 786440 | tf_op jit(solution)/shard_map/ppermute | solution.py:410
  41.3 4.3 %copy-start.4 = (bf16[512,256]{1,0:T(8,128)(2,1)S(1)}, bf16[512,256]{1,0:T(8,128)(2,1)}, u32[]{:S(2)}) copy-start(bf16[512,256]{1,0:T(8,128)(2,1)} %get-tuple-element.29.refs_0_) | copy-start | bytes 786436
  41.3 28.5 %all-to-all-start.1 = ((bf16[4,288,768]{2,1,0:T(8,128)(2,1)}), bf16[4,288,768]{2,1,0:T(8,128)(2,1)S(1)}, u32[]{:S(2)}, u32[]{:S(2)}) async-start(bf16[4,288,768]{2,1,0:T(8,128)(2,1)} %get-tuple-element.28), calls=%async_computation.1 | async-start | bytes 3538944 | tf_op jit(solution)/shard_map/all_to_all | solution.py:427
  47.2 10.9 %collective-permute-start.10 = (bf16[4,512,256]{2,1,0:T(8,128)(2,1)S(1)}, bf16[4,512,256]{2,1,0:T(8,128)(2,1)S(1)}, u32[]{:S(2)}, u32[]{:S(2)}) collective-permute-start(bf16[4,512,256]{2,1,0:T(8,128)(2,1)S(1)} %get-tuple-element.31.refs_1_), channel_id=1, source_target_pairs={{0,32},{32,0},{1,33},{33,1},{2,34},{34,2},{3,35},{35,3},{4,36},{36... | collective-permute-start | bytes 3145736 | tf_op jit(solution)/shard_map/ppermute | solution.py:378
  51.3 18.5 %collective-permute-start = (bf16[512,256]{1,0:T(8,128)(2,1)}, bf16[512,256]{1,0:T(8,128)(2,1)S(1)}, u32[]{:S(2)}, u32[]{:S(2)}) collective-permute-start(bf16[512,256]{1,0:T(8,128)(2,1)} %get-tuple-element.26), channel_id=1, source_target_pairs={{0,280},{8,272},{16,264},{24,256},{1,281},{9,273},{17,265},{25,257... | collective-permute-start | bytes 786440 | tf_op jit(solution)/shard_map/ppermute | solution.py:406
  58.2 1.0 copy-start.10
  61.5 1.0 copy-start.13
  62.6 0.8 copy-start.14
  63.4 15.0 %copy-start.2 = (bf16[1,1536,256]{2,1,0:T(8,128)(2,1)S(1)}, bf16[1,1536,256]{2,1,0:T(8,128)(2,1)}, u32[]{:S(2)}) copy-start(bf16[1,1536,256]{2,1,0:T(8,128)(2,1)} %param.17) | copy-start | bytes 2359300
  63.4 18.0 %copy-start.7 = (s32[64,8]{0,1:T(8,128)S(1)}, s32[64,8]{0,1:T(8,128)}, u32[]{:S(2)}) copy-start(s32[64,8]{0,1:T(8,128)} %param.13) | copy-start | bytes 6148
  63.4 18.0 %copy-start.8 = (f32[64,8]{0,1:T(8,128)S(1)}, f32[64,8]{0,1:T(8,128)}, u32[]{:S(2)}) copy-start(f32[64,8]{0,1:T(8,128)} %param.14) | copy-start | bytes 6148
  70.0 26.1 %collective-permute-start.11 = (bf16[288,768]{1,0:T(8,128)(2,1)S(1)}, bf16[288,768]{1,0:T(8,128)(2,1)S(1)}, u32[]{:S(2)}, u32[]{:S(2)}) collective-permute-start(bf16[288,768]{1,0:T(8,128)(2,1)S(1)} %get-tuple-element.34), channel_id=1, source_target_pairs={{0,256},{256,0},{1,257},{257,1},{2,258},{258,2},{3,259},{259,3},{4... | collective-permute-start | bytes 1327112 | tf_op jit(solution)/shard_map/ppermute | solution.py:450
  76.3 20.0 %collective-permute-start.1 = (bf16[512,256]{1,0:T(8,128)(2,1)S(1)}, bf16[512,256]{1,0:T(8,128)(2,1)S(1)}, u32[]{:S(2)}, u32[]{:S(2)}) collective-permute-start(bf16[512,256]{1,0:T(8,128)(2,1)S(1)} %collective-permute-done.refs_2_.refs_0_), channel_id=1, source_target_pairs={{256,320},{320,384},{384,448},{448,256},{257,321},{321,385},{385,4... | collective-permute-start | bytes 786440 | tf_op jit(solution)/shard_map/ppermute | solution.py:413
  77.0 19.3 %collective-permute-start.2 = (bf16[512,256]{1,0:T(8,128)(2,1)S(1)}, bf16[512,256]{1,0:T(8,128)(2,1)S(1)}, u32[]{:S(2)}, u32[]{:S(2)}) collective-permute-start(bf16[512,256]{1,0:T(8,128)(2,1)S(1)} %collective-permute-done.refs_2_.refs_0_), channel_id=1, source_target_pairs={{256,384},{320,448},{384,256},{448,320},{257,385},{321,449},{385,2... | collective-permute-start | bytes 786440 | tf_op jit(solution)/shard_map/ppermute | solution.py:413
  77.7 18.7 %collective-permute-start.3 = (bf16[512,256]{1,0:T(8,128)(2,1)S(1)}, bf16[512,256]{1,0:T(8,128)(2,1)S(1)}, u32[]{:S(2)}, u32[]{:S(2)}) collective-permute-start(bf16[512,256]{1,0:T(8,128)(2,1)S(1)} %collective-permute-done.refs_2_.refs_0_), channel_id=1, source_target_pairs={{256,448},{320,256},{384,320},{448,384},{257,449},{321,257},{385,3... | collective-permute-start | bytes 786440 | tf_op jit(solution)/shard_map/ppermute | solution.py:413
  78.4 35.6 %collective-permute-start.13 = (bf16[1536,256]{1,0:T(8,128)(2,1)S(1)}, bf16[1536,256]{1,0:T(8,128)(2,1)S(1)}, u32[]{:S(2)}, u32[]{:S(2)}) collective-permute-start(bf16[1536,256]{1,0:T(8,128)(2,1)S(1)} %bitcast.17), channel_id=1, source_target_pairs={{0,32},{32,0},{1,33},{33,1},{2,34},{34,2},{3,35},{35,3},{4,36},{36... | collective-permute-start | bytes 2359304 | tf_op jit(solution)/shard_map/ppermute | solution.py:378
  97.0 19.3 %copy-start.9 = (bf16[4,512,256]{2,1,0:T(8,128)(2,1)}, bf16[4,512,256]{2,1,0:T(8,128)(2,1)S(1)}, u32[]{:S(2)}) copy-start(bf16[4,512,256]{2,1,0:T(8,128)(2,1)S(1)} %get-tuple-element.38.refs_1_) | copy-start | bytes 3145732
  97.0 26.8 %collective-permute-start.12 = (bf16[4,512,256]{2,1,0:T(8,128)(2,1)S(1)}, bf16[4,512,256]{2,1,0:T(8,128)(2,1)}, u32[]{:S(2)}, u32[]{:S(2)}) collective-permute-start(bf16[4,512,256]{2,1,0:T(8,128)(2,1)S(1)} %get-tuple-element.38.refs_1_), channel_id=1, source_target_pairs={{0,32},{32,0},{1,33},{33,1},{2,34},{34,2},{3,35},{35,3},{4,36},{36... | collective-permute-start | bytes 3145736 | tf_op jit(solution)/shard_map/ppermute | solution.py:378
  116.4 7.5 %copy-start.12 = (f32[8,128]{1,0:T(8,128)}, f32[8,128]{1,0:T(8,128)S(1)}, u32[]{:S(2)}) copy-start(f32[8,128]{1,0:T(8,128)S(1)} %get-tuple-element.42.refs_5_) | copy-start | bytes 12292
  116.4 17.9 %all-to-all-start.2 = ((bf16[32,40,128]{2,1,0:T(8,128)(2,1)}), bf16[32,40,128]{2,1,0:T(8,128)(2,1)S(1)}, u32[]{:S(2)}, u32[]{:S(2)}) async-start(bf16[32,40,128]{2,1,0:T(8,128)(2,1)} %bitcast.8), calls=%async_computation.2 | async-start | bytes 655360 | tf_op jit(solution)/shard_map/all_to_all | solution.py:480
  136.7 6.9 %collective-permute-start.14 = (f32[64,256]{1,0:T(8,128)S(1)}, f32[64,256]{1,0:T(8,128)S(1)}, u32[]{:S(2)}, u32[]{:S(2)}) collective-permute-start(f32[64,256]{1,0:T(8,128)S(1)} %get-tuple-element.48), channel_id=1, source_target_pairs={{0,32},{32,0},{1,33},{33,1},{2,34},{34,2},{3,35},{35,3},{4,36},{36... | collective-permute-start | bytes 196616 | tf_op jit(solution)/shard_map/ppermute | solution.py:378
  (1 other events, 0.7 us)
